TPU v7x, 32 devices: a whole 2x2x4 slice. The times are simulated.
32 devices in a mesh: batch: 8 (over z, core), pix: 4 (over y, x).
Axes of the slice: x: 2, y: 2, z: 4, core: 2. Of those that a mesh axis runs over, the one named last changes fastest.
Arguments:
- queries: float32 [64, 100, 256], P('batch'), may hold values from -6 to 6
- features: bfloat16 [64, 4096, 256], P('batch', 'pix'), may hold values from -6 to 6
- mask_features: bfloat16 [64, 16384, 256], P('batch', 'pix'), may hold values from -0.59765625 to 0.59765625
- attend_bits: int32 [64, 100, 256], P('batch', None, 'pix'), may hold values from 0 to 65535
- reopen_flags: int32 [64, 100], P('batch'), may hold values 0 or 1
- matched_queries: int32 [64, 50], P('batch'), may hold values from 0 to 99, as said below
- query_cotan: bfloat16 [64, 100, 256], P('batch'), may hold values from -6 to 6
- mask_cotan: bfloat16 [64, 50, 16384], P('batch', None, 'pix'), may hold values from -6 to 6
- query_weight: float32 [256, 256], replicated, may hold values from -0.5 to 0.5
- query_bias: float32 [256], replicated, may hold values from -1.8 to 1.8
- keyval_weight: float32 [256, 512], replicated, may hold values from -0.5 to 0.5
- value_bias: float32 [256], replicated, may hold values from -1.8 to 1.8
- cross_out: float32 [256, 256], replicated, may hold values from -9 to 9
- cross_out_bias: float32 [256], replicated, may hold values from -1.8 to 1.8
- norm_gain: float32 [3, 256], replicated, may hold values from 0.5 to 1.5
- norm_bias: float32 [3, 256], replicated, may hold values from -1.8 to 1.8
- self_weight: float32 [256, 768], replicated, may hold values from -0.5 to 0.5
- self_bias: float32 [2, 256], replicated, may hold values from -1.8 to 1.8
- self_out: float32 [256, 256], replicated, may hold values from -2.4 to 2.4
- self_out_bias: float32 [256], replicated, may hold values from -1.8 to 1.8
- hidden_weight: float32 [256, 2048], replicated, may hold values from -0.375 to 0.375
- hidden_bias: float32 [2048], replicated, may hold values from -1.8 to 1.8
- hidden_out: float32 [2048, 256], replicated, may hold values from -0.125 to 0.125
- hidden_out_bias: float32 [256], replicated, may hold values from -1.8 to 1.8
- embed_weight: float32 [3, 256, 256], replicated, may hold values from -0.375 to 0.375
- embed_bias: float32 [3, 256], replicated, may hold values from -1.8 to 1.8
Outputs:
- queries_out: float32 [64, 100, 256], P('batch')
- mask_logits: float32 [64, 100, 16384], P('batch', None, 'pix')
- queries_grad: float32 [64, 100, 256], P('batch')
- features_grad: float32 [64, 4096, 256], P('batch', 'pix')
- mask_features_grad: float32 [64, 16384, 256], P('batch', 'pix')
- grad_query_weight: float32 [256, 256], replicated
- grad_query_bias: float32 [256], replicated
- grad_keyval_weight: float32 [256, 512], replicated
- grad_value_bias: float32 [256], replicated
- grad_cross_out: float32 [256, 256], replicated
- grad_cross_out_bias: float32 [256], replicated
- grad_norm_gain: float32 [3, 256], replicated
- grad_norm_bias: float32 [3, 256], replicated
- grad_self_weight: float32 [256, 768], replicated
- grad_self_bias: float32 [2, 256], replicated
- grad_self_out: float32 [256, 256], replicated
- grad_self_out_bias: float32 [256], replicated
- grad_hidden_weight: float32 [256, 2048], replicated
- grad_hidden_bias: float32 [2048], replicated
- grad_hidden_out: float32 [2048, 256], replicated
- grad_hidden_out_bias: float32 [256], replicated
- grad_embed_weight: float32 [3, 256, 256], replicated
- grad_embed_bias: float32 [3, 256], replicated
Inputs may be any that keep to these rules, and one draw needn't show every extreme that they name: `attend_bits`: bit b of word w of a query's row gives pixel 16 w + b of the image's row-major 1/8-scale map; 1 means the query attends to that pixel. `matched_queries`: the 50 entries of one image are distinct query indices; entry m pairs that query with row m of mask_cotan.
All inputs are finite; a program needn't handle non-finite values. No bound on the sum of `reopen_flags` on one device may be relied on, other than what follows from the above.
Results may differ from a plain program's by a relative error of at most 0.04.
The roundings to bfloat16 on the way count: a program that leaves them out, or rounds other values in their place, can miss the bound.
Values sent between devices are 32-bit elements; how exact they have to be, the bound alone decides.
No kernel may reach another device: no remote copies, remote signals or barrier semaphores. Data moves between devices by JAX's collectives and lax.ppermute only.
A program may use at most 256 MiB of HBM per device.

v0:
```python
import functools
import math

import jax
import jax.numpy as jnp
import numpy as np
from jax import lax
from jax.experimental import pallas as pl
from jax.experimental.pallas import tpu as pltpu
from jax.sharding import PartitionSpec as P

HEADS = 8
EPS = 1e-05
PENALTY = 10000.0
F32 = jnp.float32
LOW = jnp.bfloat16
HIGH = lax.Precision.HIGHEST
CURVE = math.sqrt(2.0 / math.pi)
CUBE = 0.044715
MIB = 1 << 20
PARTS = 4

T_CROSS, T_SELF, T_SELFOUT, T_EMBED, T_HIDDEN = 0, 1, 4, 5, 8


def up(n, m):
    return (n + m - 1) // m * m


def nn(a, b, precision=None):
    return lax.dot_general(a, b, (((1,), (0,)), ((), ())), precision=precision, preferred_element_type=F32)


def nt(a, b, precision=None):
    return lax.dot_general(a, b, (((1,), (1,)), ((), ())), precision=precision, preferred_element_type=F32)


def tn(a, b, precision=None):
    return lax.dot_general(a, b, (((0,), (0,)), ((), ())), precision=precision, preferred_element_type=F32)


def head_mask(width):
    shape = (HEADS, 1, width)
    head = width // HEADS
    return lax.broadcasted_iota(jnp.int32, shape, 2) // head == lax.broadcasted_iota(jnp.int32, shape, 0)


def spread(x, mask):
    rows, width = x.shape
    return jnp.where(mask, x[None], 0.0).reshape(HEADS * rows, width)


def gather_heads(x, mask):
    total, width = x.shape
    return jnp.sum(jnp.where(mask, x.reshape(HEADS, total // HEADS, width), 0.0), 0)


def spread_low(x, mask):
    return spread(x, mask).astype(LOW)


def head_onehot(width, lanes, transposed=False):
    head = width // HEADS
    if transposed:
        shape, a, b = (width, lanes), 0, 1
    else:
        shape, a, b = (lanes, width), 1, 0
    hit = lax.broadcasted_iota(jnp.int32, shape, a) // head == lax.broadcasted_iota(jnp.int32, shape, b)
    return hit.astype(F32)


def slabs_in(scr, value):
    for t in range(scr.shape[0]):
        scr[t] = value[:, t * 128:(t + 1) * 128]


def take_image(scr, image, count, images):
    rows = pl.ds(image, count, images)
    return jnp.concatenate([scr[t, rows, :] for t in range(scr.shape[0])], 1)


def put_image(scr, image, count, images, value):
    for t in range(scr.shape[0]):
        scr[t, pl.ds(image, count, images), :] = value[:, t * 128:(t + 1) * 128]


def slabs(rows, columns):
    return pltpu.VMEM((columns // 128, rows, 128), F32)


def cost(flops, nbytes, trans=0):
    return pl.CostEstimate(flops=int(flops), bytes_accessed=int(nbytes), transcendentals=int(trans))


def whole(x):
    shape = x.shape
    return pl.BlockSpec(shape, lambda *_: (0,) * len(shape))


def params(mib):
    return pltpu.CompilerParams(vmem_limit_bytes=mib * MIB, dimension_semantics=("arbitrary",))


def of_step(keys, n, i):
    key = keys[-1]
    for j in range(len(keys) - 2, -1, -1):
        key = jnp.where(i < (j + 1) * n, keys[j], key)
    return key


def turned_heads(x, fill):
    return jnp.transpose(jnp.concatenate([x, fill], 0))[:, 0:x.shape[0]].astype(LOW)


def attend_kernel(keys, n, with_mask, me_ref, *refs):
    q_ref, f_ref, bits_ref, flag_ref, wq_ref, bq_ref, wkv_ref, vb_ref, elo_ref, ehi_ref = refs[:10]
    refs = refs[10:]
    if with_mask:
        mc_ref, mf_ref, mf_own_ref = refs[:3]
        refs = refs[3:]
    e_ref, kv_ref, cq_ref = refs[:3]
    pays, refs = refs[3:3 + len(keys)], refs[3 + len(keys):]
    if with_mask:
        es_ref, refs = refs[0], refs[1:]
        mc_scr, refs = refs[0], refs[1:]
    q_scr, w_scr, all_scr, wq_scr, wkv_scr, vb_scr, pay_ref = refs
    i = pl.program_id(0)
    images = flag_ref.shape[0]
    image = (me_ref[0] ^ of_step(keys, n, i)) * n + i % n
    width = q_ref.shape[1]
    count = q_ref.shape[0] // images
    rows = q_scr.shape[0]
    pixels = f_ref.shape[1]
    tall = rows + HEADS
    head = width // HEADS

    @pl.when(i == 0)
    def _():
        q_scr[...] = jnp.zeros_like(q_scr)
        w_scr[...] = jnp.zeros_like(w_scr)
        slabs_in(all_scr, q_ref[...])
        wq_scr[...] = wq_ref[...].astype(LOW)
        wkv_scr[0:width] = jnp.transpose(wkv_ref[:, :width]).astype(LOW)
        wkv_scr[width:] = jnp.transpose(wkv_ref[:, width:]).astype(LOW)
        vb_scr[...] = jnp.transpose(jnp.broadcast_to(vb_ref[...], (128, width)))
        pay_ref[...] = jnp.zeros_like(pay_ref)
        if with_mask:
            es_ref[...] = jnp.zeros_like(es_ref)
            slabs_in(mc_scr, mc_ref[...].astype(F32).reshape(mc_ref.shape[0] * images, mc_ref.shape[2]))

    if with_mask:
        matched = mc_ref.shape[0]
        pay_ref[tall:tall + matched] = nn(take_image(mc_scr, image, matched, images).astype(LOW), mf_ref[0])

        @pl.when(i < n)
        def _():
            own = take_image(mc_scr, me_ref[0] * n + i % n, matched, images).astype(LOW)
            es_ref[i % n, 0:matched] = nn(own, mf_own_ref[0])

    q_scr[0:count] = take_image(all_scr, image, count, images)
    w_scr[:, 0:count] = jnp.where(flag_ref[pl.ds(image, 1), :] > 0, 65535, bits_ref[0])

    scale = 1.0 / math.sqrt(head)
    cq = ((nn(q_scr[...].astype(LOW), wq_scr[...]) + bq_ref[...]) * scale).astype(LOW).astype(F32)
    cq_ref[0] = cq

    bits = w_scr[...]
    low = (bits & 255).astype(F32).astype(LOW)
    high = (bits >> 8).astype(F32).astype(LOW)
    byte = (tn(low, elo_ref[...]) + tn(high, ehi_ref[...])).astype(jnp.int32)
    shift = lax.broadcasted_iota(jnp.int32, (rows, pixels), 1) & 7
    pen = jnp.where(((byte >> shift) & 1) == 1, 0.0, -PENALTY)

    keyval = nt(wkv_scr[...], f_ref[0])
    ck = keyval[:width].astype(LOW)
    cv = (keyval[width:] + jnp.concatenate([vb_scr[...]] * (pixels // 128), 1)).astype(LOW)
    kv_ref[0, :width] = ck
    kv_ref[0, width:] = cv

    def scores(h):
        at = slice(h * head, (h + 1) * head)
        return nn(cq[:, at].astype(LOW), ck[at]) + pen

    lane = lax.broadcasted_iota(jnp.int32, (rows, 128), 1)
    stats = jnp.zeros((rows, 128), F32)
    parts = []
    following = scores(0)
    for h in range(HEADS):
        s = following
        if h + 1 < HEADS:
            following = scores(h + 1)
        m = jnp.max(s, -1, keepdims=True)
        e = jnp.exp(s - m)
        total = jnp.sum(e, -1, keepdims=True)
        e_low = e.astype(LOW)
        e_ref[0, h] = e_low
        parts.append(nt(cv[h * head:(h + 1) * head], e_low))
        stats = jnp.where(lane == h, m, stats)
        stats = jnp.where(lane == HEADS + h, total, stats)
    pay_ref[0:rows] = jnp.transpose(jnp.concatenate(parts, 0))
    full = jnp.concatenate([stats, jnp.ones((128 - rows, 128), F32)], 0)
    turned = jnp.transpose(full)
    pay_ref[rows:tall, 0:128] = turned[0:HEADS]
    pay_ref[rows:tall, 128:256] = turned[HEADS:2 * HEADS]
    for j, out in enumerate(pays):
        @pl.when(i // n == j)
        def _(out=out):
            out[0] = pay_ref[0:out.shape[1]]


def attend(keys, me, queries, features, bits, reopen_flags, query_weight, query_bias, keyval_weight, value_bias, parts,
           masks=None):
    images, pixels, width = features.shape
    words, count = bits.shape[1:]
    rows = up(count, 8)
    pixel = np.arange(pixels)
    word = np.arange(words)
    here = pixel[None, :] // 16 == word[:, None]
    e_lo = (here & (pixel[None, :] % 16 < 8)).astype(LOW)
    e_hi = (here & (pixel[None, :] % 16 >= 8)).astype(LOW)
    n = images // parts
    steps = n * len(keys)

    def theirs(*shape):
        return pl.BlockSpec(
            (1,) + shape, lambda i, me: ((me[0] ^ of_step(keys, n, i)) * n + i % n,) + (0,) * len(shape))

    def of_key(j, *shape):
        return pl.BlockSpec((1,) + shape, lambda i, me: (jnp.clip(i - j * n, 0, n - 1),) + (0,) * len(shape))

    per = lambda *shape: pl.BlockSpec((1,) + shape, lambda i, me: (i,) + (0,) * len(shape))
    args = (queries, features, bits, reopen_flags, query_weight, query_bias[None], keyval_weight, value_bias[None], e_lo, e_hi)
    in_specs = [whole(a) for a in args]
    in_specs[1] = theirs(pixels, width)
    in_specs[2] = theirs(words, count)
    flops = 2 * steps * (pixels * width * 2 * width + 2 * HEADS * rows * pixels * width)
    nbytes = steps * (pixels * width * 6 + HEADS * rows * pixels * 2)
    tall = rows + HEADS
    out_shape = [
        jax.ShapeDtypeStruct((steps, HEADS, rows, pixels), LOW),
        jax.ShapeDtypeStruct((steps, 2 * width, pixels), LOW),
        jax.ShapeDtypeStruct((steps, rows, width), F32),
    ]
    scratch = []
    if masks is not None:
        matched, _, wide = masks[0].shape
        args += masks + masks[1:]
        in_specs += [whole(masks[0]), theirs(wide, width),
                     pl.BlockSpec((1, wide, width), lambda i, me: (me[0] * n + jnp.minimum(i, n - 1), 0, 0))]
        nbytes += steps * wide * (width + matched) * 2
        scratch = [slabs(matched * images, wide)]
        tall += up(matched, 8)
    out_shape += [jax.ShapeDtypeStruct((n, tall, width), F32)] * len(keys)
    out_specs = [per(HEADS, rows, pixels), per(2 * width, pixels), per(rows, width)]
    out_specs += [of_key(j, tall, width) for j in range(len(keys))]
    if masks is not None:
        out_shape.append(jax.ShapeDtypeStruct((n, up(matched, 8), width), F32))
        out_specs.append(whole(out_shape[-1]))
    return pl.pallas_call(
        functools.partial(attend_kernel, keys, n, masks is not None),
        grid_spec=pltpu.PrefetchScalarGridSpec(
            num_scalar_prefetch=1,
            grid=(steps,),
            in_specs=in_specs,
            out_specs=tuple(out_specs),
            scratch_shapes=scratch + [
                pltpu.VMEM((rows, width), F32),
                pltpu.VMEM((words, rows), jnp.int32),
                slabs(count * images, width),
                pltpu.VMEM((width, width), LOW),
                pltpu.VMEM((2 * width, width), LOW),
                pltpu.VMEM((width, 128), F32),
                pltpu.VMEM((tall, width), F32),
            ],
        ),
        out_shape=tuple(out_shape),
        compiler_params=params(60),
        cost_estimate=cost(flops, nbytes, steps * HEADS * rows * pixels),
        name="attend",
    )(me, *args)


def combine_kernel(rows, *refs):
    parts, es_ref, out_ref = refs[:-2], refs[-2], refs[-1]
    images, full, width = out_ref.shape
    tall = rows + HEADS
    onehot = head_onehot(width, HEADS)
    for i in range(images):
        ms = [p[i, rows:tall, 0:128] for p in parts]
        ls = [p[i, rows:tall, 128:256] for p in parts]
        top = functools.reduce(jnp.maximum, ms)
        rs = [jnp.exp(m - top) for m in ms]
        total = sum(r * l for r, l in zip(rs, ls))
        acc = jnp.zeros((rows, width), F32)
        for p, r in zip(parts, rs):
            acc = acc + p[i, 0:rows] * tn(r / total, onehot, HIGH)[0:rows]
        es = es_ref[i]
        for p in parts[1:]:
            es = es + p[i, tall:]
        out_ref[i, 0:rows] = acc
        out_ref[i, rows:tall, 0:128] = top
        out_ref[i, rows:tall, 128:256] = total
        out_ref[i, tall:] = es


def combine(parts, es, rows):
    shape = parts[1].shape
    return pl.pallas_call(
        functools.partial(combine_kernel, rows),
        out_shape=jax.ShapeDtypeStruct(shape, F32),
        compiler_params=pltpu.CompilerParams(vmem_limit_bytes=16 * MIB),
        cost_estimate=cost(1e6, 5 * 4 * math.prod(shape)),
        name="combine",
    )(*parts, es)


def lower_kernel(*refs):
    n = len(refs) // 2
    for raw, out in zip(refs[:n], refs[n:]):
        out[...] = raw[...].astype(LOW)


def lower(weights):
    out_shape = tuple(jax.ShapeDtypeStruct(w.shape, LOW) for w in weights)
    size = sum(math.prod(w.shape) for w in weights)
    return pl.pallas_call(
        lower_kernel,
        out_shape=out_shape,
        compiler_params=pltpu.CompilerParams(vmem_limit_bytes=24 * MIB),
        cost_estimate=cost(size, 6 * size),
        name="lower",
    )(*weights)


def norm_forward(x, gain, bias):
    centre = x - jnp.mean(x, -1, keepdims=True)
    inverse = lax.rsqrt(jnp.mean(centre * centre, -1, keepdims=True) + EPS)
    normed = centre * inverse
    return normed * gain + bias, normed, inverse


def norm_backward(normed, inverse, gain, grad):
    dnormed = grad * gain
    return inverse * (
        dnormed - jnp.mean(dnormed, -1, keepdims=True) - normed * jnp.mean(dnormed * normed, -1, keepdims=True)
    )


def gelu_pair(x):
    square = x * x
    t = jnp.tanh(x * (CURVE + (CURVE * CUBE) * square))
    half = 0.5 + 0.5 * t
    slope = half + (0.5 * x) * (1.0 - t * t) * (CURVE + (3.0 * CURVE * CUBE) * square)
    return x * half, slope


def column_sum(x):
    return jnp.sum(x, 0, keepdims=True)


def chain_kernel(
    pieces, me_ref, *refs
):
    att_parts, refs = refs[:pieces], refs[pieces:]
    locals_, refs = refs[:PARTS], refs[PARTS:]
    chain_body(me_ref, att_parts, locals_, *refs)


def chain_body(
    me_ref, att_parts, locals_, q_ref, match_ref, cot_ref, wc_ref, bc_ref, gain_ref, nbias_ref, ws_ref, bs_ref, wso_ref,
    bso_ref, wh_ref, bh_ref, who_ref, bho_ref, we_ref, be_ref,
    x3_ref, emb_ref, dn_ref, dt_ref, dp1_ref, mine_ref, away_ref,
    g_ref, all_scr, cot_scr, out_scr, att_scr, emb_scr, loc_scr,
    q_scr, sq_scr, sk_scr, sv_scr, so_scr, pr_scr, h_scr, gp_scr, dso_scr, dm_scr
):
    step = pl.program_id(0)
    batch, rows, width = dn_ref.shape
    matched = match_ref.shape[1]
    count, images = cot_ref.shape[:2]
    tall = rows + HEADS
    flat = batch * rows
    hidden = wh_ref.shape[1]
    scale = 1.0 / math.sqrt(width // HEADS)
    hm = head_mask(width)

    @pl.when(step == 0)
    def _():
        q_scr[...] = jnp.zeros_like(q_scr)
        g_ref[...] = jnp.zeros_like(g_ref)
        n = att_parts[0].shape[0]
        for k, part in enumerate(att_parts):
            att_scr[pl.ds((me_ref[0] ^ k) * n, n)] = part[...]
        n = locals_[0].shape[0]
        for k, part in enumerate(locals_):
            loc_scr[pl.ds((me_ref[0] ^ k) * n, n)] = part[:, rows:tall]
        slabs_in(all_scr, q_ref[...])
        slabs_in(cot_scr, cot_ref[...].astype(F32).reshape(count * images, width))

    def put(tile, value):
        g_ref[tile * width:(tile + 1) * width] += value

    bias_at = (T_HIDDEN + 2 * (hidden // width)) * width

    def put_bias(index, value):
        g_ref[bias_at + index:bias_at + index + 1] += value

    first = step * batch
    for b in range(batch):
        q_scr[b, 0:count] = take_image(all_scr, first + b, count, images)
    att = att_scr[pl.ds(first, batch), 0:rows].reshape(flat, width)
    att_low = att.astype(LOW)
    queries = q_scr[...].reshape(flat, width)
    x1, n1, i1 = norm_forward(queries + nn(att_low, wc_ref[...]) + bc_ref[...], gain_ref[0:1], nbias_ref[0:1])
    x1_low = x1.astype(LOW)
    mixed = nn(x1_low, ws_ref[...])
    three = (batch, rows, width)
    sq_scr[...] = ((mixed[:, :width] + bs_ref[0:1]) * scale).reshape(three)
    sk_scr[...] = mixed[:, width:2 * width].reshape(three)
    sv_scr[...] = (mixed[:, 2 * width:] + bs_ref[1:2]).reshape(three)

    head = width // HEADS
    lanes = lambda h: slice(h * 128, (h + 1) * 128)
    fill = jnp.zeros((128 - rows, width), F32)

    def tall_heads(x):
        return spread_low(jnp.concatenate([x, fill], 0), hm)

    def turn(x):
        return jnp.transpose(jnp.concatenate([x, fill], 0))[:, 0:rows].astype(LOW)

    def by_head(turned, x):
        return jnp.transpose(jnp.concatenate(
            [nn(turned[h * head:(h + 1) * head], x[:, lanes(h)]) for h in range(HEADS)], 0))[0:rows]

    for b in range(batch):
        ss = nt(sk_scr[b].astype(LOW), tall_heads(sq_scr[b]))
        keys = lax.broadcasted_iota(jnp.int32, ss.shape, 0)
        ss = jnp.where(keys < count, ss, -1e30)
        p = jnp.exp(ss - jnp.max(ss, 0, keepdims=True))
        p = p * (1.0 / jnp.sum(p, 0, keepdims=True))
        pr_scr[b] = p
        so_scr[b] = by_head(turn(sv_scr[b]), p.astype(LOW))
    so_low = so_scr[...].reshape(flat, width).astype(LOW)
    x2, n2, i2 = norm_forward(x1 + nn(so_low, wso_ref[...]) + bso_ref[...], gain_ref[1:2], nbias_ref[1:2])
    x2_low = x2.astype(LOW)
    block = 2 * width

    def ff_forward(j, acc):
        cols = pl.ds(pl.multiple_of(j * block, block), block)
        h, slope = gelu_pair(nn(x2_low, wh_ref[:, cols]) + bh_ref[:, cols])
        h = h.astype(LOW)
        h_scr[:, cols] = h
        gp_scr[:, cols] = slope.astype(gp_scr.dtype)
        return acc + nn(h, who_ref[cols, :])

    ff = lax.fori_loop(0, hidden // block, ff_forward, jnp.zeros((flat, width), F32))
    x3, n3, i3 = norm_forward(x2 + ff + bho_ref[...], gain_ref[2:3], nbias_ref[2:3])
    for b in range(batch):
        put_image(out_scr, first + b, count, images, x3[b * rows:b * rows + count])

    x3_low = x3.astype(LOW)
    h1, slope1 = gelu_pair(nn(x3_low, we_ref[0]) + be_ref[0:1])
    h1 = h1.astype(LOW)
    h2, slope2 = gelu_pair(nn(h1, we_ref[1]) + be_ref[1:2])
    h2 = h2.astype(LOW)
    emb = nn(h2, we_ref[2]) + be_ref[2:3]
    for b in range(batch):
        put_image(emb_scr, first + b, count, images, emb[b * rows:b * rows + count])

    grads = []
    for b in range(batch):
        spots = match_ref[pl.ds(first + b, 1), :]
        pick = (lax.broadcasted_iota(jnp.int32, (rows, matched), 0) == spots).astype(F32).astype(LOW)
        grads.append(nn(pick, att_scr[first + b, tall:tall + matched].astype(LOW)))
    dz3 = jnp.concatenate(grads, 0)
    dz3_low = dz3.astype(LOW)
    put(T_EMBED + 2, tn(h2, dz3_low))
    put_bias(19, column_sum(dz3_low.astype(F32)))
    dz2 = (nt(dz3_low, we_ref[2]) * slope2).astype(LOW)
    put(T_EMBED + 1, tn(h1, dz2))
    put_bias(18, column_sum(dz2.astype(F32)))
    dz1 = (nt(dz2, we_ref[1]) * slope1).astype(LOW)
    put(T_EMBED, tn(x3_low, dz1))
    put_bias(17, column_sum(dz1.astype(F32)))
    for b in range(batch):
        q_scr[b, 0:count] = take_image(cot_scr, first + b, count, images)
    dx3 = q_scr[...].reshape(flat, width) + nt(dz1, we_ref[0])
    put_bias(3, column_sum(dx3 * n3))
    put_bias(6, column_sum(dx3))
    dp3 = norm_backward(n3, i3, gain_ref[2:3], dx3)
    dff = dp3.astype(LOW)
    put_bias(16, column_sum(dff.astype(F32)))

    def ff_backward(j, acc):
        cols = pl.ds(pl.multiple_of(j * block, block), block)
        base = (T_HIDDEN + hidden // width) * width
        spot = pl.ds(pl.multiple_of(base + j * block, block), block)
        g_ref[spot] += tn(h_scr[:, cols], dff)
        dz = (nt(dff, who_ref[cols, :]) * gp_scr[:, cols].astype(F32)).astype(LOW)
        gh = tn(x2_low, dz)
        sums = column_sum(dz.astype(F32))
        for t in range(block // width):
            tile = pl.ds(pl.multiple_of(T_HIDDEN * width + j * block + t * width, width), width)
            g_ref[tile] += gh[:, t * width:(t + 1) * width]
            g_ref[pl.ds(bias_at + 8 + j * (block // width) + t, 1)] += sums[:, t * width:(t + 1) * width]
        return acc + nt(dz, wh_ref[:, cols])

    dx2 = dp3 + lax.fori_loop(0, hidden // block, ff_backward, jnp.zeros((flat, width), F32))
    put_bias(2, column_sum(dx2 * n2))
    put_bias(5, column_sum(dx2))
    dp2 = norm_backward(n2, i2, gain_ref[1:2], dx2)
    dsa = dp2.astype(LOW)
    put(T_SELFOUT, tn(so_low, dsa))
    put_bias(7, column_sum(dsa.astype(F32)))
    dso_scr[...] = nt(dsa, wso_ref[...]).reshape(three)

    for b in range(batch):
        dsox = tall_heads(dso_scr[b])
        p = pr_scr[b]
        dp = nt(sv_scr[b].astype(LOW), dsox)
        dss = (p * (dp - jnp.sum(p * dp, 0, keepdims=True))).astype(LOW)
        dm_scr[b, :, 0:width] = by_head(turn(sk_scr[b]), dss) * scale
        dm_scr[b, :, width:2 * width] = nn(dss, tall_heads(sq_scr[b]))
        dm_scr[b, :, 2 * width:] = nn(p.astype(LOW), dsox)

    dm = dm_scr[...].reshape(flat, 3 * width).astype(LOW)
    gs = tn(x1_low, dm)
    for t in range(3):
        put(T_SELF + t, gs[:, t * width:(t + 1) * width])
    put_bias(20, column_sum(dm[:, :width].astype(F32)))
    put_bias(21, column_sum(dm[:, 2 * width:].astype(F32)))
    dx1 = dp2 + nt(dm, ws_ref[...])
    put_bias(1, column_sum(dx1 * n1))
    put_bias(4, column_sum(dx1))
    dp1 = norm_backward(n1, i1, gain_ref[0:1], dx1)
    dp1_ref[...] = dp1.reshape(three)
    dca = dp1.astype(LOW)
    put(T_CROSS, tn(att_low, dca))
    put_bias(0, column_sum(dca.astype(F32)))
    d_att = nt(dca, wc_ref[...]).reshape(three)
    onehot = head_onehot(width, HEADS)
    back = head_onehot(width, 128, True)
    for b in range(batch):
        top = att_scr[first + b, rows:tall, 0:128]
        total = att_scr[first + b, rows:tall, 128:256]
        ratio = jnp.exp(loc_scr[first + b, :, 0:128] - top) / total
        dn = d_att[b] * tn(ratio, onehot, HIGH)[0:rows]
        dn_ref[b] = dn
        dt_ref[b] = -nn(dn * att_scr[first + b, 0:rows], back, HIGH)

    @pl.when(step == 1)
    def _():
        x3_ref[...] = jnp.concatenate([out_scr[t] for t in range(out_scr.shape[0])], 1)
        emb_ref[...] = jnp.concatenate([emb_scr[t] for t in range(emb_scr.shape[0])], 1)
        share = mine_ref.shape[0]
        at = me_ref[1] * 2 + me_ref[2]
        mine_ref[...] = g_ref[pl.ds(pl.multiple_of(at * share, 8), share)]
        away_ref[...] = g_ref[pl.ds(pl.multiple_of((at + 1 - 2 * me_ref[2]) * share, 8), share)]


def chain(me, parts, pays, queries, matched, query_cotan, weights, n_pix):
    full, width = parts[0].shape[1:]
    images = pays[0].shape[0] * len(pays)
    count = query_cotan.shape[0]
    rows = up(count, 8)
    batch = images // 2
    hidden = weights[8].shape[1]
    tiles = T_HIDDEN + 2 * (hidden // width)
    grads = up(tiles * width + 22, 256)
    half = lambda *shape: pl.BlockSpec((batch,) + shape, lambda i, *_: (i,) + (0,) * len(shape))
    pieces = len(parts)
    args = tuple(parts) + tuple(pays) + (queries, matched, query_cotan) + weights
    in_specs = [whole(a) for a in args]
    out_shape = (
        jax.ShapeDtypeStruct((count * images, width), F32),
        jax.ShapeDtypeStruct((count * images, width), F32),
        jax.ShapeDtypeStruct((images, rows, width), F32),
        jax.ShapeDtypeStruct((images, rows, 128), F32),
        jax.ShapeDtypeStruct((images, rows, width), F32),
        jax.ShapeDtypeStruct((grads // n_pix // 2, width), F32),
        jax.ShapeDtypeStruct((grads // n_pix // 2, width), F32),
    )
    flat = batch * rows
    three = (batch, rows, width)
    many = slabs(count * images, width)
    return pl.pallas_call(
        functools.partial(chain_kernel, pieces),
        grid_spec=pltpu.PrefetchScalarGridSpec(
            num_scalar_prefetch=1,
            grid=(2,),
            in_specs=in_specs,
            out_specs=(whole(out_shape[0]), whole(out_shape[1]), half(rows, width), half(rows, 128), half(rows, width),
                       whole(out_shape[5]), whole(out_shape[6])),
            scratch_shapes=[
                pltpu.VMEM((grads, width), F32),
                many,
                many,
                many,
                pltpu.VMEM((images, full, width), F32),
                many,
                pltpu.VMEM((images, HEADS, width), F32),
                pltpu.VMEM(three, F32),
                pltpu.VMEM(three, F32),
                pltpu.VMEM(three, F32),
                pltpu.VMEM(three, F32),
                pltpu.VMEM(three, F32),
                pltpu.VMEM((batch, rows, HEADS * 128), F32),
                pltpu.VMEM((flat, hidden), LOW),
                pltpu.VMEM((flat, hidden), LOW),
                pltpu.VMEM(three, F32),
                pltpu.VMEM((batch, rows, 3 * width), F32),
            ],
        ),
        out_shape=out_shape,
        compiler_params=params(62),
        cost_estimate=cost(2 * 8e9, 20e6, 4e6),
        name="chain",
    )(me, *args)


def mask_out_kernel(emb_ref, match_ref, mc_ref, mf_ref, logit_old, grad_old, logit_ref, grad_ref, chosen_scr,
                    emb_scr, low_scr, logit_scr, mc_scr):
    images, matched, width = chosen_scr.shape
    count = logit_ref.shape[0] // images
    part = mc_ref.shape[2]

    @pl.when(pl.program_id(0) == 0)
    def _():
        slabs_in(emb_scr, emb_ref[...])
        low_scr[...] = jnp.zeros_like(low_scr)
        for b in range(images):
            pick = (lax.broadcasted_iota(jnp.int32, (count, matched), 0) == match_ref[b:b + 1, :]).astype(F32).astype(LOW)
            emb = take_image(emb_scr, b, count, images).astype(LOW)
            low_scr[b, 0:count] = emb.astype(F32)
            chosen_scr[b] = tn(pick, emb)

    slabs_in(mc_scr, mc_ref[...].astype(F32).reshape(matched * images, part))
    for b in range(images):
        put_image(logit_scr, b, count, images, nt(low_scr[b].astype(LOW), mf_ref[b])[0:count])
        grad_ref[b] = tn(take_image(mc_scr, b, matched, images).astype(LOW), chosen_scr[b].astype(LOW))
    for t in range(part // 128):
        logit_ref[:, t * 128:(t + 1) * 128] = logit_scr[t]


def mask_out(emb, matched_queries, mask_cotan, mask_features, count, pieces, steps, old=None):
    matched, images, pixels = mask_cotan.shape
    width = emb.shape[1]
    part = pixels // pieces
    first, last = steps
    out_shape = (
        jax.ShapeDtypeStruct((count * images, pixels), F32),
        jax.ShapeDtypeStruct((images, pixels, width), F32),
    )
    args = (emb, matched_queries, mask_cotan, mask_features)
    here = pl.BlockSpec(memory_space=pl.ANY)
    kernel = mask_out_kernel
    aliases = {}
    specs = []
    if old is None:
        def kernel(a, b, c, d, *rest):
            mask_out_kernel(a, b, c, d, None, None, *rest)
    else:
        args += old
        aliases = {4: 0, 5: 1}
        specs = [here, here]
    return pl.pallas_call(
        kernel,
        grid=(last - first,),
        in_specs=[
            whole(emb),
            whole(matched_queries),
            pl.BlockSpec((matched, images, part), lambda j: (0, 0, j + first)),
            pl.BlockSpec((images, part, width), lambda j: (0, j + first, 0)),
        ] + specs,
        out_specs=(
            pl.BlockSpec((count * images, part), lambda j: (0, j + first)),
            pl.BlockSpec((images, part, width), lambda j: (0, j + first, 0)),
        ),
        out_shape=out_shape,
        input_output_aliases=aliases,
        scratch_shapes=[pltpu.VMEM((images, matched, width), F32),
                        slabs(count * images, width), pltpu.VMEM((images, up(count, 8), width), F32),
                        slabs(count * images, part), slabs(matched * images, part)],
        compiler_params=params(60),
        cost_estimate=cost(
            2 * images * pixels * width * 160 * (last - first) / pieces,
            images * pixels * (width * 6 + count * 4 + matched * 2) * (last - first) / pieces),
        name="mask_out",
    )(*args)


def attend_back_kernel(keys, n, last, me_ref, e_ref, kv_ref, f_ref, cq_ref, dn_ref, dt_ref, wkv_ref, acc_old, vb_old,
                       fg_ref, qps, acc_ref, vb_ref, g_ref, w_scr):
    i = pl.program_id(0)
    rows, width = cq_ref.shape[1:]
    pixels = f_ref.shape[1]
    head = width // HEADS

    @pl.when(i == 0)
    def _():
        acc_ref[...] = jnp.zeros_like(acc_ref) if acc_old is None else acc_old[...]
        vb_ref[...] = jnp.zeros_like(vb_ref) if vb_old is None else vb_old[...]
        w_scr[0:width] = jnp.transpose(wkv_ref[:, :width]).astype(LOW)
        w_scr[width:] = jnp.transpose(wkv_ref[:, width:]).astype(LOW)

    dn = dn_ref[0]
    fill = jnp.zeros((128 - rows, width), F32)
    cq_turned = turned_heads(cq_ref[0], fill)
    dn_turned = turned_heads(dn, fill)

    def weigh(h):
        at = slice(h * head, (h + 1) * head)
        return nn(dn[:, at].astype(LOW), kv_ref[0, width + h * head:width + (h + 1) * head]) + dt_ref[0, :, h:h + 1]

    parts, keys_sum, values_sum = [], [], []
    following = weigh(0)
    for h in range(HEADS):
        at = slice(h * head, (h + 1) * head)
        dw = following
        if h + 1 < HEADS:
            following = weigh(h + 1)
        e_low = e_ref[0, h]
        ds = (e_low.astype(F32) * dw).astype(LOW)
        values_sum.append(nn(dn_turned[at], e_low).astype(LOW))
        keys_sum.append(nn(cq_turned[at], ds).astype(LOW))
        parts.append(nt(kv_ref[0, at], ds))
    part = jnp.transpose(jnp.concatenate(parts, 0))
    for j, out in enumerate(qps):
        @pl.when(i // n == j)
        def _(out=out):
            out[0] = part
    turned = jnp.concatenate(keys_sum + values_sum, 0)
    acc_ref[...] += nn(turned, f_ref[0])
    summed = turned[width:].astype(F32)
    lanes_sum = summed[:, 0:128]
    for t in range(1, pixels // 128):
        lanes_sum = lanes_sum + summed[:, t * 128:(t + 1) * 128]
    vb_ref[...] += lanes_sum
    fg_ref[0] = tn(turned, w_scr[...])

    if last:
        @pl.when(i == pl.num_programs(0) - 1)
        def _():
            sums = jnp.sum(jnp.transpose(vb_ref[...]), 0, keepdims=True)
            fill = jnp.zeros((g_ref.shape[0] - 2 * width - 1, width), F32)
            g_ref[...] = jnp.concatenate(
                [jnp.transpose(acc_ref[0:width]), jnp.transpose(acc_ref[width:]), sums, fill], 0)


def attend_back(keys, me, kept, offset, features, dn, dt, keyval_weight, old, last):
    e, kv, cq = kept
    images, pixels, width = features.shape
    rows = cq.shape[1]
    n = images // PARTS
    steps = n * len(keys)

    def theirs(*shape):
        return pl.BlockSpec(
            (1,) + shape, lambda i, me: ((me[0] ^ of_step(keys, n, i)) * n + i % n,) + (0,) * len(shape))

    def of_key(j, *shape):
        return pl.BlockSpec((1,) + shape, lambda i, me: (jnp.clip(i - j * n, 0, n - 1),) + (0,) * len(shape))

    per = lambda *shape: pl.BlockSpec((1,) + shape, lambda i, me: (i + offset,) + (0,) * len(shape))
    tall = HEADS * rows
    flops = 2 * steps * (4 * tall * pixels * width + 4 * pixels * width * width)
    nbytes = steps * (tall * pixels * 2 + pixels * width * 10)
    sums = (jax.ShapeDtypeStruct((2 * width, width), F32), jax.ShapeDtypeStruct((width, 128), F32))
    fg = jax.ShapeDtypeStruct((images, pixels, width), F32)
    qps = (jax.ShapeDtypeStruct((n, rows, width), F32),) * len(keys)
    scratch = [pltpu.VMEM((2 * width, width), LOW)]
    middle = sums
    if last:
        middle = (jax.ShapeDtypeStruct((2 * width + 32, width), F32),)
        scratch = [pltpu.VMEM(x.shape, F32) for x in sums] + scratch
    args = (e, kv, features, cq, dn, dt, keyval_weight)
    in_specs = [per(HEADS, rows, pixels), per(2 * width, pixels), theirs(pixels, width),
                per(rows, width), theirs(rows, width), theirs(rows, 128), whole(keyval_weight)]
    aliases = {}

    def kernel(*refs):
        ins, refs = refs[:8], refs[8:]
        w_scr, refs = refs[-1], refs[:-1]
        acc_old = vb_old = g = None
        if old is not None:
            acc_old, vb_old, refs = refs[1], refs[2], refs[3:]
        fg, refs = refs[0], refs[1:]
        if last:
            g, refs = refs[0], refs[1:]
            qp, (acc, vb) = refs[:len(keys)], refs[len(keys):]
        else:
            (acc, vb), qp = refs[:2], refs[2:]
        attend_back_kernel(keys, n, last, *ins, acc_old, vb_old, fg, qp, acc, vb, g, w_scr)

    if old is not None:
        args += old
        in_specs += [pl.BlockSpec(memory_space=pl.ANY)] + [whole(x) for x in sums]
        aliases = {8: 0}
    return pl.pallas_call(
        kernel,
        grid_spec=pltpu.PrefetchScalarGridSpec(
            num_scalar_prefetch=1,
            grid=(steps,),
            in_specs=in_specs,
            out_specs=(theirs(pixels, width),) + tuple(whole(x) for x in middle) + tuple(
                of_key(j, rows, width) for j in range(len(keys))),
            scratch_shapes=scratch,
        ),
        out_shape=(fg,) + middle + qps,
        input_output_aliases=aliases,
        compiler_params=params(60),
        cost_estimate=cost(flops, nbytes),
        name="attend_back",
    )(me, *args)


def query_sum_kernel(me_ref, *refs):
    parts, kv_ref, outs = refs[:PARTS], refs[PARTS], refs[PARTS + 1:]
    n, rows, width = parts[0].shape
    total = parts[0][...]
    for p in parts[1:]:
        total = total + p[...]
    total = total.reshape(n * rows, width)
    share = kv_ref.shape[0] // PARTS
    for k, out in enumerate(outs):
        out[0:n * rows] = total
        out[n * rows:] = kv_ref[pl.ds(pl.multiple_of((me_ref[0] ^ k) * share, 8), share)]


def query_sum(me, parts, g_kv):
    n, rows, width = parts[0].shape
    args = tuple(parts) + (g_kv,)
    out = jax.ShapeDtypeStruct((n * rows + g_kv.shape[0] // PARTS, width), F32)
    return pl.pallas_call(
        query_sum_kernel,
        grid_spec=pltpu.PrefetchScalarGridSpec(
            num_scalar_prefetch=1, grid=(1,), in_specs=[whole(a) for a in args], out_specs=(whole(out),) * PARTS),
        out_shape=(out,) * PARTS,
        compiler_params=params(16),
        cost_estimate=cost(1e6, 3e6),
        name="query_sum",
    )(me, *args)


def query_back_kernel(pieces, me_ref, *refs):
    parts = refs[:pieces]
    (q_ref, dp_ref, wq_ref, qg_ref, mine_ref, away_ref, scr, sum_scr, all_scr, out_scr, g_scr, tail_scr) = refs[pieces:]
    images, rows, width = dp_ref.shape
    count = q_ref.shape[0] // images
    scale = 1.0 / math.sqrt(width // HEADS)
    n = images // pieces
    kv = jnp.zeros((parts[0].shape[0] - n * rows, width), F32)
    for k, part in enumerate(parts):
        sum_scr[pl.ds((me_ref[0] ^ k) * n, n)] = part[0:n * rows].reshape(n, rows, width)
        kv = kv + part[n * rows:]
    scr[...] = jnp.zeros_like(scr)
    slabs_in(all_scr, q_ref[...])
    for b in range(images):
        scr[b, 0:count] = take_image(all_scr, b, count, images)
    d_cq = (sum_scr[...].reshape(images * rows, width) * scale).astype(LOW)
    out = dp_ref[...] + nt(d_cq, wq_ref[...].astype(LOW)).reshape(images, rows, width)
    for b in range(images):
        put_image(out_scr, b, count, images, out[b, 0:count])
    qg_ref[...] = jnp.concatenate([out_scr[t] for t in range(out_scr.shape[0])], 1)
    g_scr[0:width] = tn(scr[...].reshape(images * rows, width).astype(LOW), d_cq)
    g_scr[width:] = jnp.zeros((g_scr.shape[0] - width, width), F32)
    g_scr[width:width + 1] = column_sum(d_cq.astype(F32))
    share = g_scr.shape[0] // pieces
    small = mine_ref.shape[0]
    tail_scr[0:kv.shape[0]] = kv
    tail_scr[kv.shape[0]:] = g_scr[pl.ds(pl.multiple_of(me_ref[0] * share, 8), share)]
    mine_ref[...] = tail_scr[pl.ds(pl.multiple_of(me_ref[2] * small, 8), small)]
    away_ref[...] = tail_scr[pl.ds(pl.multiple_of((1 - me_ref[2]) * small, 8), small)]


def query_back(me, parts, queries, dp1, query_weight):
    images, rows, width = dp1.shape
    pieces = len(parts)
    args = tuple(parts) + (queries, dp1, query_weight)
    share = parts[0].shape[0] - images // pieces * rows
    full = (width + 32) // pieces + share
    half = jax.ShapeDtypeStruct((full // 2, width), F32)
    out_shape = (jax.ShapeDtypeStruct(queries.shape, F32), half, half)
    return pl.pallas_call(
        functools.partial(query_back_kernel, pieces),
        grid_spec=pltpu.PrefetchScalarGridSpec(
            num_scalar_prefetch=1,
            grid=(1,),
            in_specs=[whole(a) for a in args],
            out_specs=tuple(whole(o) for o in out_shape),
            scratch_shapes=[pltpu.VMEM((images, rows, width), F32), pltpu.VMEM((images, rows, width), F32),
                            slabs(*queries.shape), slabs(*queries.shape), pltpu.VMEM((width + 32, width), F32),
                            pltpu.VMEM((full, width), F32)],
        ),
        out_shape=out_shape,
        compiler_params=params(24),
        cost_estimate=cost(5e8, 8e6),
        name="query_back",
    )(me, *args)


def unpack_kernel(split, me_ref, *refs):
    own, other = refs[:8], refs[8:16]
    (tail, tail2,
     query_ref, query_bias_ref, keyval_ref, value_bias_ref, cross_ref, cross_bias_ref, gain_ref, nbias_ref,
     self_ref, self_bias_ref, selfout_ref, selfout_bias_ref, hidden_ref, hidden_bias_ref, hidout_ref, hidout_bias_ref,
     embed_ref, embed_bias_ref, g, t) = refs[16:]
    pix, core, z = me_ref[1], me_ref[2], me_ref[3]
    width = query_ref.shape[0]
    short = own[0].shape[0] // 2
    for half, eight in ((core, own), (1 - core, other)):
        for k in range(4):
            for j in range(4):
                at = ((pix ^ k) * 2 + half) * 4 + (z ^ j)
                piece = eight[2 * k + j // 2]
                g[pl.ds(pl.multiple_of(at * short, 8), short)] = piece[j % 2 * short:(j % 2 + 1) * short]
    small = tail.shape[0] // 4
    for half, ref in ((core, tail), (1 - core, tail2)):
        for k in range(4):
            at = (pix ^ k) * 2 + half
            t[pl.ds(pl.multiple_of(at * small, 8), small)] = ref[k * small:(k + 1) * small]

    def tile(n, k=1):
        return g[n * width:(n + k) * width]

    many = hidden_ref.shape[1] // width
    bias = (T_HIDDEN + 2 * many) * width
    cross_ref[...] = tile(T_CROSS)
    selfout_ref[...] = tile(T_SELFOUT)
    embed_ref[...] = tile(T_EMBED, 3)
    hidout_ref[...] = tile(T_HIDDEN + many, many)
    for n in range(3):
        self_ref[:, n * width:(n + 1) * width] = tile(T_SELF + n)
    for n in range(many):
        hidden_ref[:, n * width:(n + 1) * width] = tile(T_HIDDEN + n)
        hidden_bias_ref[:, n * width:(n + 1) * width] = g[bias + 8 + n:bias + 9 + n]
    cross_bias_ref[...] = g[bias:bias + 1]
    gain_ref[...] = g[bias + 1:bias + 4]
    nbias_ref[...] = g[bias + 4:bias + 7]
    selfout_bias_ref[...] = g[bias + 7:bias + 8]
    hidout_bias_ref[...] = g[bias + 16:bias + 17]
    embed_bias_ref[...] = g[bias + 17:bias + 20]
    self_bias_ref[...] = g[bias + 20:bias + 22]
    block = 2 * small
    low, high = [], []
    for k in range(4):
        low.append(t[k * block:k * block + split])
        high.append(t[k * block + split:(k + 1) * block])
    low, high = jnp.concatenate(low, 0), jnp.concatenate(high, 0)
    keyval_ref[:, 0:width] = low[0:width]
    keyval_ref[:, width:] = low[width:2 * width]
    value_bias_ref[...] = low[2 * width:2 * width + 1]
    query_ref[...] = high[0:width]
    query_bias_ref[...] = high[width:width + 1]


def unpack(me, pieces, tails, split, width, hidden):
    args = tuple(pieces) + tuple(tails)
    shapes = ((width, width), (1, width), (width, 2 * width), (1, width), (width, width), (1, width), (3, width), (3, width),
              (width, 3 * width), (2, width), (width, width), (1, width), (width, hidden), (1, hidden), (hidden, width),
              (1, width), (3 * width, width), (3, width))
    out_shape = tuple(jax.ShapeDtypeStruct(shape, F32) for shape in shapes)
    rows = sum(p.shape[0] for p in pieces)
    return pl.pallas_call(
        functools.partial(unpack_kernel, split),
        grid_spec=pltpu.PrefetchScalarGridSpec(
            num_scalar_prefetch=1,
            grid=(1,),
            in_specs=[whole(a) for a in args],
            out_specs=tuple(whole(o) for o in out_shape),
            scratch_shapes=[pltpu.VMEM((rows, width), F32), pltpu.VMEM((2 * tails[0].shape[0], width), F32)],
        ),
        out_shape=out_shape,
        compiler_params=params(32),
        cost_estimate=cost(1e6, 16e6),
        name="unpack",
    )(me, *args)


def beside(*values):
    return lax.optimization_barrier(values)


def swap(x, axis, n, key):
    return lax.ppermute(x, axis, [(d, d ^ key) for d in range(n)])


def scatter_out(x, axis, n):
    me = lax.axis_index(axis)
    chunks = [lax.dynamic_index_in_dim(x, me ^ k, 0, keepdims=False) for k in range(n)]
    return tuple(c if k == 0 else swap(c, axis, n, k) for k, c in enumerate(chunks))


def gather_in(x, axis, n):
    return tuple(x if k == 0 else swap(x, axis, n, k) for k in range(n))


def side(axis, key):
    return (lax.axis_index(axis) // key) % 2


def halve(x, axis, n, key):
    halves = x.reshape((2, -1) + x.shape[1:])
    mine = lax.dynamic_index_in_dim(halves, side(axis, key), 0, keepdims=False)
    away = lax.dynamic_index_in_dim(halves, 1 - side(axis, key), 0, keepdims=False)
    return mine, swap(away, axis, n, key)


def join(mine, other, axis, key):
    first = side(axis, key) == 0
    return jnp.concatenate([jnp.where(first, mine, other), jnp.where(first, other, mine)], 0)


def local(
    queries, features, mask_features, attend_bits, reopen_flags, matched_queries, query_cotan, mask_cotan,
    query_weight, query_bias, keyval_weight, value_bias, cross_out, cross_out_bias, norm_gain, norm_bias,
    self_weight, self_bias, self_out, self_out_bias, hidden_weight, hidden_bias, hidden_out, hidden_out_bias,
    embed_weight, embed_bias, *, n_pix, n_batch,
):
    images, count, width = queries.shape
    hidden = hidden_weight.shape[1]
    rows = up(count, 8)
    tall = rows + HEADS
    pix = lax.axis_index("pix")
    direct = n_pix == 4 and n_batch == 8

    queries = jnp.transpose(queries, (1, 0, 2)).reshape(count * images, width)
    query_cotan = jnp.transpose(query_cotan, (1, 0, 2))
    mask_cotan = jnp.transpose(mask_cotan, (1, 0, 2))
    bits = jnp.transpose(attend_bits, (0, 2, 1))
    core = lax.axis_index("batch") % 2
    chip = lax.axis_index("batch") // 2
    me = jnp.stack([pix if direct else 0 * pix, pix, core, chip]).astype(jnp.int32)

    def forward(keys, flags, masks=None):
        return attend(keys, me, queries, features, bits, flags, query_weight, query_bias, keyval_weight, value_bias,
                      PARTS, masks)

    far, near = (3, 1, 2), (0,)
    *kept, pay3, pay1, pay2, es = forward(far, reopen_flags, (mask_cotan, mask_features))
    pay3, pay1, pay2, reopen_flags = beside(pay3, pay1, pay2, reopen_flags)
    pays = {3: pay3, 1: pay1, 2: pay2}
    got = {k: swap(pays[k], "pix", n_pix, k) for k in far} if direct else {}
    *kept_near, pays[0] = forward(near, reopen_flags)
    if direct:
        pays[0], *arrived = beside(pays[0], *[got[k] for k in far])
        got.update(zip(far, arrived))
        got[0] = pays[0]
    pays = [pays[k] for k in range(PARTS)]
    weights = (
        cross_out, cross_out_bias[None], norm_gain, norm_bias, self_weight, self_bias, self_out, self_out_bias[None],
        hidden_weight, hidden_bias[None], hidden_out, hidden_out_bias[None], embed_weight, embed_bias,
    )
    large = (0, 4, 6, 8, 10, 12)
    if direct:
        share = combine([got[k] for k in range(PARTS)], es, rows)
        share, *raw = beside(share, *[weights[k] for k in large])
        att = gather_in(share, "pix", n_pix)
    else:
        raw = [weights[k] for k in large]
        pay = jnp.concatenate([jnp.concatenate([pays[0], es], 1)] + pays[1:], 0)
        top = lax.pmax(pay[:, rows:tall, :128], "pix")
        ratio = jnp.exp(pay[:, rows:tall, :128] - top)

        def widen(x):
            return jnp.repeat(jnp.transpose(x, (0, 2, 1))[:, :rows], width // HEADS, axis=2)

        numer, total, es = lax.psum(
            (pay[:, :rows] * widen(ratio), pay[:, rows:tall, 128:] * ratio, pay[:, tall:]), "pix")
        att = (jnp.concatenate([numer / widen(total), jnp.concatenate([top, total], 2), es], 1),)
    lowered = dict(zip(large, lower(raw)))
    weights = tuple(lowered.get(k, w) for k, w in enumerate(weights))
    x3, emb, dn, dt, dp1, mine, away = chain(
        me, att, pays, queries, matched_queries, query_cotan, weights, n_pix)

    def unflat(x):
        return jnp.transpose(x.reshape(count, images, -1), (1, 0, 2))

    blocks = mask_features.shape[1] // 512
    mask = functools.partial(mask_out, emb, matched_queries, mask_cotan, mask_features, count, blocks)

    def backward(keys, old, last=False):
        offset = 0 if keys[0] in near else far.index(keys[0]) * images // PARTS
        return attend_back(keys, me, kept_near if keys[0] in near else kept, offset, features, dn, dt, keyval_weight, old, last)

    def z_scatter(chunks):
        got = [lax.dynamic_index_in_dim(chunks, chip ^ k, 0, keepdims=False) for k in range(4)]
        return [got[0]] + [swap(got[k], "batch", n_batch, 2 * k) for k in (1, 2, 3)]

    other = swap(away, "batch", n_batch, 1)
    if direct:
        fg, acc, vb, qp0 = backward(near, None)
        other, fg, acc, vb, qp0 = beside(other, fg, acc, vb, qp0)
        sums = z_scatter((mine + other).reshape(n_batch // 2, -1, width))
        feat_grad, g_kv, qp3, qp1, qp2 = backward(far, (fg, acc, vb), True)
        *sums, feat_grad, g_kv, qp1, qp2, qp3 = beside(*sums, feat_grad, g_kv, qp1, qp2, qp3)
        qp1, qp2, qp3 = [swap(q, "pix", n_pix, k) for k, q in zip((1, 2, 3), (qp1, qp2, qp3))]
        own = functools.reduce(jnp.add, sums)
        same = [own] + [swap(own, "batch", n_batch, k) for k in (2, 4, 6)]
        cuts = [blocks * k // 8 for k in (0, 2, 5, 8)]
        outs = mask((cuts[0], cuts[1]))
        qp1, qp2, qp3, outs = beside(qp1, qp2, qp3, outs)
        split = g_kv.shape[0] // n_pix
        parts = query_sum(me, (qp0, qp1, qp2, qp3), g_kv)
        parts = tuple(p if k == 0 else swap(p, "pix", n_pix, k) for k, p in enumerate(parts))
        outs = mask((cuts[1], cuts[2]), outs)
        parts, outs, *same = beside(parts, outs, *same)
        low, high = jnp.concatenate(same[:2], 0), jnp.concatenate(same[2:], 0)
        low1, high2 = swap(low, "pix", n_pix, 1), swap(high, "pix", n_pix, 2)
        low0, high0 = swap(low, "batch", n_batch, 1), swap(high, "batch", n_batch, 1)
        queries_grad, tail, tail2 = query_back(me, parts, queries, dp1, query_weight)
        tail2 = swap(tail2, "batch", n_batch, 1)
        outs = mask((cuts[2], cuts[3]), outs)
        low1, high2, low0, high0, tail2, outs = beside(low1, high2, low0, high0, tail2, outs)
        tail = tail + tail2
        tail2 = swap(tail, "batch", n_batch, 2)
        low2, high1 = swap(low, "pix", n_pix, 2), swap(high, "pix", n_pix, 1)
        low3, high3 = swap(low1, "pix", n_pix, 2), swap(high2, "pix", n_pix, 1)
        tail = tail + tail2
        tail = tail + swap(tail, "batch", n_batch, 4)
        tail = jnp.concatenate([tail] + [swap(tail, "pix", n_pix, k) for k in (1, 2, 3)], 0)
        pieces = [low, high, low1, high1, low2, high2, low3, high3]
        pieces += [low0, high0] + [swap(p, "batch", n_batch, 1) for p in pieces[2:]]
        tails = (tail, swap(tail, "batch", n_batch, 1))
        grads = unpack(me, pieces, tails, split, width, hidden)
        (d_query, d_query_bias, d_keyval, d_value_bias, d_cross, d_cross_bias, d_gain, d_nbias, d_self, d_self_bias,
         d_selfout, d_selfout_bias, d_hidden, d_hidden_bias, d_hidout, d_hidout_bias, d_embed, d_embed_bias) = grads
    else:
        old, parts = None, {}
        for keys, last in ((near, False), (far, True)):
            back = backward(keys, old, last)
            count_sums = 1 if last else 2
            old = back[:1 + count_sums]
            parts.update(zip(keys, back[1 + count_sums:]))
        feat_grad, g_kv = old
        parts = [parts[k] for k in range(PARTS)]
        qp = jnp.concatenate(parts, 0)
        outs = mask((0, blocks))
        sums = jnp.concatenate([lax.psum(qp, "pix").reshape(images * rows, width), g_kv], 0)
        queries_grad, tail, tail2 = query_back(me, (sums,), queries, dp1, query_weight)
        first = core == 0
        tail = jnp.concatenate([jnp.where(first, tail, tail2), jnp.where(first, tail2, tail)], 0)
        g_q = lax.psum(tail[g_kv.shape[0]:], "batch")
        g_kv = lax.psum(g_kv, ("batch", "pix"))
        every = [(2 * z, 2 * z + 1) for z in range(n_batch // 2)]
        groups = [[z[c] for z in every] for c in range(2)]
        part = lax.psum(mine + other, "batch", axis_index_groups=groups)
        both = lax.all_gather(part, "batch", axis_index_groups=[list(z) for z in every])
        packed = lax.all_gather(both, "pix").reshape(-1, width)

        def tile(t, k=1):
            return packed[t * width:(t + k) * width]

        def wide(t, k):
            return jnp.concatenate([tile(t + j) for j in range(k)], 1)

        many = hidden // width
        bias = packed[(T_HIDDEN + 2 * many) * width:]
        d_query, d_query_bias = g_q[:width], g_q[width]
        d_keyval, d_value_bias = jnp.concatenate([g_kv[:width], g_kv[width:2 * width]], 1), g_kv[2 * width]
        d_cross, d_cross_bias, d_gain, d_nbias = tile(T_CROSS), bias[0], bias[1:4], bias[4:7]
        d_self, d_self_bias, d_selfout, d_selfout_bias = wide(T_SELF, 3), bias[20:22], tile(T_SELFOUT), bias[7]
        d_hidden, d_hidden_bias = wide(T_HIDDEN, many), bias[8:8 + many]
        d_hidout, d_hidout_bias = tile(T_HIDDEN + many, many), bias[16]
        d_embed, d_embed_bias = tile(T_EMBED, 3), bias[17:20]
    logits, mask_grad = outs
    return (
        unflat(x3),
        unflat(logits),
        unflat(queries_grad),
        feat_grad,
        mask_grad,
        d_query,
        d_query_bias.reshape(-1),
        d_keyval,
        d_value_bias.reshape(-1),
        d_cross,
        d_cross_bias.reshape(-1),
        d_gain,
        d_nbias,
        d_self,
        d_self_bias,
        d_selfout,
        d_selfout_bias.reshape(-1),
        d_hidden,
        d_hidden_bias.reshape(-1),
        d_hidout,
        d_hidout_bias.reshape(-1),
        d_embed.reshape(3, width, width),
        d_embed_bias,
    )


def solution(mesh):
    n_pix, n_batch = mesh.shape["pix"], mesh.shape["batch"]
    rep = P()
    row, pixel, column = P("batch", None, None), P("batch", "pix", None), P("batch", None, "pix")
    in_specs = (row, pixel, pixel, column, P("batch", None), P("batch", None), row, column) + (rep,) * 18
    out_specs = (row, column, row, pixel, pixel) + (rep,) * 18
    body = functools.partial(local, n_pix=n_pix, n_batch=n_batch)
    return jax.shard_map(body, mesh=mesh, in_specs=in_specs, out_specs=out_specs, check_vma=False)
```

profile of v0, /device:TPU:0, one launch (start us, length us, event | category | flops | bytes accessed | tf_op | source)
XLA Modules:
  0.0 251.7 jit_solution(10241515395077860291)
XLA Ops:
  1.3 24.5 %attend.2 = (bf16[6,8,104,1024]{3,2,1,0:T(8,128)(2,1)}, bf16[6,512,1024]{2,1,0:T(8,128)(2,1)}, f32[6,104,256]{2,1,0:T(8,128)}, f32[2,168,256]{2,1,0:T(8,128)}, f...) custom-call(s32[4]{0:T(128)} %pad_add_fusion.me_ref.refs_0_, f32[800,256]{1,0:T(8,128)} %bitcast.40, ...), custom_call_target="tpu_custom_call" | custom-call | flops 6845104128 | bytes 34701312 | tf_op jit(solution)/shard_map/attend/pallas_call | solution.py:259
  25.8 3.9 %collective-permute-start = (f32[2,168,256]{2,1,0:T(8,128)}, f32[2,168,256]{2,1,0:T(8,128)S(1)}, u32[]{:S(2)}, u32[]{:S(2)}) collective-permute-start(f32[2,168,256]{2,1,0:T(8,128)} %get-tuple-element.143.refs_7_), channel_id=1, source_target_pairs={{0,3},{1,2},{2,1},{3,0},{4,7},{5,6},{6,5},{7,4},{8,11},{9,10},{10,... | collective-permute-start | bytes 1032200 | tf_op jit(solution)/shard_map/ppermute | solution.py:985
  30.4 8.5 %attend.3 = (bf16[2,8,104,1024]{3,2,1,0:T(8,128)(2,1)}, bf16[2,512,1024]{2,1,0:T(8,128)(2,1)}, f32[2,104,256]{2,1,0:T(8,128)}, f32[2,112,256]{2,1,0:T(8,128)}) custom-call(s32[4]{0:T(128)} %pad_add_fusion.me_ref.refs_0_, f32[800,256]{1,0:T(8,128)} %bitcast.41, bf16[8,1024,256]{2,1,0:T(8,128)(2,1)} %refs_3_.7, s32[8,64,100]{2,1,0:T(8,128)} %bitcast.51, ...), custom_call_target="tpu_custom_call" | custom-call | flops 2281701376 | bytes 6553600 | tf_op jit(solution)/shard_map/attend/pallas_call | solution.py:259
  39.7 6.2 %collective-permute-done.1.refs_1_ = f32[2,168,256]{2,1,0:T(8,128)} collective-permute-done((f32[2,168,256]{2,1,0:T(8,128)}, f32[2,168,256]{2,1,0:T(8,128)}, u32[]{:S(2)}, u32[]{:S(2)}) %collective-permute-start.1) | collective-permute-done | bytes 344096 | tf_op jit(solution)/shard_map/ppermute | solution.py:985
  45.8 1.0 copy-done.18
  47.7 2.2 combine.1.refs_0_
  49.9 1.6 collective-permute-start.3
  51.5 1.4 collective-permute-start.4
  53.5 1.6 copy-done.2
  56.0 0.9 copy-done.20
  57.3 1.0 copy-done.25
  58.3 1.0 copy-done.26
  62.0 6.4 %collective-permute-done.4.refs_2_ = f32[2,168,256]{2,1,0:T(8,128)S(1)} collective-permute-done((f32[2,168,256]{2,1,0:T(8,128)S(1)}, f32[2,168,256]{2,1,0:T(8,128)S(1)}, u32[]{:S(2)}, u32[]{:S(2)}) %collective-permute-start.4) | collective-permute-done | bytes 344096 | tf_op jit(solution)/shard_map/ppermute | solution.py:985
  69.4 37.6 %chain.1 = (f32[800,256]{1,0:T(8,128)}, f32[800,256]{1,0:T(8,128)}, f32[8,104,256]{2,1,0:T(8,128)}, f32[8,104,128]{2,1,0:T(8,128)}, f32[8,104,256]{2,1,0:T(8,128...) custom-call(s32[4]{0:T(128)} %pad_add_fusion.me_ref.refs_0_, f32[2,168,256]{2,1,0:T(8,128)} %copy-done.16, ...), custom_call_target="tpu_custom_call" | custom-call | flops 16000000000 | bytes 20000000 | tf_op jit(solution)/shard_map/chain/pallas_call | solution.py:586
  107.1 9.9 %attend_back.2 = (f32[8,1024,256]{2,1,0:T(8,128)}, f32[512,256]{1,0:T(8,128)}, f32[256,128]{1,0:T(8,128)}, f32[2,104,256]{2,1,0:T(8,128)}) custom-call(s32[4]{0:T(128)} %pad_add_fusion.me_ref.refs_0_, bf16[2,8,104,1024]{3,2,1,0:T(8,128)(2,1)} %get-tuple-element.166.refs_1_, bf16[2,512,1024]{2,1,0:T(8,128)(2,1)} %get-tuple-element.167.refs_2_, ...), custom_call_target="tpu_custom_call" | custom-call | flops 4563402752 | bytes 8650752 | tf_op jit(solution)/shard_map/attend_back/pallas_call | solution.py:799
  117.2 1.6 collective-permute-start.7
  118.9 2.6 %collective-permute-start.8 = (f32[200,256]{1,0:T(8,128)S(1)}, f32[200,256]{1,0:T(8,128)S(1)}, u32[]{:S(2)}, u32[]{:S(2)}) collective-permute-start(f32[200,256]{1,0:T(8,128)S(1)} %get-tuple-element.254), channel_id=1, source_target_pairs={{0,16},{4,20},{8,24},{12,28},{16,0},{20,4},{24,8},{28,12},{1,17},{... | collective-permute-start | bytes 614408 | tf_op jit(solution)/shard_map/ppermute | solution.py:985
  121.7 20.9 %attend_back.3 = (f32[8,1024,256]{2,1,0:T(8,128)}, f32[544,256]{1,0:T(8,128)}, f32[2,104,256]{2,1,0:T(8,128)}, f32[2,104,256]{2,1,0:T(8,128)}, f32[2,104,256]{2,1,0:T(8,128)}) custom-call(s32[4]{0:T(128)} %pad_add_fusion.me_ref.refs_0_, bf16[6,8,104,1024]{3,2,1,0:T(8,128)(2,1)} %get-tuple-element.178.refs_1_, ...), custom_call_target="tpu_custom_call", output_to_operand_aliasing={{0}: (8, {})} | custom-call | flops 13690208256 | bytes 25952256 | tf_op jit(solution)/shard_map/attend_back/pallas_call | solution.py:799
  142.6 1.2 collective-permute-start.10
  144.7 1.5 collective-permute-start.12
  147.0 8.4 %mask_out.3 = (f32[800,4096]{1,0:T(8,128)}, f32[8,4096,256]{2,1,0:T(8,128)}) custom-call(f32[800,256]{1,0:T(8,128)} %get-tuple-element.192.a.emb_ref, s32[8,50]{1,0:T(8,128)} %match_ref.3, bf16[50,8,4096]{2,1,0:T(8,128)(2,1)} %bitcast.46, bf16[8,4096,256]{2,1,0:T(8,128)(2,1)} %mf_ref.3), custom_call_target="tpu_custom_call" | custom-call | flops 671088640 | bytes 16678912 | tf_op jit(solution)/shard_map/mask_out/pallas_call | solution.py:666
  155.4 1.4 query_sum.1
  157.5 1.1 collective-permute-start.13
  158.7 1.0 collective-permute-start.14
  159.7 1.4 collective-permute-start.15
  161.0 3.5 %collective-permute-start.17 = (f32[200,256]{1,0:T(8,128)S(1)}, f32[200,256]{1,0:T(8,128)}, u32[]{:S(2)}, u32[]{:S(2)}) collective-permute-start(f32[200,256]{1,0:T(8,128)S(1)} %add_add_fusion), channel_id=1, source_target_pairs={{0,16},{4,20},{8,24},{12,28},{16,0},{20,4},{24,8},{28,12},{1,17},{... | collective-permute-start | bytes 614408 | tf_op jit(solution)/shard_map/ppermute | solution.py:985
  164.7 11.7 %mask_out.4 = (f32[800,4096]{1,0:T(8,128)}, f32[8,4096,256]{2,1,0:T(8,128)}) custom-call(f32[800,256]{1,0:T(8,128)} %get-tuple-element.192.a.emb_ref, s32[8,50]{1,0:T(8,128)} %match_ref.3, bf16[50,8,4096]{2,1,0:T(8,128)(2,1)} %bitcast.47, bf16[8,4096,256]{2,1,0:T(8,128)(2,1)} %mf_ref.3, ...), custom_call_target="tpu_custom_call", output_to_operand_aliasing={{0}: (4, {}), {1}: (5, {})} | custom-call | flops 1006632960 | bytes 25018368 | tf_op jit(solution)/shard_map/mask_out/pallas_call | solution.py:666
  178.7 1.1 constant_dynamic-update-slice_fusion.3
  180.7 1.6 collective-permute-start.20
  184.1 1.0 copy-done.9
  185.1 1.0 copy-done.11
  186.1 1.0 copy-done.13
  187.1 1.0 copy-done.15
  188.0 2.1 query_back.1
  190.5 1.0 collective-permute-done.23
  191.5 1.5 collective-permute-start.24
  193.0 11.7 %mask_out.5 = (f32[800,4096]{1,0:T(8,128)}, f32[8,4096,256]{2,1,0:T(8,128)}) custom-call(f32[800,256]{1,0:T(8,128)} %get-tuple-element.192.a.emb_ref, s32[8,50]{1,0:T(8,128)} %match_ref.3, bf16[50,8,4096]{2,1,0:T(8,128)(2,1)} %bitcast.48, bf16[8,4096,256]{2,1,0:T(8,128)(2,1)} %mf_ref.3, ...), custom_call_target="tpu_custom_call", output_to_operand_aliasing={{0}: (4, {}), {1}: (5, {})} | custom-call | flops 1006632960 | bytes 25018368 | tf_op jit(solution)/shard_map/mask_out/pallas_call | solution.py:666
  204.7 4.1 %collective-permute-start.34 = (f32[104,256]{1,0:T(8,128)S(1)}, f32[104,256]{1,0:T(8,128)S(1)}, u32[]{:S(2)}, u32[]{:S(2)}) collective-permute-start(f32[104,256]{1,0:T(8,128)S(1)} %add.48), channel_id=1, source_target_pairs={{0,8},{4,12},{8,0},{12,4},{16,24},{20,28},{24,16},{28,20},{1,9},{5... | collective-permute-start | bytes 319496 | tf_op jit(solution)/shard_map/ppermute | solution.py:985
  208.7 3.1 %collective-permute-done.34 = f32[104,256]{1,0:T(8,128)S(1)} collective-permute-done((f32[104,256]{1,0:T(8,128)S(1)}, f32[104,256]{1,0:T(8,128)S(1)}, u32[]{:S(2)}, u32[]{:S(2)}) %collective-permute-start.34) | collective-permute-done | bytes 106528 | tf_op jit(solution)/shard_map/ppermute | solution.py:985
  211.9 2.8 %collective-permute-start.35 = (f32[104,256]{1,0:T(8,128)S(1)}, f32[104,256]{1,0:T(8,128)S(1)}, u32[]{:S(2)}, u32[]{:S(2)}) collective-permute-start(f32[104,256]{1,0:T(8,128)S(1)} %add.49), channel_id=1, source_target_pairs={{0,16},{4,20},{8,24},{12,28},{16,0},{20,4},{24,8},{28,12},{1,17},{... | collective-permute-start | bytes 319496 | tf_op jit(solution)/shard_map/ppermute | solution.py:985
  214.7 4.8 %collective-permute-done.35 = f32[104,256]{1,0:T(8,128)S(1)} collective-permute-done((f32[104,256]{1,0:T(8,128)S(1)}, f32[104,256]{1,0:T(8,128)S(1)}, u32[]{:S(2)}, u32[]{:S(2)}) %collective-permute-start.35) | collective-permute-done | bytes 106528 | tf_op jit(solution)/shard_map/ppermute | solution.py:985
  220.2 1.1 collective-permute-start.37
  221.2 1.8 collective-permute-start.38
  223.6 1.5 collective-permute-start.26
  226.3 1.7 collective-permute-done.38
  228.1 8.1 %collective-permute-done.25.refs_4_ = f32[400,256]{1,0:T(8,128)S(1)} collective-permute-done((f32[400,256]{1,0:T(8,128)S(1)}, f32[400,256]{1,0:T(8,128)S(1)}, u32[]{:S(2)}, u32[]{:S(2)}) %collective-permute-start.25) | collective-permute-done | bytes 409632 | tf_op jit(solution)/shard_map/ppermute | solution.py:985
  236.2 6.9 %collective-permute-done.26.refs_6_ = f32[400,256]{1,0:T(8,128)S(1)} collective-permute-done((f32[400,256]{1,0:T(8,128)S(1)}, f32[400,256]{1,0:T(8,128)S(1)}, u32[]{:S(2)}, u32[]{:S(2)}) %collective-permute-start.26) | collective-permute-done | bytes 409632 | tf_op jit(solution)/shard_map/ppermute | solution.py:985
  246.6 4.9 %unpack.1 = (f32[256,256]{1,0:T(8,128)}, f32[1,256]{1,0:T(1,128)}, f32[256,512]{1,0:T(8,128)}, f32[1,256]{1,0:T(1,128)}, f32[256,256]{1,0:T(8,128)}, /*index=5*/...) custom-call(s32[4]{0:T(128)S(1)} %copy-done.24, ...), custom_call_target="tpu_custom_call" | custom-call | flops 1000000 | bytes 16000000 | tf_op jit(solution)/shard_map/unpack/pallas_call | solution.py:964
  (127 shorter events, 23.0 us)
Async XLA Ops:
  25.8 20.0 %copy-start.23 = (f32[2,56,256]{2,1,0:T(8,128)S(1)}, f32[2,56,256]{2,1,0:T(8,128)}, u32[]{:S(2)}) copy-start(f32[2,56,256]{2,1,0:T(8,128)} %get-tuple-element.150.refs_4_) | copy-start | bytes 344068
  25.8 27.7 %copy-start.1 = (f32[256,2048]{1,0:T(8,128)S(1)}, f32[256,2048]{1,0:T(8,128)}, u32[]{:S(2)}) copy-start(f32[256,2048]{1,0:T(8,128)} %refs_3_.5) | copy-start | bytes 6291460
  25.8 27.7 %copy-start.5 = (f32[256,768]{1,0:T(8,128)S(1)}, f32[256,768]{1,0:T(8,128)}, u32[]{:S(2)}) copy-start(f32[256,768]{1,0:T(8,128)} %refs_1_.4) | copy-start | bytes 2359300
  25.8 27.7 %copy-start.6 = (f32[3,256,256]{2,1,0:T(8,128)S(1)}, f32[3,256,256]{2,1,0:T(8,128)}, u32[]{:S(2)}) copy-start(f32[3,256,256]{2,1,0:T(8,128)} %refs_5_) | copy-start | bytes 2359300
  25.8 13.1 %collective-permute-start = (f32[2,168,256]{2,1,0:T(8,128)}, f32[2,168,256]{2,1,0:T(8,128)S(1)}, u32[]{:S(2)}, u32[]{:S(2)}) collective-permute-start(f32[2,168,256]{2,1,0:T(8,128)} %get-tuple-element.143.refs_7_), channel_id=1, source_target_pairs={{0,3},{1,2},{2,1},{3,0},{4,7},{5,6},{6,5},{7,4},{8,11},{9,10},{10,... | collective-permute-start | bytes 1032200 | tf_op jit(solution)/shard_map/ppermute | solution.py:985
  29.8 16.0 %collective-permute-start.1 = (f32[2,168,256]{2,1,0:T(8,128)}, f32[2,168,256]{2,1,0:T(8,128)}, u32[]{:S(2)}, u32[]{:S(2)}) collective-permute-start(f32[2,168,256]{2,1,0:T(8,128)} %get-tuple-element.144.refs_5_), channel_id=1, source_target_pairs={{0,1},{1,0},{2,3},{3,2},{4,5},{5,4},{6,7},{7,6},{8,9},{9,8},{10,11... | collective-permute-start | bytes 1032200 | tf_op jit(solution)/shard_map/ppermute | solution.py:985
  30.3 15.5 %collective-permute-start.2 = (f32[2,168,256]{2,1,0:T(8,128)}, f32[2,168,256]{2,1,0:T(8,128)}, u32[]{:S(2)}, u32[]{:S(2)}) collective-permute-start(f32[2,168,256]{2,1,0:T(8,128)} %get-tuple-element.145.refs_6_), channel_id=1, source_target_pairs={{0,2},{1,3},{2,0},{3,1},{4,6},{5,7},{6,4},{7,5},{8,10},{9,11},{10,... | collective-permute-start | bytes 1032200 | tf_op jit(solution)/shard_map/ppermute | solution.py:985
  49.9 19.5 %copy-start.16 = (f32[2,168,256]{2,1,0:T(8,128)}, f32[2,168,256]{2,1,0:T(8,128)S(1)}, u32[]{:S(2)}) copy-start(f32[2,168,256]{2,1,0:T(8,128)S(1)} %combine.1.refs_0_) | copy-start | bytes 1032196
  49.9 12.1 %collective-permute-start.3 = (f32[2,168,256]{2,1,0:T(8,128)S(1)}, f32[2,168,256]{2,1,0:T(8,128)S(1)}, u32[]{:S(2)}, u32[]{:S(2)}) collective-permute-start(f32[2,168,256]{2,1,0:T(8,128)S(1)} %combine.1.refs_0_), channel_id=1, source_target_pairs={{0,1},{1,0},{2,3},{3,2},{4,5},{5,4},{6,7},{7,6},{8,9},{9,8},{10,11... | collective-permute-start | bytes 1032200 | tf_op jit(solution)/shard_map/ppermute | solution.py:985
  51.5 17.0 %collective-permute-start.4 = (f32[2,168,256]{2,1,0:T(8,128)S(1)}, f32[2,168,256]{2,1,0:T(8,128)S(1)}, u32[]{:S(2)}, u32[]{:S(2)}) collective-permute-start(f32[2,168,256]{2,1,0:T(8,128)S(1)} %combine.1.refs_0_), channel_id=1, source_target_pairs={{0,2},{1,3},{2,0},{3,1},{4,6},{5,7},{6,4},{7,5},{8,10},{9,11},{10,... | collective-permute-start | bytes 1032200 | tf_op jit(solution)/shard_map/ppermute | solution.py:985
  52.9 15.6 %collective-permute-start.5 = (f32[2,168,256]{2,1,0:T(8,128)S(1)}, f32[2,168,256]{2,1,0:T(8,128)S(1)}, u32[]{:S(2)}, u32[]{:S(2)}) collective-permute-start(f32[2,168,256]{2,1,0:T(8,128)S(1)} %combine.1.refs_0_), channel_id=1, source_target_pairs={{0,3},{1,2},{2,1},{3,0},{4,7},{5,6},{6,5},{7,4},{8,11},{9,10},{10,... | collective-permute-start | bytes 1032200 | tf_op jit(solution)/shard_map/ppermute | solution.py:985
  107.0 10.0 %collective-permute-start.6 = (f32[800,256]{1,0:T(8,128)}, f32[800,256]{1,0:T(8,128)S(1)}, u32[]{:S(2)}, u32[]{:S(2)}) collective-permute-start(f32[800,256]{1,0:T(8,128)} %get-tuple-element.165), channel_id=1, source_target_pairs={{0,4},{4,0},{8,12},{12,8},{16,20},{20,16},{24,28},{28,24},{1,5},{5... | collective-permute-start | bytes 2457608 | tf_op jit(solution)/shard_map/ppermute | solution.py:985
  117.2 25.4 %collective-permute-start.7 = (f32[200,256]{1,0:T(8,128)S(1)}, f32[200,256]{1,0:T(8,128)S(1)}, u32[]{:S(2)}, u32[]{:S(2)}) collective-permute-start(f32[200,256]{1,0:T(8,128)S(1)} %get-tuple-element.255), channel_id=1, source_target_pairs={{0,8},{4,12},{8,0},{12,4},{16,24},{20,28},{24,16},{28,20},{1,9},{5... | collective-permute-start | bytes 614408 | tf_op jit(solution)/shard_map/ppermute | solution.py:985
  118.9 23.8 %collective-permute-start.8 = (f32[200,256]{1,0:T(8,128)S(1)}, f32[200,256]{1,0:T(8,128)S(1)}, u32[]{:S(2)}, u32[]{:S(2)}) collective-permute-start(f32[200,256]{1,0:T(8,128)S(1)} %get-tuple-element.254), channel_id=1, source_target_pairs={{0,16},{4,20},{8,24},{12,28},{16,0},{20,4},{24,8},{28,12},{1,17},{... | collective-permute-start | bytes 614408 | tf_op jit(solution)/shard_map/ppermute | solution.py:985
  121.5 21.2 %collective-permute-start.9 = (f32[200,256]{1,0:T(8,128)S(1)}, f32[200,256]{1,0:T(8,128)S(1)}, u32[]{:S(2)}, u32[]{:S(2)}) collective-permute-start(f32[200,256]{1,0:T(8,128)S(1)} %get-tuple-element.253), channel_id=1, source_target_pairs={{0,24},{4,28},{8,16},{12,20},{16,8},{20,12},{24,0},{28,4},{1,25},{... | collective-permute-start | bytes 614408 | tf_op jit(solution)/shard_map/ppermute | solution.py:985
  142.6 12.7 %collective-permute-start.10 = (f32[2,104,256]{2,1,0:T(8,128)}, f32[2,104,256]{2,1,0:T(8,128)S(1)}, u32[]{:S(2)}, u32[]{:S(2)}) collective-permute-start(f32[2,104,256]{2,1,0:T(8,128)} %get-tuple-element.189), channel_id=1, source_target_pairs={{0,1},{1,0},{2,3},{3,2},{4,5},{5,4},{6,7},{7,6},{8,9},{9,8},{10,11... | collective-permute-start | bytes 638984 | tf_op jit(solution)/shard_map/ppermute | solution.py:985
  143.8 11.6 %collective-permute-start.11 = (f32[2,104,256]{2,1,0:T(8,128)}, f32[2,104,256]{2,1,0:T(8,128)S(1)}, u32[]{:S(2)}, u32[]{:S(2)}) collective-permute-start(f32[2,104,256]{2,1,0:T(8,128)} %get-tuple-element.190), channel_id=1, source_target_pairs={{0,2},{1,3},{2,0},{3,1},{4,6},{5,7},{6,4},{7,5},{8,10},{9,11},{10,... | collective-permute-start | bytes 638984 | tf_op jit(solution)/shard_map/ppermute | solution.py:985
  144.7 10.7 %collective-permute-start.12 = (f32[2,104,256]{2,1,0:T(8,128)}, f32[2,104,256]{2,1,0:T(8,128)S(1)}, u32[]{:S(2)}, u32[]{:S(2)}) collective-permute-start(f32[2,104,256]{2,1,0:T(8,128)} %get-tuple-element.191), channel_id=1, source_target_pairs={{0,3},{1,2},{2,1},{3,0},{4,7},{5,6},{6,5},{7,4},{8,11},{9,10},{10,... | collective-permute-start | bytes 638984 | tf_op jit(solution)/shard_map/ppermute | solution.py:985
  146.3 18.3 %collective-permute-start.16 = (f32[200,256]{1,0:T(8,128)S(1)}, f32[200,256]{1,0:T(8,128)}, u32[]{:S(2)}, u32[]{:S(2)}) collective-permute-start(f32[200,256]{1,0:T(8,128)S(1)} %add_add_fusion), channel_id=1, source_target_pairs={{0,8},{4,12},{8,0},{12,4},{16,24},{20,28},{24,16},{28,20},{1,9},{5... | collective-permute-start | bytes 614408 | tf_op jit(solution)/shard_map/ppermute | solution.py:985
  157.5 19.7 %collective-permute-start.13 = (f32[344,256]{1,0:T(8,128)}, f32[344,256]{1,0:T(8,128)S(1)}, u32[]{:S(2)}, u32[]{:S(2)}) collective-permute-start(f32[344,256]{1,0:T(8,128)} %get-tuple-element.200), channel_id=1, source_target_pairs={{0,1},{1,0},{2,3},{3,2},{4,5},{5,4},{6,7},{7,6},{8,9},{9,8},{10,11... | collective-permute-start | bytes 1056776 | tf_op jit(solution)/shard_map/ppermute | solution.py:985
  158.7 19.3 %collective-permute-start.14 = (f32[344,256]{1,0:T(8,128)S(1)}, f32[344,256]{1,0:T(8,128)S(1)}, u32[]{:S(2)}, u32[]{:S(2)}) collective-permute-start(f32[344,256]{1,0:T(8,128)S(1)} %get-tuple-element.201), channel_id=1, source_target_pairs={{0,2},{1,3},{2,0},{3,1},{4,6},{5,7},{6,4},{7,5},{8,10},{9,11},{10,... | collective-permute-start | bytes 1056776 | tf_op jit(solution)/shard_map/ppermute | solution.py:985
  159.6 24.5 %copy-start = (f32[8,100,256]{2,0,1:T(8,128)S(1)}, f32[8,100,256]{2,0,1:T(8,128)}, u32[]{:S(2)}) copy-start(f32[8,100,256]{2,0,1:T(8,128)} %param.30) | copy-start | bytes 2457604
  159.7 24.5 %copy-start.3 = (f32[256,256]{1,0:T(8,128)S(1)}, f32[256,256]{1,0:T(8,128)}, u32[]{:S(2)}) copy-start(f32[256,256]{1,0:T(8,128)} %refs_6_.5) | copy-start | bytes 786436
  159.7 24.5 %copy-start.4 = (f32[8,104,256]{2,1,0:T(8,128)S(1)}, f32[8,104,256]{2,1,0:T(8,128)}, u32[]{:S(2)}) copy-start(f32[8,104,256]{2,1,0:T(8,128)} %get-tuple-element.219.refs_5_) | copy-start | bytes 2555908
  159.7 19.0 %collective-permute-start.15 = (f32[344,256]{1,0:T(8,128)S(1)}, f32[344,256]{1,0:T(8,128)S(1)}, u32[]{:S(2)}, u32[]{:S(2)}) collective-permute-start(f32[344,256]{1,0:T(8,128)S(1)} %get-tuple-element.202), channel_id=1, source_target_pairs={{0,3},{1,2},{2,1},{3,0},{4,7},{5,6},{6,5},{7,4},{8,11},{9,10},{10,... | collective-permute-start | bytes 1056776 | tf_op jit(solution)/shard_map/ppermute | solution.py:985
  161.0 16.2 %collective-permute-start.17 = (f32[200,256]{1,0:T(8,128)S(1)}, f32[200,256]{1,0:T(8,128)}, u32[]{:S(2)}, u32[]{:S(2)}) collective-permute-start(f32[200,256]{1,0:T(8,128)S(1)} %add_add_fusion), channel_id=1, source_target_pairs={{0,16},{4,20},{8,24},{12,28},{16,0},{20,4},{24,8},{28,12},{1,17},{... | collective-permute-start | bytes 614408 | tf_op jit(solution)/shard_map/ppermute | solution.py:985
  164.5 12.7 %collective-permute-start.18 = (f32[200,256]{1,0:T(8,128)S(1)}, f32[200,256]{1,0:T(8,128)}, u32[]{:S(2)}, u32[]{:S(2)}) collective-permute-start(f32[200,256]{1,0:T(8,128)S(1)} %add_add_fusion), channel_id=1, source_target_pairs={{0,24},{4,28},{8,16},{12,20},{16,8},{20,12},{24,0},{28,4},{1,25},{... | collective-permute-start | bytes 614408 | tf_op jit(solution)/shard_map/ppermute | solution.py:985
  180.7 23.9 %collective-permute-start.20 = (f32[400,256]{1,0:T(8,128)S(1)}, f32[400,256]{1,0:T(8,128)S(1)}, u32[]{:S(2)}, u32[]{:S(2)}) collective-permute-start(f32[400,256]{1,0:T(8,128)S(1)} %constant_dynamic-update-slice_fusion.2.refs_1_), channel_id=1, source_target_pairs={{0,2},{1,3},{2,0},{3,1},{4,6},{5,7},{6,4},{7,5},{8,10},{9,11},{10,... | collective-permute-start | bytes 1228808 | tf_op jit(solution)/shard_map/ppermute | solution.py:985
  182.3 22.3 %collective-permute-start.22 = (f32[400,256]{1,0:T(8,128)S(1)}, f32[400,256]{1,0:T(8,128)S(1)}, u32[]{:S(2)}, u32[]{:S(2)}) collective-permute-start(f32[400,256]{1,0:T(8,128)S(1)} %constant_dynamic-update-slice_fusion.2.refs_1_), channel_id=1, source_target_pairs={{0,4},{4,0},{8,12},{12,8},{16,20},{20,16},{24,28},{28,24},{1,5},{5... | collective-permute-start | bytes 1228808 | tf_op jit(solution)/shard_map/ppermute | solution.py:985
  183.3 21.4 %collective-permute-start.19 = (f32[400,256]{1,0:T(8,128)S(1)}, f32[400,256]{1,0:T(8,128)S(1)}, u32[]{:S(2)}, u32[]{:S(2)}) collective-permute-start(f32[400,256]{1,0:T(8,128)S(1)} %constant_dynamic-update-slice_fusion.refs_0_), channel_id=1, source_target_pairs={{0,1},{1,0},{2,3},{3,2},{4,5},{5,4},{6,7},{7,6},{8,9},{9,8},{10,11... | collective-permute-start | bytes 1228808 | tf_op jit(solution)/shard_map/ppermute | solution.py:985
  183.9 20.8 %collective-permute-start.21 = (f32[400,256]{1,0:T(8,128)S(1)}, f32[400,256]{1,0:T(8,128)}, u32[]{:S(2)}, u32[]{:S(2)}) collective-permute-start(f32[400,256]{1,0:T(8,128)S(1)} %constant_dynamic-update-slice_fusion.refs_0_), channel_id=1, source_target_pairs={{0,4},{4,0},{8,12},{12,8},{16,20},{20,16},{24,28},{28,24},{1,5},{5... | collective-permute-start | bytes 1228808 | tf_op jit(solution)/shard_map/ppermute | solution.py:985
  190.2 1.3 collective-permute-start.23
  191.5 32.2 %collective-permute-start.24 = (f32[400,256]{1,0:T(8,128)S(1)}, f32[400,256]{1,0:T(8,128)S(1)}, u32[]{:S(2)}, u32[]{:S(2)}) collective-permute-start(f32[400,256]{1,0:T(8,128)S(1)} %constant_dynamic-update-slice_fusion.2.refs_1_), channel_id=1, source_target_pairs={{0,1},{1,0},{2,3},{3,2},{4,5},{5,4},{6,7},{7,6},{8,9},{9,8},{10,11... | collective-permute-start | bytes 1228808 | tf_op jit(solution)/shard_map/ppermute | solution.py:985
  204.7 7.2 %collective-permute-start.34 = (f32[104,256]{1,0:T(8,128)S(1)}, f32[104,256]{1,0:T(8,128)S(1)}, u32[]{:S(2)}, u32[]{:S(2)}) collective-permute-start(f32[104,256]{1,0:T(8,128)S(1)} %add.48), channel_id=1, source_target_pairs={{0,8},{4,12},{8,0},{12,4},{16,24},{20,28},{24,16},{28,20},{1,9},{5... | collective-permute-start | bytes 319496 | tf_op jit(solution)/shard_map/ppermute | solution.py:985
  211.9 7.6 %collective-permute-start.35 = (f32[104,256]{1,0:T(8,128)S(1)}, f32[104,256]{1,0:T(8,128)S(1)}, u32[]{:S(2)}, u32[]{:S(2)}) collective-permute-start(f32[104,256]{1,0:T(8,128)S(1)} %add.49), channel_id=1, source_target_pairs={{0,16},{4,20},{8,24},{12,28},{16,0},{20,4},{24,8},{28,12},{1,17},{... | collective-permute-start | bytes 319496 | tf_op jit(solution)/shard_map/ppermute | solution.py:985
  219.5 5.6 %collective-permute-start.36 = (f32[104,256]{1,0:T(8,128)S(1)}, f32[104,256]{1,0:T(8,128)S(1)}, u32[]{:S(2)}, u32[]{:S(2)}) collective-permute-start(f32[104,256]{1,0:T(8,128)S(1)} %add.50), channel_id=1, source_target_pairs={{0,1},{1,0},{2,3},{3,2},{4,5},{5,4},{6,7},{7,6},{8,9},{9,8},{10,11... | collective-permute-start | bytes 319496 | tf_op jit(solution)/shard_map/ppermute | solution.py:985
  220.2 6.1 %collective-permute-start.37 = (f32[104,256]{1,0:T(8,128)S(1)}, f32[104,256]{1,0:T(8,128)S(1)}, u32[]{:S(2)}, u32[]{:S(2)}) collective-permute-start(f32[104,256]{1,0:T(8,128)S(1)} %add.50), channel_id=1, source_target_pairs={{0,2},{1,3},{2,0},{3,1},{4,6},{5,7},{6,4},{7,5},{8,10},{9,11},{10,... | collective-permute-start | bytes 319496 | tf_op jit(solution)/shard_map/ppermute | solution.py:985
  221.2 6.8 %collective-permute-start.38 = (f32[104,256]{1,0:T(8,128)S(1)}, f32[104,256]{1,0:T(8,128)S(1)}, u32[]{:S(2)}, u32[]{:S(2)}) collective-permute-start(f32[104,256]{1,0:T(8,128)S(1)} %add.50), channel_id=1, source_target_pairs={{0,3},{1,2},{2,1},{3,0},{4,7},{5,6},{6,5},{7,4},{8,11},{9,10},{10,... | collective-permute-start | bytes 319496 | tf_op jit(solution)/shard_map/ppermute | solution.py:985
  223.1 13.1 %collective-permute-start.25 = (f32[400,256]{1,0:T(8,128)S(1)}, f32[400,256]{1,0:T(8,128)S(1)}, u32[]{:S(2)}, u32[]{:S(2)}) collective-permute-start(f32[400,256]{1,0:T(8,128)S(1)} %constant_dynamic-update-slice_fusion.refs_0_), channel_id=1, source_target_pairs={{0,2},{1,3},{2,0},{3,1},{4,6},{5,7},{6,4},{7,5},{8,10},{9,11},{10,... | collective-permute-start | bytes 1228808 | tf_op jit(solution)/shard_map/ppermute | solution.py:985
  223.6 19.4 %collective-permute-start.26 = (f32[400,256]{1,0:T(8,128)S(1)}, f32[400,256]{1,0:T(8,128)S(1)}, u32[]{:S(2)}, u32[]{:S(2)}) collective-permute-start(f32[400,256]{1,0:T(8,128)S(1)} %collective-permute-done.19.refs_2_), channel_id=1, source_target_pairs={{0,2},{1,3},{2,0},{3,1},{4,6},{5,7},{6,4},{7,5},{8,10},{9,11},{10,... | collective-permute-start | bytes 1228808 | tf_op jit(solution)/shard_map/ppermute | solution.py:985
  225.1 18.0 %collective-permute-start.27 = (f32[400,256]{1,0:T(8,128)S(1)}, f32[400,256]{1,0:T(8,128)S(1)}, u32[]{:S(2)}, u32[]{:S(2)}) collective-permute-start(f32[400,256]{1,0:T(8,128)S(1)} %collective-permute-done.20.refs_5_), channel_id=1, source_target_pairs={{0,1},{1,0},{2,3},{3,2},{4,5},{5,4},{6,7},{7,6},{8,9},{9,8},{10,11... | collective-permute-start | bytes 1228808 | tf_op jit(solution)/shard_map/ppermute | solution.py:985
  226.3 17.3 %collective-permute-start.28 = (f32[400,256]{1,0:T(8,128)S(1)}, f32[400,256]{1,0:T(8,128)S(1)}, u32[]{:S(2)}, u32[]{:S(2)}) collective-permute-start(f32[400,256]{1,0:T(8,128)S(1)} %collective-permute-done.19.refs_2_), channel_id=1, source_target_pairs={{0,4},{4,0},{8,12},{12,8},{16,20},{20,16},{24,28},{28,24},{1,5},{5... | collective-permute-start | bytes 1228808 | tf_op jit(solution)/shard_map/ppermute | solution.py:985
  228.0 15.7 %collective-permute-start.31 = (f32[400,256]{1,0:T(8,128)S(1)}, f32[400,256]{1,0:T(8,128)S(1)}, u32[]{:S(2)}, u32[]{:S(2)}) collective-permute-start(f32[400,256]{1,0:T(8,128)S(1)} %collective-permute-done.20.refs_5_), channel_id=1, source_target_pairs={{0,4},{4,0},{8,12},{12,8},{16,20},{20,16},{24,28},{28,24},{1,5},{5... | collective-permute-start | bytes 1228808 | tf_op jit(solution)/shard_map/ppermute | solution.py:985
  236.2 9.3 %collective-permute-start.39 = (f32[416,256]{1,0:T(8,128)S(1)}, f32[416,256]{1,0:T(8,128)S(1)}, u32[]{:S(2)}, u32[]{:S(2)}) collective-permute-start(f32[416,256]{1,0:T(8,128)S(1)} %pad_maximum_fusion.refs_16_), channel_id=1, source_target_pairs={{0,4},{4,0},{8,12},{12,8},{16,20},{20,16},{24,28},{28,24},{1,5},{5... | collective-permute-start | bytes 1277960 | tf_op jit(solution)/shard_map/ppermute | solution.py:985
  243.1 1.7 collective-permute-start.29
  243.1 2.3 collective-permute-start.30
  243.6 2.4 collective-permute-start.32
  243.7 2.9 %collective-permute-start.33 = (f32[400,256]{1,0:T(8,128)S(1)}, f32[400,256]{1,0:T(8,128)S(1)}, u32[]{:S(2)}, u32[]{:S(2)}) collective-permute-start(f32[400,256]{1,0:T(8,128)S(1)} %collective-permute-done.27.refs_7_), channel_id=1, source_target_pairs={{0,4},{4,0},{8,12},{12,8},{16,20},{20,16},{24,28},{28,24},{1,5},{5... | collective-permute-start | bytes 1228808 | tf_op jit(solution)/shard_map/ppermute | solution.py:985
  (27 other events, 61.3 us)
where the time goes:
time: 253 us; the launch traced here: 252 us
  Pallas kernels  144 us (57%)
  starting transfers between devices  42.5 us (17%)
  waiting for transfers between devices  42.2 us (17%)
  local copies, waits for them, and re-layouts  21 us (8%)
    ppermute x40, starting transfers between devices, swap(): return lax.ppermute(x, axis, [(d, d ^ key) for d in range(n)])  42.5 us
    ppermute x40, waiting for transfers between devices, swap(): return lax.ppermute(x, axis, [(d, d ^ key) for d in range(n)])  42.2 us
    pallas_call x1, Pallas kernels, chain(): pl.pallas_call(functools.partial(chain_kernel, pieces), grid_spec=pltpu.P...  37.6 us
    pallas_call x2, Pallas kernels, attend(): pl.pallas_call(functools.partial(attend_kernel, keys, n, masks is not Non...  33 us
    pallas_call x3, Pallas kernels, mask_out(): pl.pallas_call(kernel, grid=(last - first,), in_specs=[whole(emb), whole(...  31.7 us
    pallas_call x2, Pallas kernels, attend_back(): pl.pallas_call(kernel, grid_spec=pltpu.PrefetchScalarGridSpec(num_scalar_...  30.8 us
    unnamed x72, local copies, waits for them, and re-layouts  19 us
  transfers between devices with their start and end apart: 40, of which 14 were waited for; matrix products, arithmetic and copies ran while one was open for 0% of the time, Pallas kernels for 30%

commit v1 on v0

--- a/solution.py
+++ b/solution.py
@@ -112,18 +112,10 @@
     return jnp.transpose(jnp.concatenate([x, fill], 0))[:, 0:x.shape[0]].astype(LOW)
 
 
-def attend_kernel(keys, n, with_mask, me_ref, *refs):
-    q_ref, f_ref, bits_ref, flag_ref, wq_ref, bq_ref, wkv_ref, vb_ref, elo_ref, ehi_ref = refs[:10]
-    refs = refs[10:]
-    if with_mask:
-        mc_ref, mf_ref, mf_own_ref = refs[:3]
-        refs = refs[3:]
-    e_ref, kv_ref, cq_ref = refs[:3]
-    pays, refs = refs[3:3 + len(keys)], refs[3 + len(keys):]
-    if with_mask:
-        es_ref, refs = refs[0], refs[1:]
-        mc_scr, refs = refs[0], refs[1:]
-    q_scr, w_scr, all_scr, wq_scr, wkv_scr, vb_scr, pay_ref = refs
+def attend_kernel(keys, n, me_ref, q_ref, f_ref, bits_ref, flag_ref, wq_ref, bq_ref, wkv_ref, vb_ref, elo_ref, ehi_ref,
+                  mc_ref, mf_ref, e_ref, kv_ref, cq_ref, *refs):
+    pays = refs[:len(keys)]
+    mc_scr, q_scr, w_scr, all_scr, wq_scr, wkv_scr, vb_scr, pay_ref = refs[len(keys):]
     i = pl.program_id(0)
     images = flag_ref.shape[0]
     image = (me_ref[0] ^ of_step(keys, n, i)) * n + i % n
@@ -144,19 +136,10 @@
         wkv_scr[width:] = jnp.transpose(wkv_ref[:, width:]).astype(LOW)
         vb_scr[...] = jnp.transpose(jnp.broadcast_to(vb_ref[...], (128, width)))
         pay_ref[...] = jnp.zeros_like(pay_ref)
-        if with_mask:
-            es_ref[...] = jnp.zeros_like(es_ref)
-            slabs_in(mc_scr, mc_ref[...].astype(F32).reshape(mc_ref.shape[0] * images, mc_ref.shape[2]))
-
-    if with_mask:
-        matched = mc_ref.shape[0]
-        pay_ref[tall:tall + matched] = nn(take_image(mc_scr, image, matched, images).astype(LOW), mf_ref[0])
-
-        @pl.when(i < n)
-        def _():
-            own = take_image(mc_scr, me_ref[0] * n + i % n, matched, images).astype(LOW)
-            es_ref[i % n, 0:matched] = nn(own, mf_own_ref[0])
-
+        slabs_in(mc_scr, mc_ref[...].astype(F32).reshape(mc_ref.shape[0] * images, mc_ref.shape[2]))
+
+    matched = mc_ref.shape[0]
+    pay_ref[tall:tall + matched] = nn(take_image(mc_scr, image, matched, images).astype(LOW), mf_ref[0])
     q_scr[0:count] = take_image(all_scr, image, count, images)
     w_scr[:, 0:count] = jnp.where(flag_ref[pl.ds(image, 1), :] > 0, 65535, bits_ref[0])
 
@@ -205,11 +188,11 @@
     for j, out in enumerate(pays):
         @pl.when(i // n == j)
         def _(out=out):
-            out[0] = pay_ref[0:out.shape[1]]
-
-
-def attend(keys, me, queries, features, bits, reopen_flags, query_weight, query_bias, keyval_weight, value_bias, parts,
-           masks=None):
+            out[0] = pay_ref[...]
+
+
+def attend(keys, me, queries, features, bits, reopen_flags, query_weight, query_bias, keyval_weight, value_bias,
+           mask_cotan, mask_features, parts):
     images, pixels, width = features.shape
     words, count = bits.shape[1:]
     rows = up(count, 8)
@@ -229,41 +212,34 @@
         return pl.BlockSpec((1,) + shape, lambda i, me: (jnp.clip(i - j * n, 0, n - 1),) + (0,) * len(shape))
 
     per = lambda *shape: pl.BlockSpec((1,) + shape, lambda i, me: (i,) + (0,) * len(shape))
-    args = (queries, features, bits, reopen_flags, query_weight, query_bias[None], keyval_weight, value_bias[None], e_lo, e_hi)
+    args = (queries, features, bits, reopen_flags, query_weight, query_bias[None], keyval_weight, value_bias[None], e_lo, e_hi,
+            mask_cotan, mask_features)
+    matched, _, wide = mask_cotan.shape
     in_specs = [whole(a) for a in args]
     in_specs[1] = theirs(pixels, width)
     in_specs[2] = theirs(words, count)
+    in_specs[11] = theirs(wide, width)
     flops = 2 * steps * (pixels * width * 2 * width + 2 * HEADS * rows * pixels * width)
     nbytes = steps * (pixels * width * 6 + HEADS * rows * pixels * 2)
-    tall = rows + HEADS
+    tall = rows + HEADS + up(matched, 8)
+    nbytes += steps * wide * (width + matched) * 2
     out_shape = [
         jax.ShapeDtypeStruct((steps, HEADS, rows, pixels), LOW),
         jax.ShapeDtypeStruct((steps, 2 * width, pixels), LOW),
         jax.ShapeDtypeStruct((steps, rows, width), F32),
     ]
-    scratch = []
-    if masks is not None:
-        matched, _, wide = masks[0].shape
-        args += masks + masks[1:]
-        in_specs += [whole(masks[0]), theirs(wide, width),
-                     pl.BlockSpec((1, wide, width), lambda i, me: (me[0] * n + jnp.minimum(i, n - 1), 0, 0))]
-        nbytes += steps * wide * (width + matched) * 2
-        scratch = [slabs(matched * images, wide)]
-        tall += up(matched, 8)
     out_shape += [jax.ShapeDtypeStruct((n, tall, width), F32)] * len(keys)
     out_specs = [per(HEADS, rows, pixels), per(2 * width, pixels), per(rows, width)]
     out_specs += [of_key(j, tall, width) for j in range(len(keys))]
-    if masks is not None:
-        out_shape.append(jax.ShapeDtypeStruct((n, up(matched, 8), width), F32))
-        out_specs.append(whole(out_shape[-1]))
     return pl.pallas_call(
-        functools.partial(attend_kernel, keys, n, masks is not None),
+        functools.partial(attend_kernel, keys, n),
         grid_spec=pltpu.PrefetchScalarGridSpec(
             num_scalar_prefetch=1,
             grid=(steps,),
             in_specs=in_specs,
             out_specs=tuple(out_specs),
-            scratch_shapes=scratch + [
+            scratch_shapes=[
+                slabs(matched * images, wide),
                 pltpu.VMEM((rows, width), F32),
                 pltpu.VMEM((words, rows), jnp.int32),
                 slabs(count * images, width),
@@ -281,7 +257,7 @@
 
 
 def combine_kernel(rows, *refs):
-    parts, es_ref, out_ref = refs[:-2], refs[-2], refs[-1]
+    parts, out_ref = refs[:-1], refs[-1]
     images, full, width = out_ref.shape
     tall = rows + HEADS
     onehot = head_onehot(width, HEADS)
@@ -294,24 +270,22 @@
         acc = jnp.zeros((rows, width), F32)
         for p, r in zip(parts, rs):
             acc = acc + p[i, 0:rows] * tn(r / total, onehot, HIGH)[0:rows]
-        es = es_ref[i]
-        for p in parts[1:]:
-            es = es + p[i, tall:]
+        es = functools.reduce(jnp.add, [p[i, tall:] for p in parts])
         out_ref[i, 0:rows] = acc
         out_ref[i, rows:tall, 0:128] = top
         out_ref[i, rows:tall, 128:256] = total
         out_ref[i, tall:] = es
 
 
-def combine(parts, es, rows):
-    shape = parts[1].shape
+def combine(parts, rows):
+    shape = parts[0].shape
     return pl.pallas_call(
         functools.partial(combine_kernel, rows),
         out_shape=jax.ShapeDtypeStruct(shape, F32),
-        compiler_params=pltpu.CompilerParams(vmem_limit_bytes=16 * MIB),
+        compiler_params=pltpu.CompilerParams(vmem_limit_bytes=32 * MIB),
         cost_estimate=cost(1e6, 5 * 4 * math.prod(shape)),
         name="combine",
-    )(*parts, es)
+    )(*parts)
 
 
 def lower_kernel(*refs):
@@ -326,7 +300,7 @@
     return pl.pallas_call(
         lower_kernel,
         out_shape=out_shape,
-        compiler_params=pltpu.CompilerParams(vmem_limit_bytes=24 * MIB),
+        compiler_params=pltpu.CompilerParams(vmem_limit_bytes=60 * MIB),
         cost_estimate=cost(size, 6 * size),
         name="lower",
     )(*weights)
@@ -893,27 +867,27 @@
                             pltpu.VMEM((full, width), F32)],
         ),
         out_shape=out_shape,
-        compiler_params=params(24),
+        compiler_params=params(60),
         cost_estimate=cost(5e8, 8e6),
         name="query_back",
     )(me, *args)
 
 
 def unpack_kernel(split, me_ref, *refs):
-    own, other = refs[:8], refs[8:16]
+    own, other = refs[:5], refs[5:10]
     (tail, tail2,
      query_ref, query_bias_ref, keyval_ref, value_bias_ref, cross_ref, cross_bias_ref, gain_ref, nbias_ref,
      self_ref, self_bias_ref, selfout_ref, selfout_bias_ref, hidden_ref, hidden_bias_ref, hidout_ref, hidout_bias_ref,
-     embed_ref, embed_bias_ref, g, t) = refs[16:]
-    pix, core, z = me_ref[1], me_ref[2], me_ref[3]
+     embed_ref, embed_bias_ref, g, t) = refs[10:]
+    pix, core = me_ref[1], me_ref[2]
     width = query_ref.shape[0]
-    short = own[0].shape[0] // 2
-    for half, eight in ((core, own), (1 - core, other)):
-        for k in range(4):
-            for j in range(4):
-                at = ((pix ^ k) * 2 + half) * 4 + (z ^ j)
-                piece = eight[2 * k + j // 2]
-                g[pl.ds(pl.multiple_of(at * short, 8), short)] = piece[j % 2 * short:(j % 2 + 1) * short]
+    short = own[1].shape[0]
+    places = (((0, 0), (0, 1)), ((1, 0),), ((2, 1),), ((2, 0), (3, 0)), ((1, 1), (3, 1)))
+    for half, five in ((core, own), (1 - core, other)):
+        for piece, spots in zip(five, places):
+            for row, (k, second) in enumerate(spots):
+                at = ((pix ^ k) * 2 + half) * 2 + second
+                g[pl.ds(pl.multiple_of(at * short, 8), short)] = piece[row * short:(row + 1) * short]
     small = tail.shape[0] // 4
     for half, ref in ((core, tail), (1 - core, tail2)):
         for k in range(4):
@@ -1032,20 +1006,12 @@
     chip = lax.axis_index("batch") // 2
     me = jnp.stack([pix if direct else 0 * pix, pix, core, chip]).astype(jnp.int32)
 
-    def forward(keys, flags, masks=None):
-        return attend(keys, me, queries, features, bits, flags, query_weight, query_bias, keyval_weight, value_bias,
-                      PARTS, masks)
-
-    far, near = (3, 1, 2), (0,)
-    *kept, pay3, pay1, pay2, es = forward(far, reopen_flags, (mask_cotan, mask_features))
-    pay3, pay1, pay2, reopen_flags = beside(pay3, pay1, pay2, reopen_flags)
-    pays = {3: pay3, 1: pay1, 2: pay2}
-    got = {k: swap(pays[k], "pix", n_pix, k) for k in far} if direct else {}
-    *kept_near, pays[0] = forward(near, reopen_flags)
-    if direct:
-        pays[0], *arrived = beside(pays[0], *[got[k] for k in far])
-        got.update(zip(far, arrived))
-        got[0] = pays[0]
+    order = (3, 1, 2, 0)
+    e, kv, cq, *pays = attend(order, me, queries, features, bits, reopen_flags, query_weight, query_bias, keyval_weight,
+                              value_bias, mask_cotan, mask_features, PARTS)
+    kept = (e, kv, cq)
+    pays = dict(zip(order, pays))
+    got = {k: swap(pays[k], "pix", n_pix, k) if k else pays[k] for k in order} if direct else {}
     pays = [pays[k] for k in range(PARTS)]
     weights = (
         cross_out, cross_out_bias[None], norm_gain, norm_bias, self_weight, self_bias, self_out, self_out_bias[None],
@@ -1053,12 +1019,12 @@
     )
     large = (0, 4, 6, 8, 10, 12)
     if direct:
-        share = combine([got[k] for k in range(PARTS)], es, rows)
+        share = combine([got[k] for k in range(PARTS)], rows)
         share, *raw = beside(share, *[weights[k] for k in large])
         att = gather_in(share, "pix", n_pix)
     else:
         raw = [weights[k] for k in large]
-        pay = jnp.concatenate([jnp.concatenate([pays[0], es], 1)] + pays[1:], 0)
+        pay = jnp.concatenate(pays, 0)
         top = lax.pmax(pay[:, rows:tall, :128], "pix")
         ratio = jnp.exp(pay[:, rows:tall, :128] - top)
 
@@ -1080,54 +1046,61 @@
     mask = functools.partial(mask_out, emb, matched_queries, mask_cotan, mask_features, count, blocks)
 
     def backward(keys, old, last=False):
-        offset = 0 if keys[0] in near else far.index(keys[0]) * images // PARTS
-        return attend_back(keys, me, kept_near if keys[0] in near else kept, offset, features, dn, dt, keyval_weight, old, last)
+        offset = order.index(keys[0]) * images // PARTS
+        return attend_back(keys, me, kept, offset, features, dn, dt, keyval_weight, old, last)
 
     def z_scatter(chunks):
-        got = [lax.dynamic_index_in_dim(chunks, chip ^ k, 0, keepdims=False) for k in range(4)]
+        got = [lax.dynamic_index_in_dim(chunks, (chip ^ k) % 2 * 2 + (chip ^ k) // 2, 0, keepdims=False) for k in range(4)]
         return [got[0]] + [swap(got[k], "batch", n_batch, 2 * k) for k in (1, 2, 3)]
 
     other = swap(away, "batch", n_batch, 1)
     if direct:
-        fg, acc, vb, qp0 = backward(near, None)
-        other, fg, acc, vb, qp0 = beside(other, fg, acc, vb, qp0)
+        fg, acc, vb, qp3 = backward((3,), None)
+        other, fg, acc, vb, qp3 = beside(other, fg, acc, vb, qp3)
         sums = z_scatter((mine + other).reshape(n_batch // 2, -1, width))
-        feat_grad, g_kv, qp3, qp1, qp2 = backward(far, (fg, acc, vb), True)
-        *sums, feat_grad, g_kv, qp1, qp2, qp3 = beside(*sums, feat_grad, g_kv, qp1, qp2, qp3)
-        qp1, qp2, qp3 = [swap(q, "pix", n_pix, k) for k, q in zip((1, 2, 3), (qp1, qp2, qp3))]
+        qp3 = swap(qp3, "pix", n_pix, 3)
+        feat_grad, g_kv, qp1, qp2, qp0 = backward((1, 2, 0), (fg, acc, vb), True)
+        *sums, feat_grad, g_kv, qp0, qp1, qp2, qp3 = beside(*sums, feat_grad, g_kv, qp0, qp1, qp2, qp3)
+        qp1, qp2 = swap(qp1, "pix", n_pix, 1), swap(qp2, "pix", n_pix, 2)
         own = functools.reduce(jnp.add, sums)
-        same = [own] + [swap(own, "batch", n_batch, k) for k in (2, 4, 6)]
+        other = swap(own, "batch", n_batch, 4)
         cuts = [blocks * k // 8 for k in (0, 2, 5, 8)]
         outs = mask((cuts[0], cuts[1]))
-        qp1, qp2, qp3, outs = beside(qp1, qp2, qp3, outs)
+        qp1, qp2, other, outs = beside(qp1, qp2, other, outs)
+        own = join(own, other, "batch", 4)
+        other = swap(own, "batch", n_batch, 2)
         split = g_kv.shape[0] // n_pix
-        parts = query_sum(me, (qp0, qp1, qp2, qp3), g_kv)
+        *parts, outs = beside(*query_sum(me, (qp0, qp1, qp2, qp3), g_kv), outs)
         parts = tuple(p if k == 0 else swap(p, "pix", n_pix, k) for k, p in enumerate(parts))
         outs = mask((cuts[1], cuts[2]), outs)
-        parts, outs, *same = beside(parts, outs, *same)
-        low, high = jnp.concatenate(same[:2], 0), jnp.concatenate(same[2:], 0)
+        *parts, other, outs = beside(*parts, other, outs)
+        own = join(own, other, "batch", 2)
+        low, high = own[:own.shape[0] // 2], own[own.shape[0] // 2:]
         low1, high2 = swap(low, "pix", n_pix, 1), swap(high, "pix", n_pix, 2)
-        low0, high0 = swap(low, "batch", n_batch, 1), swap(high, "batch", n_batch, 1)
+        own2 = swap(own, "batch", n_batch, 1)
         queries_grad, tail, tail2 = query_back(me, parts, queries, dp1, query_weight)
-        tail2 = swap(tail2, "batch", n_batch, 1)
+        tail = tail + swap(tail2, "batch", n_batch, 1)
+        tail2 = swap(tail, "batch", n_batch, 2)
+        low1, high2, own2, tail2, outs = beside(low1, high2, own2, tail2, outs)
+        low3, high3 = jnp.concatenate([low, low1], 0), jnp.concatenate([high, high2], 0)
+        low3, high3 = swap(low3, "pix", n_pix, 2), swap(high3, "pix", n_pix, 1)
+        low12, high22 = swap(low1, "batch", n_batch, 1), swap(high2, "batch", n_batch, 1)
+        tail = tail + tail2
+        tail2 = swap(tail, "batch", n_batch, 4)
         outs = mask((cuts[2], cuts[3]), outs)
-        low1, high2, low0, high0, tail2, outs = beside(low1, high2, low0, high0, tail2, outs)
+        low12, high22, tail2, outs = beside(low12, high22, tail2, outs)
+        low3, high3, outs = beside(low3, high3, outs)
         tail = tail + tail2
-        tail2 = swap(tail, "batch", n_batch, 2)
-        low2, high1 = swap(low, "pix", n_pix, 2), swap(high, "pix", n_pix, 1)
-        low3, high3 = swap(low1, "pix", n_pix, 2), swap(high2, "pix", n_pix, 1)
-        tail = tail + tail2
-        tail = tail + swap(tail, "batch", n_batch, 4)
         tail = jnp.concatenate([tail] + [swap(tail, "pix", n_pix, k) for k in (1, 2, 3)], 0)
-        pieces = [low, high, low1, high1, low2, high2, low3, high3]
-        pieces += [low0, high0] + [swap(p, "batch", n_batch, 1) for p in pieces[2:]]
+        pieces = [own, low1, high2, low3, high3]
+        pieces += [own2, low12, high22, swap(low3, "batch", n_batch, 1), swap(high3, "batch", n_batch, 1)]
         tails = (tail, swap(tail, "batch", n_batch, 1))
         grads = unpack(me, pieces, tails, split, width, hidden)
         (d_query, d_query_bias, d_keyval, d_value_bias, d_cross, d_cross_bias, d_gain, d_nbias, d_self, d_self_bias,
          d_selfout, d_selfout_bias, d_hidden, d_hidden_bias, d_hidout, d_hidout_bias, d_embed, d_embed_bias) = grads
     else:
         old, parts = None, {}
-        for keys, last in ((near, False), (far, True)):
+        for keys, last in (((3,), False), ((1, 2, 0), True)):
             back = backward(keys, old, last)
             count_sums = 1 if last else 2
             old = back[:1 + count_sums]

time: 253 us -> 231 us (0.913)
  local copies, waits for them, and re-layouts: 21 us -> 3.34 us
  starting transfers between devices: 42.5 us -> 36.2 us
  other arithmetic: 0.84 us -> 5.41 us
    unnamed x72 -> x28, local copies, waits for them, and re-layouts: 19 us -> 3.26 us
    ppermute x40 -> x34, starting transfers between devices: 42.5 us -> 36.2 us  [swap(): return lax.ppermute(x, axis, [(d, d ^ key) for d in range(n)])]
    pallas_call x2 -> x1, Pallas kernels: 33 us -> 27.6 us  [attend(): pl.pallas_call(functools.partial(attend_kernel, keys, n), grid_spec=pltpu...]
    pallas_call x1, Pallas kernels: 0.31 us -> 4.47 us  [lower(): pl.pallas_call(lower_kernel, out_shape=out_shape, compiler_params=pltpu.C...]
    ppermute x40 -> x34, waiting for transfers between devices: 42.2 us -> 40.9 us  [swap(): return lax.ppermute(x, axis, [(d, d ^ key) for d in range(n)])]
  transfers between devices with their start and end apart: 40 -> 34, of which waited for: 14 -> 14; matrix products, arithmetic and copies ran while one was open for 0% -> 2% of each run, Pallas kernels for 30% -> 31%
where the time goes in v1:
time: 231 us; the launch traced here: 230 us
  Pallas kernels  143 us (62%)
  waiting for transfers between devices  40.9 us (18%)
  starting transfers between devices  36.2 us (16%)
  other arithmetic  5.41 us (2%)
  local copies, waits for them, and re-layouts  3.34 us (1%)
    ppermute x34, waiting for transfers between devices, swap(): return lax.ppermute(x, axis, [(d, d ^ key) for d in range(n)])  40.9 us
    pallas_call x1, Pallas kernels, chain(): pl.pallas_call(functools.partial(chain_kernel, pieces), grid_spec=pltpu.P...  37.7 us
    ppermute x34, starting transfers between devices, swap(): return lax.ppermute(x, axis, [(d, d ^ key) for d in range(n)])  36.2 us
    pallas_call x3, Pallas kernels, mask_out(): pl.pallas_call(kernel, grid=(last - first,), in_specs=[whole(emb), whole(...  31.7 us
    pallas_call x2, Pallas kernels, attend_back(): pl.pallas_call(kernel, grid_spec=pltpu.PrefetchScalarGridSpec(num_scalar_...  30.9 us
    pallas_call x1, Pallas kernels, attend(): pl.pallas_call(functools.partial(attend_kernel, keys, n), grid_spec=pltpu...  27.6 us
    pallas_call x1, Pallas kernels, unpack(): pl.pallas_call(functools.partial(unpack_kernel, split), grid_spec=pltpu.P...  5.11 us
  transfers between devices with their start and end apart: 34, of which 14 were waited for; matrix products, arithmetic and copies ran while one was open for 2% of the time, Pallas kernels for 31%

profile of v1, /device:TPU:0, one launch (start us, length us, event | category | flops | bytes accessed | tf_op | source)
XLA Modules:
  0.0 230.4 jit_solution(5835346870895278585)
XLA Ops:
  1.3 27.6 %attend.1 = (bf16[8,8,104,1024]{3,2,1,0:T(8,128)(2,1)}, bf16[8,512,1024]{2,1,0:T(8,128)(2,1)}, f32[8,104,256]{2,1,0:T(8,128)}, f32[2,168,256]{2,1,0:T(8,128)}, f...) custom-call(s32[4]{0:T(128)} %pad_add_fusion.me_ref.refs_0_, f32[800,256]{1,0:T(8,128)} %bitcast.46, ...), custom_call_target="tpu_custom_call" | custom-call | flops 9126805504 | bytes 46268416 | tf_op jit(solution)/shard_map/attend/pallas_call | solution.py:234
  28.9 3.0 %collective-permute-start = (f32[2,168,256]{2,1,0:T(8,128)}, f32[2,168,256]{2,1,0:T(8,128)S(1)}, u32[]{:S(2)}, u32[]{:S(2)}) collective-permute-start(f32[2,168,256]{2,1,0:T(8,128)} %get-tuple-element.139.refs_5_), channel_id=1, source_target_pairs={{0,1},{1,0},{2,3},{3,2},{4,5},{5,4},{6,7},{7,6},{8,9},{9,8},{10,11... | collective-permute-start | bytes 1032200 | tf_op jit(solution)/shard_map/ppermute | solution.py:959
  31.9 1.6 collective-permute-start.1
  33.4 7.5 %collective-permute-done.refs_1_ = f32[2,168,256]{2,1,0:T(8,128)S(1)} collective-permute-done((f32[2,168,256]{2,1,0:T(8,128)}, f32[2,168,256]{2,1,0:T(8,128)S(1)}, u32[]{:S(2)}, u32[]{:S(2)}) %collective-permute-start) | collective-permute-done | bytes 344096 | tf_op jit(solution)/shard_map/ppermute | solution.py:959
  41.0 8.0 %collective-permute-done.1.refs_2_ = f32[2,168,256]{2,1,0:T(8,128)S(1)} collective-permute-done((f32[2,168,256]{2,1,0:T(8,128)}, f32[2,168,256]{2,1,0:T(8,128)S(1)}, u32[]{:S(2)}, u32[]{:S(2)}) %collective-permute-start.1) | collective-permute-done | bytes 344096 | tf_op jit(solution)/shard_map/ppermute | solution.py:959
  49.0 1.0 copy-done.2
  50.0 1.1 combine.1.refs_0_
  51.1 1.3 collective-permute-start.3
  53.2 1.4 collective-permute-start.5
  54.6 4.5 %lower.1 = (bf16[256,256]{1,0:T(8,128)(2,1)}, bf16[256,768]{1,0:T(8,128)(2,1)}, bf16[256,256]{1,0:T(8,128)(2,1)}, bf16[256,2048]{1,0:T(8,128)(2,1)}, bf16[2048,2...) custom-call(f32[256,256]{1,0:T(8,128)} %refs_0_, f32[256,768]{1,0:T(8,128)} %refs_1_, f32[256,256]{1,0:T(8,128)} %refs_2_, ...), custom_call_target="tpu_custom_call" | custom-call | flops 1572864 | bytes 9437184 | tf_op jit(solution)/shard_map/lower/pallas_call | solution.py:300
  59.1 3.0 %collective-permute-done.3.refs_1_ = f32[2,168,256]{2,1,0:T(8,128)S(1)} collective-permute-done((f32[2,168,256]{2,1,0:T(8,128)S(1)}, f32[2,168,256]{2,1,0:T(8,128)S(1)}, u32[]{:S(2)}, u32[]{:S(2)}) %collective-permute-start.3) | collective-permute-done | bytes 344096 | tf_op jit(solution)/shard_map/ppermute | solution.py:959
  62.1 6.3 %collective-permute-done.4.refs_2_ = f32[2,168,256]{2,1,0:T(8,128)S(1)} collective-permute-done((f32[2,168,256]{2,1,0:T(8,128)S(1)}, f32[2,168,256]{2,1,0:T(8,128)S(1)}, u32[]{:S(2)}, u32[]{:S(2)}) %collective-permute-start.4) | collective-permute-done | bytes 344096 | tf_op jit(solution)/shard_map/ppermute | solution.py:959
  69.3 37.7 %chain.1 = (f32[800,256]{1,0:T(8,128)}, f32[800,256]{1,0:T(8,128)}, f32[8,104,256]{2,1,0:T(8,128)}, f32[8,104,128]{2,1,0:T(8,128)}, f32[8,104,256]{2,1,0:T(8,128...) custom-call(s32[4]{0:T(128)} %pad_add_fusion.me_ref.refs_0_, f32[2,168,256]{2,1,0:T(8,128)} %copy-done.3, ...), custom_call_target="tpu_custom_call" | custom-call | flops 16000000000 | bytes 20000000 | tf_op jit(solution)/shard_map/chain/pallas_call | solution.py:560
  107.2 9.9 %attend_back.2 = (f32[8,1024,256]{2,1,0:T(8,128)}, f32[512,256]{1,0:T(8,128)}, f32[256,128]{1,0:T(8,128)}, f32[2,104,256]{2,1,0:T(8,128)}) custom-call(s32[4]{0:T(128)} %pad_add_fusion.me_ref.refs_0_, bf16[8,8,104,1024]{3,2,1,0:T(8,128)(2,1)} %get-tuple-element.158.refs_1_, bf16[8,512,1024]{2,1,0:T(8,128)(2,1)} %get-tuple-element.159.refs_2_, ...), custom_call_target="tpu_custom_call" | custom-call | flops 4563402752 | bytes 8650752 | tf_op jit(solution)/shard_map/attend_back/pallas_call | solution.py:773
  117.3 1.6 collective-permute-start.7
  118.9 2.6 %collective-permute-start.8 = (f32[200,256]{1,0:T(8,128)S(1)}, f32[200,256]{1,0:T(8,128)S(1)}, u32[]{:S(2)}, u32[]{:S(2)}) collective-permute-start(f32[200,256]{1,0:T(8,128)S(1)} %get-tuple-element.256), channel_id=1, source_target_pairs={{0,16},{4,20},{8,24},{12,28},{16,0},{20,4},{24,8},{28,12},{1,17},{... | collective-permute-start | bytes 614408 | tf_op jit(solution)/shard_map/ppermute | solution.py:959
  121.7 1.1 collective-permute-start.10
  122.8 21.0 %attend_back.3 = (f32[8,1024,256]{2,1,0:T(8,128)}, f32[544,256]{1,0:T(8,128)}, f32[2,104,256]{2,1,0:T(8,128)}, f32[2,104,256]{2,1,0:T(8,128)}, f32[2,104,256]{2,1,0:T(8,128)}) custom-call(s32[4]{0:T(128)} %pad_add_fusion.me_ref.refs_0_, bf16[8,8,104,1024]{3,2,1,0:T(8,128)(2,1)} %get-tuple-element.158.refs_1_, ...), custom_call_target="tpu_custom_call", output_to_operand_aliasing={{0}: (8, {})} | custom-call | flops 13690208256 | bytes 25952256 | tf_op jit(solution)/shard_map/attend_back/pallas_call | solution.py:773
  143.8 1.0 collective-permute-start.11
  144.8 1.5 collective-permute-start.12
  146.4 1.8 collective-permute-start.13
  148.1 8.4 %mask_out.3 = (f32[800,4096]{1,0:T(8,128)}, f32[8,4096,256]{2,1,0:T(8,128)}) custom-call(f32[800,256]{1,0:T(8,128)} %get-tuple-element.183.a.emb_ref, s32[8,50]{1,0:T(8,128)} %match_ref.3, bf16[50,8,4096]{2,1,0:T(8,128)(2,1)} %bitcast.42, bf16[8,4096,256]{2,1,0:T(8,128)(2,1)} %mf_ref.5), custom_call_target="tpu_custom_call" | custom-call | flops 671088640 | bytes 16678912 | tf_op jit(solution)/shard_map/mask_out/pallas_call | solution.py:640
  157.5 1.7 collective-permute-start.17
  161.1 1.0 collective-permute-start.15
  162.1 1.9 collective-permute-start.16
  164.0 11.7 %mask_out.4 = (f32[800,4096]{1,0:T(8,128)}, f32[8,4096,256]{2,1,0:T(8,128)}) custom-call(f32[800,256]{1,0:T(8,128)} %get-tuple-element.183.a.emb_ref, s32[8,50]{1,0:T(8,128)} %match_ref.3, bf16[50,8,4096]{2,1,0:T(8,128)(2,1)} %bitcast.43, bf16[8,4096,256]{2,1,0:T(8,128)(2,1)} %mf_ref.5, ...), custom_call_target="tpu_custom_call", output_to_operand_aliasing={{0}: (4, {}), {1}: (5, {})} | custom-call | flops 1006632960 | bytes 25018368 | tf_op jit(solution)/shard_map/mask_out/pallas_call | solution.py:640
  177.5 1.5 collective-permute-start.18
  179.5 4.2 %query_back.1 = (f32[800,256]{1,0:T(8,128)}, f32[104,256]{1,0:T(8,128)}, f32[104,256]{1,0:T(8,128)}) custom-call(s32[4]{0:T(128)} %pad_add_fusion.me_ref.refs_0_, f32[344,256]{1,0:T(8,128)} %copy-done.1, f32[344,256]{1,0:T(8,128)} %copy-done.8, f32[344,256]{1,0:T(8,128)} %copy-done.9, f32[344,256]{1,0:T(8,128)} %copy-done.10, f32[800,256]{1,0:T(8,128)} %bitcast.48, ...), custom_call_target="tpu_custom_call" | custom-call | flops 500000000 | bytes 8000000 | tf_op jit(solution)/shard_map/query_back/pallas_call | solution.py:858
  183.7 1.5 collective-permute-done.21
  185.2 0.9 add.90
  186.1 1.2 collective-permute-start.22
  187.3 3.9 %collective-permute-done.22 = f32[104,256]{1,0:T(8,128)S(1)} collective-permute-done((f32[104,256]{1,0:T(8,128)S(1)}, f32[104,256]{1,0:T(8,128)S(1)}, u32[]{:S(2)}, u32[]{:S(2)}) %collective-permute-start.22) | collective-permute-done | bytes 106528 | tf_op jit(solution)/shard_map/ppermute | solution.py:959
  191.2 0.9 pad_maximum_fusion.2
  192.2 1.0 collective-permute-start.24
  193.2 0.9 pad_maximum_fusion.1
  194.1 1.1 collective-permute-start.23
  196.4 3.1 %collective-permute-start.27 = (f32[104,256]{1,0:T(8,128)}, f32[104,256]{1,0:T(8,128)}, u32[]{:S(2)}, u32[]{:S(2)}) collective-permute-start(f32[104,256]{1,0:T(8,128)} %add.91), channel_id=1, source_target_pairs={{0,16},{4,20},{8,24},{12,28},{16,0},{20,4},{24,8},{28,12},{1,17},{... | collective-permute-start | bytes 319496 | tf_op jit(solution)/shard_map/ppermute | solution.py:959
  199.5 11.7 %mask_out.5 = (f32[800,4096]{1,0:T(8,128)}, f32[8,4096,256]{2,1,0:T(8,128)}) custom-call(f32[800,256]{1,0:T(8,128)} %get-tuple-element.183.a.emb_ref, s32[8,50]{1,0:T(8,128)} %match_ref.3, bf16[50,8,4096]{2,1,0:T(8,128)(2,1)} %bitcast.44, bf16[8,4096,256]{2,1,0:T(8,128)(2,1)} %mf_ref.5, ...), custom_call_target="tpu_custom_call", output_to_operand_aliasing={{0}: (4, {}), {1}: (5, {})} | custom-call | flops 1006632960 | bytes 25018368 | tf_op jit(solution)/shard_map/mask_out/pallas_call | solution.py:640
  211.8 1.7 collective-permute-done.23.refs_3_
  214.0 1.0 add.92
  215.0 1.1 collective-permute-start.30
  216.1 1.5 collective-permute-start.31
  217.6 1.0 collective-permute-start.32
  218.6 1.8 collective-permute-done.30
  220.3 1.7 collective-permute-done.31
  222.0 1.2 collective-permute-done.32
  223.3 1.8 collective-permute-done.33.refs_11_
  225.1 5.1 %unpack.1 = (f32[256,256]{1,0:T(8,128)}, f32[1,256]{1,0:T(1,128)}, f32[256,512]{1,0:T(8,128)}, f32[1,256]{1,0:T(1,128)}, f32[256,256]{1,0:T(8,128)}, /*index=5*/...) custom-call(s32[4]{0:T(128)S(1)} %copy-done.6, ...), custom_call_target="tpu_custom_call" | custom-call | flops 1000000 | bytes 16000000 | tf_op jit(solution)/shard_map/unpack/pallas_call | solution.py:938
  (74 shorter events, 10.5 us)
Async XLA Ops:
  28.9 12.1 %collective-permute-start = (f32[2,168,256]{2,1,0:T(8,128)}, f32[2,168,256]{2,1,0:T(8,128)S(1)}, u32[]{:S(2)}, u32[]{:S(2)}) collective-permute-start(f32[2,168,256]{2,1,0:T(8,128)} %get-tuple-element.139.refs_5_), channel_id=1, source_target_pairs={{0,1},{1,0},{2,3},{3,2},{4,5},{5,4},{6,7},{7,6},{8,9},{9,8},{10,11... | collective-permute-start | bytes 1032200 | tf_op jit(solution)/shard_map/ppermute | solution.py:959
  31.9 17.1 %collective-permute-start.1 = (f32[2,168,256]{2,1,0:T(8,128)}, f32[2,168,256]{2,1,0:T(8,128)S(1)}, u32[]{:S(2)}, u32[]{:S(2)}) collective-permute-start(f32[2,168,256]{2,1,0:T(8,128)} %get-tuple-element.140.refs_6_), channel_id=1, source_target_pairs={{0,2},{1,3},{2,0},{3,1},{4,6},{5,7},{6,4},{7,5},{8,10},{9,11},{10,... | collective-permute-start | bytes 1032200 | tf_op jit(solution)/shard_map/ppermute | solution.py:959
  33.4 15.5 %collective-permute-start.2 = (f32[2,168,256]{2,1,0:T(8,128)}, f32[2,168,256]{2,1,0:T(8,128)S(1)}, u32[]{:S(2)}, u32[]{:S(2)}) collective-permute-start(f32[2,168,256]{2,1,0:T(8,128)} %get-tuple-element.141.refs_7_), channel_id=1, source_target_pairs={{0,3},{1,2},{2,1},{3,0},{4,7},{5,6},{6,5},{7,4},{8,11},{9,10},{10,... | collective-permute-start | bytes 1032200 | tf_op jit(solution)/shard_map/ppermute | solution.py:959
  49.0 1.0 copy-start.2
  51.0 17.4 %copy-start.3 = (f32[2,168,256]{2,1,0:T(8,128)}, f32[2,168,256]{2,1,0:T(8,128)S(1)}, u32[]{:S(2)}) copy-start(f32[2,168,256]{2,1,0:T(8,128)S(1)} %combine.1.refs_0_) | copy-start | bytes 1032196
  51.1 11.1 %collective-permute-start.3 = (f32[2,168,256]{2,1,0:T(8,128)S(1)}, f32[2,168,256]{2,1,0:T(8,128)S(1)}, u32[]{:S(2)}, u32[]{:S(2)}) collective-permute-start(f32[2,168,256]{2,1,0:T(8,128)S(1)} %combine.1.refs_0_), channel_id=1, source_target_pairs={{0,1},{1,0},{2,3},{3,2},{4,5},{5,4},{6,7},{7,6},{8,9},{9,8},{10,11... | collective-permute-start | bytes 1032200 | tf_op jit(solution)/shard_map/ppermute | solution.py:959
  52.4 16.0 %collective-permute-start.4 = (f32[2,168,256]{2,1,0:T(8,128)S(1)}, f32[2,168,256]{2,1,0:T(8,128)S(1)}, u32[]{:S(2)}, u32[]{:S(2)}) collective-permute-start(f32[2,168,256]{2,1,0:T(8,128)S(1)} %combine.1.refs_0_), channel_id=1, source_target_pairs={{0,2},{1,3},{2,0},{3,1},{4,6},{5,7},{6,4},{7,5},{8,10},{9,11},{10,... | collective-permute-start | bytes 1032200 | tf_op jit(solution)/shard_map/ppermute | solution.py:959
  53.2 15.2 %collective-permute-start.5 = (f32[2,168,256]{2,1,0:T(8,128)S(1)}, f32[2,168,256]{2,1,0:T(8,128)S(1)}, u32[]{:S(2)}, u32[]{:S(2)}) collective-permute-start(f32[2,168,256]{2,1,0:T(8,128)S(1)} %combine.1.refs_0_), channel_id=1, source_target_pairs={{0,3},{1,2},{2,1},{3,0},{4,7},{5,6},{6,5},{7,4},{8,11},{9,10},{10,... | collective-permute-start | bytes 1032200 | tf_op jit(solution)/shard_map/ppermute | solution.py:959
  62.1 6.3 %copy-start.11 = (f32[2,168,256]{2,1,0:T(8,128)}, f32[2,168,256]{2,1,0:T(8,128)S(1)}, u32[]{:S(2)}) copy-start(f32[2,168,256]{2,1,0:T(8,128)S(1)} %collective-permute-done.3.refs_1_) | copy-start | bytes 1032196
  68.4 0.7 copy-start.12
  68.4 0.8 copy-start.13
  106.9 10.1 %collective-permute-start.6 = (f32[800,256]{1,0:T(8,128)}, f32[800,256]{1,0:T(8,128)S(1)}, u32[]{:S(2)}, u32[]{:S(2)}) collective-permute-start(f32[800,256]{1,0:T(8,128)} %get-tuple-element.157), channel_id=1, source_target_pairs={{0,4},{4,0},{8,12},{12,8},{16,20},{20,16},{24,28},{28,24},{1,5},{5... | collective-permute-start | bytes 2457608 | tf_op jit(solution)/shard_map/ppermute | solution.py:959
  107.1 9.9 %copy-start.7 = (f32[800,256]{1,0:T(8,128)S(1)}, f32[800,256]{1,0:T(8,128)}, u32[]{:S(2)}) copy-start(f32[800,256]{1,0:T(8,128)} %get-tuple-element.156) | copy-start | bytes 2457604
  117.3 26.5 %collective-permute-start.7 = (f32[200,256]{1,0:T(8,128)S(1)}, f32[200,256]{1,0:T(8,128)S(1)}, u32[]{:S(2)}, u32[]{:S(2)}) collective-permute-start(f32[200,256]{1,0:T(8,128)S(1)} %get-tuple-element.257), channel_id=1, source_target_pairs={{0,8},{4,12},{8,0},{12,4},{16,24},{20,28},{24,16},{28,20},{1,9},{5... | collective-permute-start | bytes 614408 | tf_op jit(solution)/shard_map/ppermute | solution.py:959
  118.9 24.8 %collective-permute-start.8 = (f32[200,256]{1,0:T(8,128)S(1)}, f32[200,256]{1,0:T(8,128)S(1)}, u32[]{:S(2)}, u32[]{:S(2)}) collective-permute-start(f32[200,256]{1,0:T(8,128)S(1)} %get-tuple-element.256), channel_id=1, source_target_pairs={{0,16},{4,20},{8,24},{12,28},{16,0},{20,4},{24,8},{28,12},{1,17},{... | collective-permute-start | bytes 614408 | tf_op jit(solution)/shard_map/ppermute | solution.py:959
  121.5 22.3 %collective-permute-start.9 = (f32[200,256]{1,0:T(8,128)S(1)}, f32[200,256]{1,0:T(8,128)S(1)}, u32[]{:S(2)}, u32[]{:S(2)}) collective-permute-start(f32[200,256]{1,0:T(8,128)S(1)} %get-tuple-element.255), channel_id=1, source_target_pairs={{0,24},{4,28},{8,16},{12,20},{16,8},{20,12},{24,0},{28,4},{1,25},{... | collective-permute-start | bytes 614408 | tf_op jit(solution)/shard_map/ppermute | solution.py:959
  121.7 22.0 %collective-permute-start.10 = (f32[2,104,256]{2,1,0:T(8,128)}, f32[2,104,256]{2,1,0:T(8,128)S(1)}, u32[]{:S(2)}, u32[]{:S(2)}) collective-permute-start(f32[2,104,256]{2,1,0:T(8,128)} %get-tuple-element.176), channel_id=1, source_target_pairs={{0,3},{1,2},{2,1},{3,0},{4,7},{5,6},{6,5},{7,4},{8,11},{9,10},{10,... | collective-permute-start | bytes 638984 | tf_op jit(solution)/shard_map/ppermute | solution.py:959
  143.8 13.6 %collective-permute-start.11 = (f32[2,104,256]{2,1,0:T(8,128)}, f32[2,104,256]{2,1,0:T(8,128)S(1)}, u32[]{:S(2)}, u32[]{:S(2)}) collective-permute-start(f32[2,104,256]{2,1,0:T(8,128)} %get-tuple-element.181), channel_id=1, source_target_pairs={{0,1},{1,0},{2,3},{3,2},{4,5},{5,4},{6,7},{7,6},{8,9},{9,8},{10,11... | collective-permute-start | bytes 638984 | tf_op jit(solution)/shard_map/ppermute | solution.py:959
  144.8 12.6 %collective-permute-start.12 = (f32[2,104,256]{2,1,0:T(8,128)}, f32[2,104,256]{2,1,0:T(8,128)S(1)}, u32[]{:S(2)}, u32[]{:S(2)}) collective-permute-start(f32[2,104,256]{2,1,0:T(8,128)} %get-tuple-element.182), channel_id=1, source_target_pairs={{0,2},{1,3},{2,0},{3,1},{4,6},{5,7},{6,4},{7,5},{8,10},{9,11},{10,... | collective-permute-start | bytes 638984 | tf_op jit(solution)/shard_map/ppermute | solution.py:959
  146.4 11.0 %collective-permute-start.13 = (f32[200,256]{1,0:T(8,128)S(1)}, f32[200,256]{1,0:T(8,128)S(1)}, u32[]{:S(2)}, u32[]{:S(2)}) collective-permute-start(f32[200,256]{1,0:T(8,128)S(1)} %add_add_fusion), channel_id=1, source_target_pairs={{0,16},{4,20},{8,24},{12,28},{16,0},{20,4},{24,8},{28,12},{1,17},{... | collective-permute-start | bytes 614408 | tf_op jit(solution)/shard_map/ppermute | solution.py:959
  148.1 11.0 %copy-start = (f32[544,256]{1,0:T(8,128)S(1)}, f32[544,256]{1,0:T(8,128)}, u32[]{:S(2)}) copy-start(f32[544,256]{1,0:T(8,128)} %get-tuple-element.191.refs_4_) | copy-start | bytes 1671172
  148.1 11.0 %copy-start.4 = (f32[2,104,256]{2,1,0:T(8,128)S(1)}, f32[2,104,256]{2,1,0:T(8,128)}, u32[]{:S(2)}) copy-start(f32[2,104,256]{2,1,0:T(8,128)} %get-tuple-element.187.refs_0_) | copy-start | bytes 638980
  148.1 11.0 %copy-start.5 = (s32[4]{0:T(128)S(1)}, s32[4]{0:T(128)}, u32[]{:S(2)}) copy-start(s32[4]{0:T(128)} %pad_add_fusion.me_ref.refs_0_) | copy-start | bytes 52
  157.5 19.1 %collective-permute-start.17 = (f32[400,256]{1,0:T(8,128)S(1)}, f32[400,256]{1,0:T(8,128)S(1)}, u32[]{:S(2)}, u32[]{:S(2)}) collective-permute-start(f32[400,256]{1,0:T(8,128)S(1)} %pad_maximum_fusion.4), channel_id=1, source_target_pairs={{0,8},{4,12},{8,0},{12,4},{16,24},{20,28},{24,16},{28,20},{1,9},{5... | collective-permute-start | bytes 1228808 | tf_op jit(solution)/shard_map/ppermute | solution.py:959
  159.8 0.7 copy-start.1
  160.5 15.1 %collective-permute-start.14 = (f32[344,256]{1,0:T(8,128)S(1)}, f32[344,256]{1,0:T(8,128)S(1)}, u32[]{:S(2)}, u32[]{:S(2)}) collective-permute-start(f32[344,256]{1,0:T(8,128)S(1)} %get-tuple-element.199), channel_id=1, source_target_pairs={{0,1},{1,0},{2,3},{3,2},{4,5},{5,4},{6,7},{7,6},{8,9},{9,8},{10,11... | collective-permute-start | bytes 1056776 | tf_op jit(solution)/shard_map/ppermute | solution.py:959
  161.1 15.5 %collective-permute-start.15 = (f32[344,256]{1,0:T(8,128)S(1)}, f32[344,256]{1,0:T(8,128)S(1)}, u32[]{:S(2)}, u32[]{:S(2)}) collective-permute-start(f32[344,256]{1,0:T(8,128)S(1)} %get-tuple-element.200), channel_id=1, source_target_pairs={{0,2},{1,3},{2,0},{3,1},{4,6},{5,7},{6,4},{7,5},{8,10},{9,11},{10,... | collective-permute-start | bytes 1056776 | tf_op jit(solution)/shard_map/ppermute | solution.py:959
  162.1 14.5 %collective-permute-start.16 = (f32[344,256]{1,0:T(8,128)S(1)}, f32[344,256]{1,0:T(8,128)S(1)}, u32[]{:S(2)}, u32[]{:S(2)}) collective-permute-start(f32[344,256]{1,0:T(8,128)S(1)} %get-tuple-element.201), channel_id=1, source_target_pairs={{0,3},{1,2},{2,1},{3,0},{4,7},{5,6},{6,5},{7,4},{8,11},{9,10},{10,... | collective-permute-start | bytes 1056776 | tf_op jit(solution)/shard_map/ppermute | solution.py:959
  175.7 0.9 copy-start.8
  176.6 0.7 copy-start.9
  176.6 0.8 copy-start.10
  177.4 13.8 %collective-permute-start.20 = (f32[800,256]{1,0:T(8,128)S(1)}, f32[800,256]{1,0:T(8,128)S(1)}, u32[]{:S(2)}, u32[]{:S(2)}) collective-permute-start(f32[800,256]{1,0:T(8,128)S(1)} %pad_maximum_fusion.refs_0_), channel_id=1, source_target_pairs={{0,4},{4,0},{8,12},{12,8},{16,20},{20,16},{24,28},{28,24},{1,5},{5... | collective-permute-start | bytes 2457608 | tf_op jit(solution)/shard_map/ppermute | solution.py:959
  177.5 13.7 %collective-permute-start.18 = (f32[400,256]{1,0:T(8,128)S(1)}, f32[400,256]{1,0:T(8,128)S(1)}, u32[]{:S(2)}, u32[]{:S(2)}) collective-permute-start(f32[400,256]{1,0:T(8,128)S(1)} %get-tuple-element.254), channel_id=1, source_target_pairs={{0,1},{1,0},{2,3},{3,2},{4,5},{5,4},{6,7},{7,6},{8,9},{9,8},{10,11... | collective-permute-start | bytes 1228808 | tf_op jit(solution)/shard_map/ppermute | solution.py:959
  179.0 12.2 %collective-permute-start.19 = (f32[400,256]{1,0:T(8,128)S(1)}, f32[400,256]{1,0:T(8,128)S(1)}, u32[]{:S(2)}, u32[]{:S(2)}) collective-permute-start(f32[400,256]{1,0:T(8,128)S(1)} %get-tuple-element.253), channel_id=1, source_target_pairs={{0,2},{1,3},{2,0},{3,1},{4,6},{5,7},{6,4},{7,5},{8,10},{9,11},{10,... | collective-permute-start | bytes 1228808 | tf_op jit(solution)/shard_map/ppermute | solution.py:959
  183.7 1.5 collective-permute-start.21
  186.1 5.1 %collective-permute-start.22 = (f32[104,256]{1,0:T(8,128)S(1)}, f32[104,256]{1,0:T(8,128)S(1)}, u32[]{:S(2)}, u32[]{:S(2)}) collective-permute-start(f32[104,256]{1,0:T(8,128)S(1)} %add.90), channel_id=1, source_target_pairs={{0,8},{4,12},{8,0},{12,4},{16,24},{20,28},{24,16},{28,20},{1,9},{5... | collective-permute-start | bytes 319496 | tf_op jit(solution)/shard_map/ppermute | solution.py:959
  192.2 19.7 %collective-permute-start.24 = (f32[800,256]{1,0:T(8,128)}, f32[800,256]{1,0:T(8,128)S(1)}, u32[]{:S(2)}, u32[]{:S(2)}) collective-permute-start(f32[800,256]{1,0:T(8,128)} %pad_maximum_fusion.2), channel_id=1, source_target_pairs={{0,1},{1,0},{2,3},{3,2},{4,5},{5,4},{6,7},{7,6},{8,9},{9,8},{10,11... | collective-permute-start | bytes 2457608 | tf_op jit(solution)/shard_map/ppermute | solution.py:959
  194.1 19.4 %collective-permute-start.23 = (f32[800,256]{1,0:T(8,128)}, f32[800,256]{1,0:T(8,128)S(1)}, u32[]{:S(2)}, u32[]{:S(2)}) collective-permute-start(f32[800,256]{1,0:T(8,128)} %pad_maximum_fusion.1), channel_id=1, source_target_pairs={{0,2},{1,3},{2,0},{3,1},{4,6},{5,7},{6,4},{7,5},{8,10},{9,11},{10,... | collective-permute-start | bytes 2457608 | tf_op jit(solution)/shard_map/ppermute | solution.py:959
  195.2 15.9 %collective-permute-start.25 = (f32[400,256]{1,0:T(8,128)S(1)}, f32[400,256]{1,0:T(8,128)}, u32[]{:S(2)}, u32[]{:S(2)}) collective-permute-start(f32[400,256]{1,0:T(8,128)S(1)} %collective-permute-done.18.refs_1_), channel_id=1, source_target_pairs={{0,4},{4,0},{8,12},{12,8},{16,20},{20,16},{24,28},{28,24},{1,5},{5... | collective-permute-start | bytes 1228808 | tf_op jit(solution)/shard_map/ppermute | solution.py:959
  195.2 15.9 %collective-permute-start.26 = (f32[400,256]{1,0:T(8,128)S(1)}, f32[400,256]{1,0:T(8,128)}, u32[]{:S(2)}, u32[]{:S(2)}) collective-permute-start(f32[400,256]{1,0:T(8,128)S(1)} %collective-permute-done.19.refs_2_), channel_id=1, source_target_pairs={{0,4},{4,0},{8,12},{12,8},{16,20},{20,16},{24,28},{28,24},{1,5},{5... | collective-permute-start | bytes 1228808 | tf_op jit(solution)/shard_map/ppermute | solution.py:959
  196.4 28.7 %copy-start.6 = (s32[4]{0:T(128)S(1)}, s32[4]{0:T(128)}, u32[]{:S(2)}) copy-start(s32[4]{0:T(128)} %pad_add_fusion.me_ref.refs_0_) | copy-start | bytes 52
  196.4 14.8 %collective-permute-start.27 = (f32[104,256]{1,0:T(8,128)}, f32[104,256]{1,0:T(8,128)}, u32[]{:S(2)}, u32[]{:S(2)}) collective-permute-start(f32[104,256]{1,0:T(8,128)} %add.91), channel_id=1, source_target_pairs={{0,16},{4,20},{8,24},{12,28},{16,0},{20,4},{24,8},{28,12},{1,17},{... | collective-permute-start | bytes 319496 | tf_op jit(solution)/shard_map/ppermute | solution.py:959
  213.5 11.5 %collective-permute-start.28 = (f32[800,256]{1,0:T(8,128)S(1)}, f32[800,256]{1,0:T(8,128)S(1)}, u32[]{:S(2)}, u32[]{:S(2)}) collective-permute-start(f32[800,256]{1,0:T(8,128)S(1)} %collective-permute-done.23.refs_3_), channel_id=1, source_target_pairs={{0,4},{4,0},{8,12},{12,8},{16,20},{20,16},{24,28},{28,24},{1,5},{5... | collective-permute-start | bytes 2457608 | tf_op jit(solution)/shard_map/ppermute | solution.py:959
  213.5 11.5 %collective-permute-start.29 = (f32[800,256]{1,0:T(8,128)S(1)}, f32[800,256]{1,0:T(8,128)S(1)}, u32[]{:S(2)}, u32[]{:S(2)}) collective-permute-start(f32[800,256]{1,0:T(8,128)S(1)} %collective-permute-done.24.refs_4_), channel_id=1, source_target_pairs={{0,4},{4,0},{8,12},{12,8},{16,20},{20,16},{24,28},{28,24},{1,5},{5... | collective-permute-start | bytes 2457608 | tf_op jit(solution)/shard_map/ppermute | solution.py:959
  215.0 5.3 %collective-permute-start.30 = (f32[104,256]{1,0:T(8,128)S(1)}, f32[104,256]{1,0:T(8,128)S(1)}, u32[]{:S(2)}, u32[]{:S(2)}) collective-permute-start(f32[104,256]{1,0:T(8,128)S(1)} %add.92), channel_id=1, source_target_pairs={{0,1},{1,0},{2,3},{3,2},{4,5},{5,4},{6,7},{7,6},{8,9},{9,8},{10,11... | collective-permute-start | bytes 319496 | tf_op jit(solution)/shard_map/ppermute | solution.py:959
  216.1 6.0 %collective-permute-start.31 = (f32[104,256]{1,0:T(8,128)S(1)}, f32[104,256]{1,0:T(8,128)S(1)}, u32[]{:S(2)}, u32[]{:S(2)}) collective-permute-start(f32[104,256]{1,0:T(8,128)S(1)} %add.92), channel_id=1, source_target_pairs={{0,2},{1,3},{2,0},{3,1},{4,6},{5,7},{6,4},{7,5},{8,10},{9,11},{10,... | collective-permute-start | bytes 319496 | tf_op jit(solution)/shard_map/ppermute | solution.py:959
  217.6 5.6 %collective-permute-start.32 = (f32[104,256]{1,0:T(8,128)S(1)}, f32[104,256]{1,0:T(8,128)S(1)}, u32[]{:S(2)}, u32[]{:S(2)}) collective-permute-start(f32[104,256]{1,0:T(8,128)S(1)} %add.92), channel_id=1, source_target_pairs={{0,3},{1,2},{2,1},{3,0},{4,7},{5,6},{6,5},{7,4},{8,11},{9,10},{10,... | collective-permute-start | bytes 319496 | tf_op jit(solution)/shard_map/ppermute | solution.py:959
  223.2 1.8 collective-permute-start.33

commit v2 on v1

--- a/solution.py
+++ b/solution.py
@@ -1064,7 +1064,7 @@
         qp1, qp2 = swap(qp1, "pix", n_pix, 1), swap(qp2, "pix", n_pix, 2)
         own = functools.reduce(jnp.add, sums)
         other = swap(own, "batch", n_batch, 4)
-        cuts = [blocks * k // 8 for k in (0, 2, 5, 8)]
+        cuts = [blocks * k // 8 for k in (0, 2, 5, 6, 8)]
         outs = mask((cuts[0], cuts[1]))
         qp1, qp2, other, outs = beside(qp1, qp2, other, outs)
         own = join(own, other, "batch", 4)
@@ -1080,14 +1080,16 @@
         own2 = swap(own, "batch", n_batch, 1)
         queries_grad, tail, tail2 = query_back(me, parts, queries, dp1, query_weight)
         tail = tail + swap(tail2, "batch", n_batch, 1)
-        tail2 = swap(tail, "batch", n_batch, 2)
-        low1, high2, own2, tail2, outs = beside(low1, high2, own2, tail2, outs)
+        low1, high2, own2, tail, outs = beside(low1, high2, own2, tail, outs)
         low3, high3 = jnp.concatenate([low, low1], 0), jnp.concatenate([high, high2], 0)
         low3, high3 = swap(low3, "pix", n_pix, 2), swap(high3, "pix", n_pix, 1)
         low12, high22 = swap(low1, "batch", n_batch, 1), swap(high2, "batch", n_batch, 1)
+        tail2 = swap(tail, "batch", n_batch, 2)
+        outs = mask((cuts[2], cuts[3]), outs)
+        tail2, outs = beside(tail2, outs)
         tail = tail + tail2
         tail2 = swap(tail, "batch", n_batch, 4)
-        outs = mask((cuts[2], cuts[3]), outs)
+        outs = mask((cuts[3], cuts[4]), outs)
         low12, high22, tail2, outs = beside(low12, high22, tail2, outs)
         low3, high3, outs = beside(low3, high3, outs)
         tail = tail + tail2

time: 231 us -> 233 us (level)
  Pallas kernels: 143 us -> 146 us
  waiting for transfers between devices: 40.9 us -> 38.4 us
    pallas_call x3 -> x4, Pallas kernels: 31.7 us -> 34.7 us  [mask_out(): pl.pallas_call(kernel, grid=(last - first,), in_specs=[whole(emb), whole(...]
    ppermute x34, waiting for transfers between devices: 40.9 us -> 38.4 us  [swap(): return lax.ppermute(x, axis, [(d, d ^ key) for d in range(n)])]
  transfers between devices with their start and end apart: 34 -> 34, of which waited for: 14 -> 13; matrix products, arithmetic and copies ran while one was open for 2% -> 2% of each run, Pallas kernels for 31% -> 32%
where the time goes in v2:
time: 233 us; the launch traced here: 232 us
  Pallas kernels  146 us (63%)
  waiting for transfers between devices  38.4 us (16%)
  starting transfers between devices  34.9 us (15%)
  other arithmetic  7.72 us (3%)
  local copies, waits for them, and re-layouts  3.42 us (1%)
    ppermute x34, waiting for transfers between devices, swap(): return lax.ppermute(x, axis, [(d, d ^ key) for d in range(n)])  38.4 us
    pallas_call x1, Pallas kernels, chain(): pl.pallas_call(functools.partial(chain_kernel, pieces), grid_spec=pltpu.P...  37.7 us
    ppermute x34, starting transfers between devices, swap(): return lax.ppermute(x, axis, [(d, d ^ key) for d in range(n)])  34.9 us
    pallas_call x4, Pallas kernels, mask_out(): pl.pallas_call(kernel, grid=(last - first,), in_specs=[whole(emb), whole(...  34.7 us
    pallas_call x2, Pallas kernels, attend_back(): pl.pallas_call(kernel, grid_spec=pltpu.PrefetchScalarGridSpec(num_scalar_...  30.8 us
    pallas_call x1, Pallas kernels, attend(): pl.pallas_call(functools.partial(attend_kernel, keys, n), grid_spec=pltpu...  27.6 us
    pallas_call x1, Pallas kernels, unpack(): pl.pallas_call(functools.partial(unpack_kernel, split), grid_spec=pltpu.P...  5.11 us
  transfers between devices with their start and end apart: 34, of which 13 were waited for; matrix products, arithmetic and copies ran while one was open for 2% of the time, Pallas kernels for 32%

profile of v2, /device:TPU:0, one launch (start us, length us, event | category | flops | bytes accessed | tf_op | source)
XLA Modules:
  0.0 232.0 jit_solution(12480878476694461849)
XLA Ops:
  1.3 27.6 %attend.1 = (bf16[8,8,104,1024]{3,2,1,0:T(8,128)(2,1)}, bf16[8,512,1024]{2,1,0:T(8,128)(2,1)}, f32[8,104,256]{2,1,0:T(8,128)}, f32[2,168,256]{2,1,0:T(8,128)}, f...) custom-call(s32[4]{0:T(128)} %pad_add_fusion.me_ref.refs_0_, f32[800,256]{1,0:T(8,128)} %bitcast.47, ...), custom_call_target="tpu_custom_call" | custom-call | flops 9126805504 | bytes 46268416 | tf_op jit(solution)/shard_map/attend/pallas_call | solution.py:234
  28.9 3.0 %collective-permute-start = (f32[2,168,256]{2,1,0:T(8,128)}, f32[2,168,256]{2,1,0:T(8,128)S(1)}, u32[]{:S(2)}, u32[]{:S(2)}) collective-permute-start(f32[2,168,256]{2,1,0:T(8,128)} %get-tuple-element.144.refs_5_), channel_id=1, source_target_pairs={{0,1},{1,0},{2,3},{3,2},{4,5},{5,4},{6,7},{7,6},{8,9},{9,8},{10,11... | collective-permute-start | bytes 1032200 | tf_op jit(solution)/shard_map/ppermute | solution.py:959
  31.9 1.6 collective-permute-start.1
  33.5 7.5 %collective-permute-done.refs_1_ = f32[2,168,256]{2,1,0:T(8,128)S(1)} collective-permute-done((f32[2,168,256]{2,1,0:T(8,128)}, f32[2,168,256]{2,1,0:T(8,128)S(1)}, u32[]{:S(2)}, u32[]{:S(2)}) %collective-permute-start) | collective-permute-done | bytes 344096 | tf_op jit(solution)/shard_map/ppermute | solution.py:959
  41.0 8.0 %collective-permute-done.1.refs_2_ = f32[2,168,256]{2,1,0:T(8,128)S(1)} collective-permute-done((f32[2,168,256]{2,1,0:T(8,128)}, f32[2,168,256]{2,1,0:T(8,128)S(1)}, u32[]{:S(2)}, u32[]{:S(2)}) %collective-permute-start.1) | collective-permute-done | bytes 344096 | tf_op jit(solution)/shard_map/ppermute | solution.py:959
  49.0 1.0 copy-done.2
  50.0 1.1 combine.1.refs_0_
  51.1 1.3 collective-permute-start.3
  53.2 1.4 collective-permute-start.5
  54.6 4.5 %lower.1 = (bf16[256,256]{1,0:T(8,128)(2,1)}, bf16[256,768]{1,0:T(8,128)(2,1)}, bf16[256,256]{1,0:T(8,128)(2,1)}, bf16[256,2048]{1,0:T(8,128)(2,1)}, bf16[2048,2...) custom-call(f32[256,256]{1,0:T(8,128)} %refs_0_, f32[256,768]{1,0:T(8,128)} %refs_1_, f32[256,256]{1,0:T(8,128)} %refs_2_, ...), custom_call_target="tpu_custom_call" | custom-call | flops 1572864 | bytes 9437184 | tf_op jit(solution)/shard_map/lower/pallas_call | solution.py:300
  59.1 3.0 %collective-permute-done.3.refs_1_ = f32[2,168,256]{2,1,0:T(8,128)S(1)} collective-permute-done((f32[2,168,256]{2,1,0:T(8,128)S(1)}, f32[2,168,256]{2,1,0:T(8,128)S(1)}, u32[]{:S(2)}, u32[]{:S(2)}) %collective-permute-start.3) | collective-permute-done | bytes 344096 | tf_op jit(solution)/shard_map/ppermute | solution.py:959
  62.1 6.3 %collective-permute-done.4.refs_2_ = f32[2,168,256]{2,1,0:T(8,128)S(1)} collective-permute-done((f32[2,168,256]{2,1,0:T(8,128)S(1)}, f32[2,168,256]{2,1,0:T(8,128)S(1)}, u32[]{:S(2)}, u32[]{:S(2)}) %collective-permute-start.4) | collective-permute-done | bytes 344096 | tf_op jit(solution)/shard_map/ppermute | solution.py:959
  69.3 37.7 %chain.1 = (f32[800,256]{1,0:T(8,128)}, f32[800,256]{1,0:T(8,128)}, f32[8,104,256]{2,1,0:T(8,128)}, f32[8,104,128]{2,1,0:T(8,128)}, f32[8,104,256]{2,1,0:T(8,128...) custom-call(s32[4]{0:T(128)} %pad_add_fusion.me_ref.refs_0_, f32[2,168,256]{2,1,0:T(8,128)} %copy-done.3, ...), custom_call_target="tpu_custom_call" | custom-call | flops 16000000000 | bytes 20000000 | tf_op jit(solution)/shard_map/chain/pallas_call | solution.py:560
  107.2 9.9 %attend_back.2 = (f32[8,1024,256]{2,1,0:T(8,128)}, f32[512,256]{1,0:T(8,128)}, f32[256,128]{1,0:T(8,128)}, f32[2,104,256]{2,1,0:T(8,128)}) custom-call(s32[4]{0:T(128)} %pad_add_fusion.me_ref.refs_0_, bf16[8,8,104,1024]{3,2,1,0:T(8,128)(2,1)} %get-tuple-element.163.refs_1_, bf16[8,512,1024]{2,1,0:T(8,128)(2,1)} %get-tuple-element.164.refs_2_, ...), custom_call_target="tpu_custom_call" | custom-call | flops 4563402752 | bytes 8650752 | tf_op jit(solution)/shard_map/attend_back/pallas_call | solution.py:773
  117.3 1.6 collective-permute-start.7
  118.9 2.6 %collective-permute-start.8 = (f32[200,256]{1,0:T(8,128)S(1)}, f32[200,256]{1,0:T(8,128)S(1)}, u32[]{:S(2)}, u32[]{:S(2)}) collective-permute-start(f32[200,256]{1,0:T(8,128)S(1)} %get-tuple-element.266), channel_id=1, source_target_pairs={{0,16},{4,20},{8,24},{12,28},{16,0},{20,4},{24,8},{28,12},{1,17},{... | collective-permute-start | bytes 614408 | tf_op jit(solution)/shard_map/ppermute | solution.py:959
  121.7 1.1 collective-permute-start.10
  122.8 20.9 %attend_back.3 = (f32[8,1024,256]{2,1,0:T(8,128)}, f32[544,256]{1,0:T(8,128)}, f32[2,104,256]{2,1,0:T(8,128)}, f32[2,104,256]{2,1,0:T(8,128)}, f32[2,104,256]{2,1,0:T(8,128)}) custom-call(s32[4]{0:T(128)} %pad_add_fusion.me_ref.refs_0_, bf16[8,8,104,1024]{3,2,1,0:T(8,128)(2,1)} %get-tuple-element.163.refs_1_, ...), custom_call_target="tpu_custom_call", output_to_operand_aliasing={{0}: (8, {})} | custom-call | flops 13690208256 | bytes 25952256 | tf_op jit(solution)/shard_map/attend_back/pallas_call | solution.py:773
  143.8 1.0 collective-permute-start.11
  144.8 1.5 collective-permute-start.12
  146.4 1.8 collective-permute-start.13
  148.2 8.3 %mask_out.4 = (f32[800,4096]{1,0:T(8,128)}, f32[8,4096,256]{2,1,0:T(8,128)}) custom-call(f32[800,256]{1,0:T(8,128)} %get-tuple-element.188.a.emb_ref, s32[8,50]{1,0:T(8,128)} %match_ref.5, bf16[50,8,4096]{2,1,0:T(8,128)(2,1)} %bitcast.42, bf16[8,4096,256]{2,1,0:T(8,128)(2,1)} %mf_ref.7), custom_call_target="tpu_custom_call" | custom-call | flops 671088640 | bytes 16678912 | tf_op jit(solution)/shard_map/mask_out/pallas_call | solution.py:640
  156.5 1.0 collective-permute-done.13
  158.3 1.5 collective-permute-start.17
  161.8 1.0 collective-permute-start.15
  162.8 1.9 collective-permute-start.16
  164.6 11.7 %mask_out.5 = (f32[800,4096]{1,0:T(8,128)}, f32[8,4096,256]{2,1,0:T(8,128)}) custom-call(f32[800,256]{1,0:T(8,128)} %get-tuple-element.188.a.emb_ref, s32[8,50]{1,0:T(8,128)} %match_ref.5, bf16[50,8,4096]{2,1,0:T(8,128)(2,1)} %bitcast.43, bf16[8,4096,256]{2,1,0:T(8,128)(2,1)} %mf_ref.7, ...), custom_call_target="tpu_custom_call", output_to_operand_aliasing={{0}: (4, {}), {1}: (5, {})} | custom-call | flops 1006632960 | bytes 25018368 | tf_op jit(solution)/shard_map/mask_out/pallas_call | solution.py:640
  178.2 1.5 collective-permute-start.18
  180.3 4.2 %query_back.1 = (f32[800,256]{1,0:T(8,128)}, f32[104,256]{1,0:T(8,128)}, f32[104,256]{1,0:T(8,128)}) custom-call(s32[4]{0:T(128)} %pad_add_fusion.me_ref.refs_0_, f32[344,256]{1,0:T(8,128)} %copy-done.1, f32[344,256]{1,0:T(8,128)} %copy-done.8, f32[344,256]{1,0:T(8,128)} %copy-done.9, f32[344,256]{1,0:T(8,128)} %copy-done.10, f32[800,256]{1,0:T(8,128)} %bitcast.49, ...), custom_call_target="tpu_custom_call" | custom-call | flops 500000000 | bytes 8000000 | tf_op jit(solution)/shard_map/query_back/pallas_call | solution.py:858
  184.5 1.5 collective-permute-done.21
  186.0 1.6 add.90
  187.6 2.6 %collective-permute-done.18.refs_1_ = f32[400,256]{1,0:T(8,128)S(1)} collective-permute-done((f32[400,256]{1,0:T(8,128)S(1)}, f32[400,256]{1,0:T(8,128)S(1)}, u32[]{:S(2)}, u32[]{:S(2)}) %collective-permute-start.18) | collective-permute-done | bytes 409632 | tf_op jit(solution)/shard_map/ppermute | solution.py:959
  190.1 1.1 collective-permute-done.19.refs_2_
  193.8 1.0 collective-permute-start.22
  195.3 1.2 collective-permute-start.26
  196.5 6.4 %mask_out.6 = (f32[800,4096]{1,0:T(8,128)}, f32[8,4096,256]{2,1,0:T(8,128)}) custom-call(f32[800,256]{1,0:T(8,128)} %get-tuple-element.188.a.emb_ref, s32[8,50]{1,0:T(8,128)} %match_ref.5, bf16[50,8,4096]{2,1,0:T(8,128)(2,1)} %bitcast.44, bf16[8,4096,256]{2,1,0:T(8,128)(2,1)} %mf_ref.7, ...), custom_call_target="tpu_custom_call", output_to_operand_aliasing={{0}: (4, {}), {1}: (5, {})} | custom-call | flops 335544320 | bytes 8339456 | tf_op jit(solution)/shard_map/mask_out/pallas_call | solution.py:640
  202.9 1.6 add.91
  204.5 2.3 collective-permute-start.27
  206.8 8.3 %mask_out.7 = (f32[800,4096]{1,0:T(8,128)}, f32[8,4096,256]{2,1,0:T(8,128)}) custom-call(f32[800,256]{1,0:T(8,128)} %get-tuple-element.188.a.emb_ref, s32[8,50]{1,0:T(8,128)} %match_ref.5, bf16[50,8,4096]{2,1,0:T(8,128)(2,1)} %bitcast.45, bf16[8,4096,256]{2,1,0:T(8,128)(2,1)} %mf_ref.7, ...), custom_call_target="tpu_custom_call", output_to_operand_aliasing={{0}: (4, {}), {1}: (5, {})} | custom-call | flops 671088640 | bytes 16678912 | tf_op jit(solution)/shard_map/mask_out/pallas_call | solution.py:640
  215.8 1.0 add.92
  216.7 1.0 collective-permute-start.30
  217.7 1.5 collective-permute-start.31
  219.2 1.1 collective-permute-start.32
  220.3 1.9 collective-permute-done.30
  222.2 1.6 collective-permute-done.31
  223.7 1.1 collective-permute-done.32
  224.9 1.8 collective-permute-done.33.refs_11_
  226.7 5.1 %unpack.1 = (f32[256,256]{1,0:T(8,128)}, f32[1,256]{1,0:T(1,128)}, f32[256,512]{1,0:T(8,128)}, f32[1,256]{1,0:T(1,128)}, f32[256,256]{1,0:T(8,128)}, /*index=5*/...) custom-call(s32[4]{0:T(128)S(1)} %copy-done.6, ...), custom_call_target="tpu_custom_call" | custom-call | flops 1000000 | bytes 16000000 | tf_op jit(solution)/shard_map/unpack/pallas_call | solution.py:938
  (75 shorter events, 11.8 us)
Async XLA Ops:
  28.9 12.1 %collective-permute-start = (f32[2,168,256]{2,1,0:T(8,128)}, f32[2,168,256]{2,1,0:T(8,128)S(1)}, u32[]{:S(2)}, u32[]{:S(2)}) collective-permute-start(f32[2,168,256]{2,1,0:T(8,128)} %get-tuple-element.144.refs_5_), channel_id=1, source_target_pairs={{0,1},{1,0},{2,3},{3,2},{4,5},{5,4},{6,7},{7,6},{8,9},{9,8},{10,11... | collective-permute-start | bytes 1032200 | tf_op jit(solution)/shard_map/ppermute | solution.py:959
  31.9 17.1 %collective-permute-start.1 = (f32[2,168,256]{2,1,0:T(8,128)}, f32[2,168,256]{2,1,0:T(8,128)S(1)}, u32[]{:S(2)}, u32[]{:S(2)}) collective-permute-start(f32[2,168,256]{2,1,0:T(8,128)} %get-tuple-element.145.refs_6_), channel_id=1, source_target_pairs={{0,2},{1,3},{2,0},{3,1},{4,6},{5,7},{6,4},{7,5},{8,10},{9,11},{10,... | collective-permute-start | bytes 1032200 | tf_op jit(solution)/shard_map/ppermute | solution.py:959
  33.5 15.5 %collective-permute-start.2 = (f32[2,168,256]{2,1,0:T(8,128)}, f32[2,168,256]{2,1,0:T(8,128)S(1)}, u32[]{:S(2)}, u32[]{:S(2)}) collective-permute-start(f32[2,168,256]{2,1,0:T(8,128)} %get-tuple-element.146.refs_7_), channel_id=1, source_target_pairs={{0,3},{1,2},{2,1},{3,0},{4,7},{5,6},{6,5},{7,4},{8,11},{9,10},{10,... | collective-permute-start | bytes 1032200 | tf_op jit(solution)/shard_map/ppermute | solution.py:959
  49.0 1.0 copy-start.2
  51.1 17.4 %copy-start.3 = (f32[2,168,256]{2,1,0:T(8,128)}, f32[2,168,256]{2,1,0:T(8,128)S(1)}, u32[]{:S(2)}) copy-start(f32[2,168,256]{2,1,0:T(8,128)S(1)} %combine.1.refs_0_) | copy-start | bytes 1032196
  51.1 11.1 %collective-permute-start.3 = (f32[2,168,256]{2,1,0:T(8,128)S(1)}, f32[2,168,256]{2,1,0:T(8,128)S(1)}, u32[]{:S(2)}, u32[]{:S(2)}) collective-permute-start(f32[2,168,256]{2,1,0:T(8,128)S(1)} %combine.1.refs_0_), channel_id=1, source_target_pairs={{0,1},{1,0},{2,3},{3,2},{4,5},{5,4},{6,7},{7,6},{8,9},{9,8},{10,11... | collective-permute-start | bytes 1032200 | tf_op jit(solution)/shard_map/ppermute | solution.py:959
  52.4 16.0 %collective-permute-start.4 = (f32[2,168,256]{2,1,0:T(8,128)S(1)}, f32[2,168,256]{2,1,0:T(8,128)S(1)}, u32[]{:S(2)}, u32[]{:S(2)}) collective-permute-start(f32[2,168,256]{2,1,0:T(8,128)S(1)} %combine.1.refs_0_), channel_id=1, source_target_pairs={{0,2},{1,3},{2,0},{3,1},{4,6},{5,7},{6,4},{7,5},{8,10},{9,11},{10,... | collective-permute-start | bytes 1032200 | tf_op jit(solution)/shard_map/ppermute | solution.py:959
  53.2 15.2 %collective-permute-start.5 = (f32[2,168,256]{2,1,0:T(8,128)S(1)}, f32[2,168,256]{2,1,0:T(8,128)S(1)}, u32[]{:S(2)}, u32[]{:S(2)}) collective-permute-start(f32[2,168,256]{2,1,0:T(8,128)S(1)} %combine.1.refs_0_), channel_id=1, source_target_pairs={{0,3},{1,2},{2,1},{3,0},{4,7},{5,6},{6,5},{7,4},{8,11},{9,10},{10,... | collective-permute-start | bytes 1032200 | tf_op jit(solution)/shard_map/ppermute | solution.py:959
  62.1 6.3 %copy-start.11 = (f32[2,168,256]{2,1,0:T(8,128)}, f32[2,168,256]{2,1,0:T(8,128)S(1)}, u32[]{:S(2)}) copy-start(f32[2,168,256]{2,1,0:T(8,128)S(1)} %collective-permute-done.3.refs_1_) | copy-start | bytes 1032196
  68.4 0.7 copy-start.12
  68.4 0.8 copy-start.13
  106.9 10.1 %collective-permute-start.6 = (f32[800,256]{1,0:T(8,128)}, f32[800,256]{1,0:T(8,128)S(1)}, u32[]{:S(2)}, u32[]{:S(2)}) collective-permute-start(f32[800,256]{1,0:T(8,128)} %get-tuple-element.162), channel_id=1, source_target_pairs={{0,4},{4,0},{8,12},{12,8},{16,20},{20,16},{24,28},{28,24},{1,5},{5... | collective-permute-start | bytes 2457608 | tf_op jit(solution)/shard_map/ppermute | solution.py:959
  107.2 9.9 %copy-start.7 = (f32[800,256]{1,0:T(8,128)S(1)}, f32[800,256]{1,0:T(8,128)}, u32[]{:S(2)}) copy-start(f32[800,256]{1,0:T(8,128)} %get-tuple-element.161) | copy-start | bytes 2457604
  117.3 26.5 %collective-permute-start.7 = (f32[200,256]{1,0:T(8,128)S(1)}, f32[200,256]{1,0:T(8,128)S(1)}, u32[]{:S(2)}, u32[]{:S(2)}) collective-permute-start(f32[200,256]{1,0:T(8,128)S(1)} %get-tuple-element.267), channel_id=1, source_target_pairs={{0,8},{4,12},{8,0},{12,4},{16,24},{20,28},{24,16},{28,20},{1,9},{5... | collective-permute-start | bytes 614408 | tf_op jit(solution)/shard_map/ppermute | solution.py:959
  118.9 24.9 %collective-permute-start.8 = (f32[200,256]{1,0:T(8,128)S(1)}, f32[200,256]{1,0:T(8,128)S(1)}, u32[]{:S(2)}, u32[]{:S(2)}) collective-permute-start(f32[200,256]{1,0:T(8,128)S(1)} %get-tuple-element.266), channel_id=1, source_target_pairs={{0,16},{4,20},{8,24},{12,28},{16,0},{20,4},{24,8},{28,12},{1,17},{... | collective-permute-start | bytes 614408 | tf_op jit(solution)/shard_map/ppermute | solution.py:959
  121.5 22.3 %collective-permute-start.9 = (f32[200,256]{1,0:T(8,128)S(1)}, f32[200,256]{1,0:T(8,128)S(1)}, u32[]{:S(2)}, u32[]{:S(2)}) collective-permute-start(f32[200,256]{1,0:T(8,128)S(1)} %get-tuple-element.265), channel_id=1, source_target_pairs={{0,24},{4,28},{8,16},{12,20},{16,8},{20,12},{24,0},{28,4},{1,25},{... | collective-permute-start | bytes 614408 | tf_op jit(solution)/shard_map/ppermute | solution.py:959
  121.7 22.1 %collective-permute-start.10 = (f32[2,104,256]{2,1,0:T(8,128)}, f32[2,104,256]{2,1,0:T(8,128)S(1)}, u32[]{:S(2)}, u32[]{:S(2)}) collective-permute-start(f32[2,104,256]{2,1,0:T(8,128)} %get-tuple-element.181), channel_id=1, source_target_pairs={{0,3},{1,2},{2,1},{3,0},{4,7},{5,6},{6,5},{7,4},{8,11},{9,10},{10,... | collective-permute-start | bytes 638984 | tf_op jit(solution)/shard_map/ppermute | solution.py:959
  143.8 16.0 %copy-start = (f32[544,256]{1,0:T(8,128)S(1)}, f32[544,256]{1,0:T(8,128)}, u32[]{:S(2)}) copy-start(f32[544,256]{1,0:T(8,128)} %get-tuple-element.196.refs_4_) | copy-start | bytes 1671172
  143.8 16.0 %copy-start.4 = (f32[2,104,256]{2,1,0:T(8,128)S(1)}, f32[2,104,256]{2,1,0:T(8,128)}, u32[]{:S(2)}) copy-start(f32[2,104,256]{2,1,0:T(8,128)} %get-tuple-element.192.refs_0_) | copy-start | bytes 638980
  143.8 16.0 %copy-start.5 = (s32[4]{0:T(128)S(1)}, s32[4]{0:T(128)}, u32[]{:S(2)}) copy-start(s32[4]{0:T(128)} %pad_add_fusion.me_ref.refs_0_) | copy-start | bytes 52
  143.8 13.6 %collective-permute-start.11 = (f32[2,104,256]{2,1,0:T(8,128)}, f32[2,104,256]{2,1,0:T(8,128)S(1)}, u32[]{:S(2)}, u32[]{:S(2)}) collective-permute-start(f32[2,104,256]{2,1,0:T(8,128)} %get-tuple-element.186), channel_id=1, source_target_pairs={{0,1},{1,0},{2,3},{3,2},{4,5},{5,4},{6,7},{7,6},{8,9},{9,8},{10,11... | collective-permute-start | bytes 638984 | tf_op jit(solution)/shard_map/ppermute | solution.py:959
  144.8 12.6 %collective-permute-start.12 = (f32[2,104,256]{2,1,0:T(8,128)}, f32[2,104,256]{2,1,0:T(8,128)S(1)}, u32[]{:S(2)}, u32[]{:S(2)}) collective-permute-start(f32[2,104,256]{2,1,0:T(8,128)} %get-tuple-element.187), channel_id=1, source_target_pairs={{0,2},{1,3},{2,0},{3,1},{4,6},{5,7},{6,4},{7,5},{8,10},{9,11},{10,... | collective-permute-start | bytes 638984 | tf_op jit(solution)/shard_map/ppermute | solution.py:959
  146.4 11.0 %collective-permute-start.13 = (f32[200,256]{1,0:T(8,128)S(1)}, f32[200,256]{1,0:T(8,128)S(1)}, u32[]{:S(2)}, u32[]{:S(2)}) collective-permute-start(f32[200,256]{1,0:T(8,128)S(1)} %add_add_fusion), channel_id=1, source_target_pairs={{0,16},{4,20},{8,24},{12,28},{16,0},{20,4},{24,8},{28,12},{1,17},{... | collective-permute-start | bytes 614408 | tf_op jit(solution)/shard_map/ppermute | solution.py:959
  158.3 19.0 %collective-permute-start.17 = (f32[400,256]{1,0:T(8,128)}, f32[400,256]{1,0:T(8,128)S(1)}, u32[]{:S(2)}, u32[]{:S(2)}) collective-permute-start(f32[400,256]{1,0:T(8,128)} %pad_maximum_fusion.4), channel_id=1, source_target_pairs={{0,8},{4,12},{8,0},{12,4},{16,24},{20,28},{24,16},{28,20},{1,9},{5... | collective-permute-start | bytes 1228808 | tf_op jit(solution)/shard_map/ppermute | solution.py:959
  160.4 0.7 copy-start.1
  161.2 15.2 %collective-permute-start.14 = (f32[344,256]{1,0:T(8,128)S(1)}, f32[344,256]{1,0:T(8,128)S(1)}, u32[]{:S(2)}, u32[]{:S(2)}) collective-permute-start(f32[344,256]{1,0:T(8,128)S(1)} %get-tuple-element.204), channel_id=1, source_target_pairs={{0,1},{1,0},{2,3},{3,2},{4,5},{5,4},{6,7},{7,6},{8,9},{9,8},{10,11... | collective-permute-start | bytes 1056776 | tf_op jit(solution)/shard_map/ppermute | solution.py:959
  161.8 15.5 %collective-permute-start.15 = (f32[344,256]{1,0:T(8,128)S(1)}, f32[344,256]{1,0:T(8,128)S(1)}, u32[]{:S(2)}, u32[]{:S(2)}) collective-permute-start(f32[344,256]{1,0:T(8,128)S(1)} %get-tuple-element.205), channel_id=1, source_target_pairs={{0,2},{1,3},{2,0},{3,1},{4,6},{5,7},{6,4},{7,5},{8,10},{9,11},{10,... | collective-permute-start | bytes 1056776 | tf_op jit(solution)/shard_map/ppermute | solution.py:959
  162.8 14.5 %collective-permute-start.16 = (f32[344,256]{1,0:T(8,128)S(1)}, f32[344,256]{1,0:T(8,128)S(1)}, u32[]{:S(2)}, u32[]{:S(2)}) collective-permute-start(f32[344,256]{1,0:T(8,128)S(1)} %get-tuple-element.206), channel_id=1, source_target_pairs={{0,3},{1,2},{2,1},{3,0},{4,7},{5,6},{6,5},{7,4},{8,11},{9,10},{10,... | collective-permute-start | bytes 1056776 | tf_op jit(solution)/shard_map/ppermute | solution.py:959
  176.3 1.0 copy-start.8
  177.3 0.7 copy-start.9
  177.3 0.8 copy-start.10
  178.2 13.1 %collective-permute-start.20 = (f32[800,256]{1,0:T(8,128)S(1)}, f32[800,256]{1,0:T(8,128)S(1)}, u32[]{:S(2)}, u32[]{:S(2)}) collective-permute-start(f32[800,256]{1,0:T(8,128)S(1)} %pad_maximum_fusion.refs_0_), channel_id=1, source_target_pairs={{0,4},{4,0},{8,12},{12,8},{16,20},{20,16},{24,28},{28,24},{1,5},{5... | collective-permute-start | bytes 2457608 | tf_op jit(solution)/shard_map/ppermute | solution.py:959
  178.2 11.9 %collective-permute-start.18 = (f32[400,256]{1,0:T(8,128)S(1)}, f32[400,256]{1,0:T(8,128)S(1)}, u32[]{:S(2)}, u32[]{:S(2)}) collective-permute-start(f32[400,256]{1,0:T(8,128)S(1)} %get-tuple-element.264), channel_id=1, source_target_pairs={{0,1},{1,0},{2,3},{3,2},{4,5},{5,4},{6,7},{7,6},{8,9},{9,8},{10,11... | collective-permute-start | bytes 1228808 | tf_op jit(solution)/shard_map/ppermute | solution.py:959
  179.7 11.5 %collective-permute-start.19 = (f32[400,256]{1,0:T(8,128)S(1)}, f32[400,256]{1,0:T(8,128)S(1)}, u32[]{:S(2)}, u32[]{:S(2)}) collective-permute-start(f32[400,256]{1,0:T(8,128)S(1)} %get-tuple-element.263), channel_id=1, source_target_pairs={{0,2},{1,3},{2,0},{3,1},{4,6},{5,7},{6,4},{7,5},{8,10},{9,11},{10,... | collective-permute-start | bytes 1228808 | tf_op jit(solution)/shard_map/ppermute | solution.py:959
  184.5 1.5 collective-permute-start.21
  192.2 22.9 %collective-permute-start.23 = (f32[800,256]{1,0:T(8,128)}, f32[800,256]{1,0:T(8,128)S(1)}, u32[]{:S(2)}, u32[]{:S(2)}) collective-permute-start(f32[800,256]{1,0:T(8,128)} %pad_maximum_fusion.2), channel_id=1, source_target_pairs={{0,1},{1,0},{2,3},{3,2},{4,5},{5,4},{6,7},{7,6},{8,9},{9,8},{10,11... | collective-permute-start | bytes 2457608 | tf_op jit(solution)/shard_map/ppermute | solution.py:959
  193.8 21.4 %collective-permute-start.22 = (f32[800,256]{1,0:T(8,128)}, f32[800,256]{1,0:T(8,128)S(1)}, u32[]{:S(2)}, u32[]{:S(2)}) collective-permute-start(f32[800,256]{1,0:T(8,128)} %pad_maximum_fusion.1), channel_id=1, source_target_pairs={{0,2},{1,3},{2,0},{3,1},{4,6},{5,7},{6,4},{7,5},{8,10},{9,11},{10,... | collective-permute-start | bytes 2457608 | tf_op jit(solution)/shard_map/ppermute | solution.py:959
  194.8 20.3 %collective-permute-start.24 = (f32[400,256]{1,0:T(8,128)S(1)}, f32[400,256]{1,0:T(8,128)}, u32[]{:S(2)}, u32[]{:S(2)}) collective-permute-start(f32[400,256]{1,0:T(8,128)S(1)} %collective-permute-done.18.refs_1_), channel_id=1, source_target_pairs={{0,4},{4,0},{8,12},{12,8},{16,20},{20,16},{24,28},{28,24},{1,5},{5... | collective-permute-start | bytes 1228808 | tf_op jit(solution)/shard_map/ppermute | solution.py:959
  194.8 20.3 %collective-permute-start.25 = (f32[400,256]{1,0:T(8,128)S(1)}, f32[400,256]{1,0:T(8,128)}, u32[]{:S(2)}, u32[]{:S(2)}) collective-permute-start(f32[400,256]{1,0:T(8,128)S(1)} %collective-permute-done.19.refs_2_), channel_id=1, source_target_pairs={{0,4},{4,0},{8,12},{12,8},{16,20},{20,16},{24,28},{28,24},{1,5},{5... | collective-permute-start | bytes 1228808 | tf_op jit(solution)/shard_map/ppermute | solution.py:959
  195.3 7.6 %collective-permute-start.26 = (f32[104,256]{1,0:T(8,128)}, f32[104,256]{1,0:T(8,128)}, u32[]{:S(2)}, u32[]{:S(2)}) collective-permute-start(f32[104,256]{1,0:T(8,128)} %add.90), channel_id=1, source_target_pairs={{0,8},{4,12},{8,0},{12,4},{16,24},{20,28},{24,16},{28,20},{1,9},{5... | collective-permute-start | bytes 319496 | tf_op jit(solution)/shard_map/ppermute | solution.py:959
  204.5 22.2 %copy-start.6 = (s32[4]{0:T(128)S(1)}, s32[4]{0:T(128)}, u32[]{:S(2)}) copy-start(s32[4]{0:T(128)} %pad_add_fusion.me_ref.refs_0_) | copy-start | bytes 52
  204.5 10.6 %collective-permute-start.27 = (f32[104,256]{1,0:T(8,128)}, f32[104,256]{1,0:T(8,128)}, u32[]{:S(2)}, u32[]{:S(2)}) collective-permute-start(f32[104,256]{1,0:T(8,128)} %add.91), channel_id=1, source_target_pairs={{0,16},{4,20},{8,24},{12,28},{16,0},{20,4},{24,8},{28,12},{1,17},{... | collective-permute-start | bytes 319496 | tf_op jit(solution)/shard_map/ppermute | solution.py:959
  215.2 11.5 %collective-permute-start.28 = (f32[800,256]{1,0:T(8,128)S(1)}, f32[800,256]{1,0:T(8,128)S(1)}, u32[]{:S(2)}, u32[]{:S(2)}) collective-permute-start(f32[800,256]{1,0:T(8,128)S(1)} %collective-permute-done.22.refs_3_), channel_id=1, source_target_pairs={{0,4},{4,0},{8,12},{12,8},{16,20},{20,16},{24,28},{28,24},{1,5},{5... | collective-permute-start | bytes 2457608 | tf_op jit(solution)/shard_map/ppermute | solution.py:959
  215.3 11.4 %collective-permute-start.29 = (f32[800,256]{1,0:T(8,128)S(1)}, f32[800,256]{1,0:T(8,128)S(1)}, u32[]{:S(2)}, u32[]{:S(2)}) collective-permute-start(f32[800,256]{1,0:T(8,128)S(1)} %collective-permute-done.23.refs_4_), channel_id=1, source_target_pairs={{0,4},{4,0},{8,12},{12,8},{16,20},{20,16},{24,28},{28,24},{1,5},{5... | collective-permute-start | bytes 2457608 | tf_op jit(solution)/shard_map/ppermute | solution.py:959
  216.7 5.5 %collective-permute-start.30 = (f32[104,256]{1,0:T(8,128)S(1)}, f32[104,256]{1,0:T(8,128)S(1)}, u32[]{:S(2)}, u32[]{:S(2)}) collective-permute-start(f32[104,256]{1,0:T(8,128)S(1)} %add.92), channel_id=1, source_target_pairs={{0,1},{1,0},{2,3},{3,2},{4,5},{5,4},{6,7},{7,6},{8,9},{9,8},{10,11... | collective-permute-start | bytes 319496 | tf_op jit(solution)/shard_map/ppermute | solution.py:959
  217.7 6.0 %collective-permute-start.31 = (f32[104,256]{1,0:T(8,128)S(1)}, f32[104,256]{1,0:T(8,128)S(1)}, u32[]{:S(2)}, u32[]{:S(2)}) collective-permute-start(f32[104,256]{1,0:T(8,128)S(1)} %add.92), channel_id=1, source_target_pairs={{0,2},{1,3},{2,0},{3,1},{4,6},{5,7},{6,4},{7,5},{8,10},{9,11},{10,... | collective-permute-start | bytes 319496 | tf_op jit(solution)/shard_map/ppermute | solution.py:959
  219.2 5.6 %collective-permute-start.32 = (f32[104,256]{1,0:T(8,128)S(1)}, f32[104,256]{1,0:T(8,128)S(1)}, u32[]{:S(2)}, u32[]{:S(2)}) collective-permute-start(f32[104,256]{1,0:T(8,128)S(1)} %add.92), channel_id=1, source_target_pairs={{0,3},{1,2},{2,1},{3,0},{4,7},{5,6},{6,5},{7,4},{8,11},{9,10},{10,... | collective-permute-start | bytes 319496 | tf_op jit(solution)/shard_map/ppermute | solution.py:959
  224.8 1.8 collective-permute-start.33

commit v3 on v1

--- a/solution.py
+++ b/solution.py
@@ -1064,7 +1064,7 @@
         qp1, qp2 = swap(qp1, "pix", n_pix, 1), swap(qp2, "pix", n_pix, 2)
         own = functools.reduce(jnp.add, sums)
         other = swap(own, "batch", n_batch, 4)
-        cuts = [blocks * k // 8 for k in (0, 2, 5, 8)]
+        cuts = [blocks * k // 8 for k in (0, 2, 4, 8)]
         outs = mask((cuts[0], cuts[1]))
         qp1, qp2, other, outs = beside(qp1, qp2, other, outs)
         own = join(own, other, "batch", 4)
@@ -1073,12 +1073,13 @@
         *parts, outs = beside(*query_sum(me, (qp0, qp1, qp2, qp3), g_kv), outs)
         parts = tuple(p if k == 0 else swap(p, "pix", n_pix, k) for k, p in enumerate(parts))
         outs = mask((cuts[1], cuts[2]), outs)
-        *parts, other, outs = beside(*parts, other, outs)
+        parts = list(parts)
+        parts[1], other, outs = beside(parts[1], other, outs)
         own = join(own, other, "batch", 2)
         low, high = own[:own.shape[0] // 2], own[own.shape[0] // 2:]
         low1, high2 = swap(low, "pix", n_pix, 1), swap(high, "pix", n_pix, 2)
         own2 = swap(own, "batch", n_batch, 1)
-        queries_grad, tail, tail2 = query_back(me, parts, queries, dp1, query_weight)
+        queries_grad, tail, tail2 = query_back(me, tuple(parts), queries, dp1, query_weight)
         tail = tail + swap(tail2, "batch", n_batch, 1)
         tail2 = swap(tail, "batch", n_batch, 2)
         low1, high2, own2, tail2, outs = beside(low1, high2, own2, tail2, outs)

time: 231 us -> 242 us (1.048)
  waiting for transfers between devices: 40.9 us -> 52.8 us
    ppermute x34, waiting for transfers between devices: 40.9 us -> 52.8 us  [swap(): return lax.ppermute(x, axis, [(d, d ^ key) for d in range(n)])]
  transfers between devices with their start and end apart: 34 -> 34, of which waited for: 14 -> 12; matrix products, arithmetic and copies ran while one was open for 2% -> 1% of each run, Pallas kernels for 31% -> 30%
where the time goes in v3:
time: 242 us; the launch traced here: 241 us
  Pallas kernels  143 us (59%)
  waiting for transfers between devices  52.8 us (22%)
  starting transfers between devices  34.1 us (14%)
  other arithmetic  5.41 us (2%)
  local copies, waits for them, and re-layouts  4.74 us (2%)
    ppermute x34, waiting for transfers between devices, swap(): return lax.ppermute(x, axis, [(d, d ^ key) for d in range(n)])  52.8 us
    pallas_call x1, Pallas kernels, chain(): pl.pallas_call(functools.partial(chain_kernel, pieces), grid_spec=pltpu.P...  37.7 us
    ppermute x34, starting transfers between devices, swap(): return lax.ppermute(x, axis, [(d, d ^ key) for d in range(n)])  34.1 us
    pallas_call x3, Pallas kernels, mask_out(): pl.pallas_call(kernel, grid=(last - first,), in_specs=[whole(emb), whole(...  31.2 us
    pallas_call x2, Pallas kernels, attend_back(): pl.pallas_call(kernel, grid_spec=pltpu.PrefetchScalarGridSpec(num_scalar_...  30.9 us
    pallas_call x1, Pallas kernels, attend(): pl.pallas_call(functools.partial(attend_kernel, keys, n), grid_spec=pltpu...  27.6 us
    pallas_call x1, Pallas kernels, unpack(): pl.pallas_call(functools.partial(unpack_kernel, split), grid_spec=pltpu.P...  5.11 us
  transfers between devices with their start and end apart: 34, of which 12 were waited for; matrix products, arithmetic and copies ran while one was open for 1% of the time, Pallas kernels for 30%

profile of v3, /device:TPU:0, one launch (start us, length us, event | category | flops | bytes accessed | tf_op | source)
XLA Modules:
  0.0 241.1 jit_solution(2490426695907805634)
XLA Ops:
  1.3 27.6 %attend.1 = (bf16[8,8,104,1024]{3,2,1,0:T(8,128)(2,1)}, bf16[8,512,1024]{2,1,0:T(8,128)(2,1)}, f32[8,104,256]{2,1,0:T(8,128)}, f32[2,168,256]{2,1,0:T(8,128)}, f...) custom-call(s32[4]{0:T(128)} %pad_add_fusion.me_ref.refs_0_, f32[800,256]{1,0:T(8,128)} %bitcast.46, ...), custom_call_target="tpu_custom_call" | custom-call | flops 9126805504 | bytes 46268416 | tf_op jit(solution)/shard_map/attend/pallas_call | solution.py:234
  28.9 3.0 %collective-permute-start = (f32[2,168,256]{2,1,0:T(8,128)}, f32[2,168,256]{2,1,0:T(8,128)S(1)}, u32[]{:S(2)}, u32[]{:S(2)}) collective-permute-start(f32[2,168,256]{2,1,0:T(8,128)} %get-tuple-element.136.refs_5_), channel_id=1, source_target_pairs={{0,1},{1,0},{2,3},{3,2},{4,5},{5,4},{6,7},{7,6},{8,9},{9,8},{10,11... | collective-permute-start | bytes 1032200 | tf_op jit(solution)/shard_map/ppermute | solution.py:959
  31.9 1.6 collective-permute-start.1
  33.4 7.5 %collective-permute-done.refs_1_ = f32[2,168,256]{2,1,0:T(8,128)S(1)} collective-permute-done((f32[2,168,256]{2,1,0:T(8,128)}, f32[2,168,256]{2,1,0:T(8,128)S(1)}, u32[]{:S(2)}, u32[]{:S(2)}) %collective-permute-start) | collective-permute-done | bytes 344096 | tf_op jit(solution)/shard_map/ppermute | solution.py:959
  41.0 8.0 %collective-permute-done.1.refs_2_ = f32[2,168,256]{2,1,0:T(8,128)S(1)} collective-permute-done((f32[2,168,256]{2,1,0:T(8,128)}, f32[2,168,256]{2,1,0:T(8,128)S(1)}, u32[]{:S(2)}, u32[]{:S(2)}) %collective-permute-start.1) | collective-permute-done | bytes 344096 | tf_op jit(solution)/shard_map/ppermute | solution.py:959
  49.0 1.0 copy-done.2
  50.0 1.1 combine.1.refs_0_
  51.1 1.3 collective-permute-start.3
  52.4 0.8 collective-permute-start.4
  53.2 1.4 collective-permute-start.5
  54.6 4.5 %lower.1 = (bf16[256,256]{1,0:T(8,128)(2,1)}, bf16[256,768]{1,0:T(8,128)(2,1)}, bf16[256,256]{1,0:T(8,128)(2,1)}, bf16[256,2048]{1,0:T(8,128)(2,1)}, bf16[2048,2...) custom-call(f32[256,256]{1,0:T(8,128)} %refs_0_, f32[256,768]{1,0:T(8,128)} %refs_1_, f32[256,256]{1,0:T(8,128)} %refs_2_, ...), custom_call_target="tpu_custom_call" | custom-call | flops 1572864 | bytes 9437184 | tf_op jit(solution)/shard_map/lower/pallas_call | solution.py:300
  59.1 3.0 %collective-permute-done.3.refs_1_ = f32[2,168,256]{2,1,0:T(8,128)S(1)} collective-permute-done((f32[2,168,256]{2,1,0:T(8,128)S(1)}, f32[2,168,256]{2,1,0:T(8,128)S(1)}, u32[]{:S(2)}, u32[]{:S(2)}) %collective-permute-start.3) | collective-permute-done | bytes 344096 | tf_op jit(solution)/shard_map/ppermute | solution.py:959
  62.1 6.3 %collective-permute-done.4.refs_2_ = f32[2,168,256]{2,1,0:T(8,128)S(1)} collective-permute-done((f32[2,168,256]{2,1,0:T(8,128)S(1)}, f32[2,168,256]{2,1,0:T(8,128)S(1)}, u32[]{:S(2)}, u32[]{:S(2)}) %collective-permute-start.4) | collective-permute-done | bytes 344096 | tf_op jit(solution)/shard_map/ppermute | solution.py:959
  69.3 37.7 %chain.1 = (f32[800,256]{1,0:T(8,128)}, f32[800,256]{1,0:T(8,128)}, f32[8,104,256]{2,1,0:T(8,128)}, f32[8,104,128]{2,1,0:T(8,128)}, f32[8,104,256]{2,1,0:T(8,128...) custom-call(s32[4]{0:T(128)} %pad_add_fusion.me_ref.refs_0_, f32[2,168,256]{2,1,0:T(8,128)} %copy-done.3, ...), custom_call_target="tpu_custom_call" | custom-call | flops 16000000000 | bytes 20000000 | tf_op jit(solution)/shard_map/chain/pallas_call | solution.py:560
  107.2 9.9 %attend_back.2 = (f32[8,1024,256]{2,1,0:T(8,128)}, f32[512,256]{1,0:T(8,128)}, f32[256,128]{1,0:T(8,128)}, f32[2,104,256]{2,1,0:T(8,128)}) custom-call(s32[4]{0:T(128)} %pad_add_fusion.me_ref.refs_0_, bf16[8,8,104,1024]{3,2,1,0:T(8,128)(2,1)} %get-tuple-element.155.refs_1_, bf16[8,512,1024]{2,1,0:T(8,128)(2,1)} %get-tuple-element.156.refs_2_, ...), custom_call_target="tpu_custom_call" | custom-call | flops 4563402752 | bytes 8650752 | tf_op jit(solution)/shard_map/attend_back/pallas_call | solution.py:773
  117.3 1.6 collective-permute-start.7
  118.9 2.6 %collective-permute-start.8 = (f32[200,256]{1,0:T(8,128)S(1)}, f32[200,256]{1,0:T(8,128)S(1)}, u32[]{:S(2)}, u32[]{:S(2)}) collective-permute-start(f32[200,256]{1,0:T(8,128)S(1)} %get-tuple-element.250), channel_id=1, source_target_pairs={{0,16},{4,20},{8,24},{12,28},{16,0},{20,4},{24,8},{28,12},{1,17},{... | collective-permute-start | bytes 614408 | tf_op jit(solution)/shard_map/ppermute | solution.py:959
  121.7 1.1 collective-permute-start.10
  122.8 21.0 %attend_back.3 = (f32[8,1024,256]{2,1,0:T(8,128)}, f32[544,256]{1,0:T(8,128)}, f32[2,104,256]{2,1,0:T(8,128)}, f32[2,104,256]{2,1,0:T(8,128)}, f32[2,104,256]{2,1,0:T(8,128)}) custom-call(s32[4]{0:T(128)} %pad_add_fusion.me_ref.refs_0_, bf16[8,8,104,1024]{3,2,1,0:T(8,128)(2,1)} %get-tuple-element.155.refs_1_, ...), custom_call_target="tpu_custom_call", output_to_operand_aliasing={{0}: (8, {})} | custom-call | flops 13690208256 | bytes 25952256 | tf_op jit(solution)/shard_map/attend_back/pallas_call | solution.py:773
  143.8 1.0 collective-permute-start.11
  144.8 1.5 collective-permute-start.12
  146.4 1.8 collective-permute-start.13
  148.1 8.4 %mask_out.3 = (f32[800,4096]{1,0:T(8,128)}, f32[8,4096,256]{2,1,0:T(8,128)}) custom-call(f32[800,256]{1,0:T(8,128)} %get-tuple-element.180.a.emb_ref, s32[8,50]{1,0:T(8,128)} %match_ref.3, bf16[50,8,4096]{2,1,0:T(8,128)(2,1)} %bitcast.42, bf16[8,4096,256]{2,1,0:T(8,128)(2,1)} %mf_ref.5), custom_call_target="tpu_custom_call" | custom-call | flops 671088640 | bytes 16678912 | tf_op jit(solution)/shard_map/mask_out/pallas_call | solution.py:640
  156.5 0.9 collective-permute-done.13
  157.5 1.7 collective-permute-start.15
  161.1 8.3 %mask_out.4 = (f32[800,4096]{1,0:T(8,128)}, f32[8,4096,256]{2,1,0:T(8,128)}) custom-call(f32[800,256]{1,0:T(8,128)} %get-tuple-element.180.a.emb_ref, s32[8,50]{1,0:T(8,128)} %match_ref.3, bf16[50,8,4096]{2,1,0:T(8,128)(2,1)} %bitcast.43, bf16[8,4096,256]{2,1,0:T(8,128)(2,1)} %mf_ref.5, ...), custom_call_target="tpu_custom_call", output_to_operand_aliasing={{0}: (4, {}), {1}: (5, {})} | custom-call | flops 671088640 | bytes 16678912 | tf_op jit(solution)/shard_map/mask_out/pallas_call | solution.py:640
  170.3 1.1 collective-permute-start.19
  171.4 1.9 collective-permute-start.20
  173.8 1.0 collective-permute-start.17
  174.9 14.1 %collective-permute-done.19.refs_2_ = f32[344,256]{1,0:T(8,128)S(1)} collective-permute-done((f32[344,256]{1,0:T(8,128)S(1)}, f32[344,256]{1,0:T(8,128)S(1)}, u32[]{:S(2)}, u32[]{:S(2)}) %collective-permute-start.19) | collective-permute-done | bytes 352288 | tf_op jit(solution)/shard_map/ppermute | solution.py:959
  189.7 0.7 copy-done.10
  190.4 4.2 %query_back.1 = (f32[800,256]{1,0:T(8,128)}, f32[104,256]{1,0:T(8,128)}, f32[104,256]{1,0:T(8,128)}) custom-call(s32[4]{0:T(128)} %pad_add_fusion.me_ref.refs_0_, f32[344,256]{1,0:T(8,128)} %copy-done.1, f32[344,256]{1,0:T(8,128)} %copy-done.8, f32[344,256]{1,0:T(8,128)} %copy-done.9, f32[344,256]{1,0:T(8,128)} %copy-done.10, f32[800,256]{1,0:T(8,128)} %bitcast.48, ...), custom_call_target="tpu_custom_call" | custom-call | flops 500000000 | bytes 8000000 | tf_op jit(solution)/shard_map/query_back/pallas_call | solution.py:858
  194.6 1.5 collective-permute-done.21
  196.1 0.9 add.90
  197.5 4.6 %collective-permute-done.22 = f32[104,256]{1,0:T(8,128)S(1)} collective-permute-done((f32[104,256]{1,0:T(8,128)S(1)}, f32[104,256]{1,0:T(8,128)S(1)}, u32[]{:S(2)}, u32[]{:S(2)}) %collective-permute-start.22) | collective-permute-done | bytes 106528 | tf_op jit(solution)/shard_map/ppermute | solution.py:959
  202.1 0.9 pad_maximum_fusion.2
  203.0 1.5 collective-permute-start.24
  204.5 0.9 pad_maximum_fusion.1
  207.1 2.1 collective-permute-start.27
  209.3 14.5 %mask_out.5 = (f32[800,4096]{1,0:T(8,128)}, f32[8,4096,256]{2,1,0:T(8,128)}) custom-call(f32[800,256]{1,0:T(8,128)} %get-tuple-element.180.a.emb_ref, s32[8,50]{1,0:T(8,128)} %match_ref.3, bf16[50,8,4096]{2,1,0:T(8,128)(2,1)} %bitcast.44, bf16[8,4096,256]{2,1,0:T(8,128)(2,1)} %mf_ref.5, ...), custom_call_target="tpu_custom_call", output_to_operand_aliasing={{0}: (4, {}), {1}: (5, {})} | custom-call | flops 1342177280 | bytes 33357824 | tf_op jit(solution)/shard_map/mask_out/pallas_call | solution.py:640
  223.8 1.0 collective-permute-done.23.refs_3_
  225.4 1.0 add.92
  227.0 1.0 collective-permute-start.31
  228.0 1.9 collective-permute-start.32
  229.9 2.2 collective-permute-done.30
  232.1 1.9 collective-permute-done.31
  234.1 1.8 collective-permute-done.33.refs_11_
  235.8 5.1 %unpack.1 = (f32[256,256]{1,0:T(8,128)}, f32[1,256]{1,0:T(1,128)}, f32[256,512]{1,0:T(8,128)}, f32[1,256]{1,0:T(1,128)}, f32[256,256]{1,0:T(8,128)}, /*index=5*/...) custom-call(s32[4]{0:T(128)S(1)} %copy-done.6, ...), custom_call_target="tpu_custom_call" | custom-call | flops 1000000 | bytes 16000000 | tf_op jit(solution)/shard_map/unpack/pallas_call | solution.py:938
  (74 shorter events, 9.7 us)
Async XLA Ops:
  28.9 12.1 %collective-permute-start = (f32[2,168,256]{2,1,0:T(8,128)}, f32[2,168,256]{2,1,0:T(8,128)S(1)}, u32[]{:S(2)}, u32[]{:S(2)}) collective-permute-start(f32[2,168,256]{2,1,0:T(8,128)} %get-tuple-element.136.refs_5_), channel_id=1, source_target_pairs={{0,1},{1,0},{2,3},{3,2},{4,5},{5,4},{6,7},{7,6},{8,9},{9,8},{10,11... | collective-permute-start | bytes 1032200 | tf_op jit(solution)/shard_map/ppermute | solution.py:959
  31.9 17.1 %collective-permute-start.1 = (f32[2,168,256]{2,1,0:T(8,128)}, f32[2,168,256]{2,1,0:T(8,128)S(1)}, u32[]{:S(2)}, u32[]{:S(2)}) collective-permute-start(f32[2,168,256]{2,1,0:T(8,128)} %get-tuple-element.137.refs_6_), channel_id=1, source_target_pairs={{0,2},{1,3},{2,0},{3,1},{4,6},{5,7},{6,4},{7,5},{8,10},{9,11},{10,... | collective-permute-start | bytes 1032200 | tf_op jit(solution)/shard_map/ppermute | solution.py:959
  33.4 15.5 %collective-permute-start.2 = (f32[2,168,256]{2,1,0:T(8,128)}, f32[2,168,256]{2,1,0:T(8,128)S(1)}, u32[]{:S(2)}, u32[]{:S(2)}) collective-permute-start(f32[2,168,256]{2,1,0:T(8,128)} %get-tuple-element.138.refs_7_), channel_id=1, source_target_pairs={{0,3},{1,2},{2,1},{3,0},{4,7},{5,6},{6,5},{7,4},{8,11},{9,10},{10,... | collective-permute-start | bytes 1032200 | tf_op jit(solution)/shard_map/ppermute | solution.py:959
  49.0 1.0 copy-start.2
  51.0 17.4 %copy-start.3 = (f32[2,168,256]{2,1,0:T(8,128)}, f32[2,168,256]{2,1,0:T(8,128)S(1)}, u32[]{:S(2)}) copy-start(f32[2,168,256]{2,1,0:T(8,128)S(1)} %combine.1.refs_0_) | copy-start | bytes 1032196
  51.1 11.1 %collective-permute-start.3 = (f32[2,168,256]{2,1,0:T(8,128)S(1)}, f32[2,168,256]{2,1,0:T(8,128)S(1)}, u32[]{:S(2)}, u32[]{:S(2)}) collective-permute-start(f32[2,168,256]{2,1,0:T(8,128)S(1)} %combine.1.refs_0_), channel_id=1, source_target_pairs={{0,1},{1,0},{2,3},{3,2},{4,5},{5,4},{6,7},{7,6},{8,9},{9,8},{10,11... | collective-permute-start | bytes 1032200 | tf_op jit(solution)/shard_map/ppermute | solution.py:959
  52.4 16.0 %collective-permute-start.4 = (f32[2,168,256]{2,1,0:T(8,128)S(1)}, f32[2,168,256]{2,1,0:T(8,128)S(1)}, u32[]{:S(2)}, u32[]{:S(2)}) collective-permute-start(f32[2,168,256]{2,1,0:T(8,128)S(1)} %combine.1.refs_0_), channel_id=1, source_target_pairs={{0,2},{1,3},{2,0},{3,1},{4,6},{5,7},{6,4},{7,5},{8,10},{9,11},{10,... | collective-permute-start | bytes 1032200 | tf_op jit(solution)/shard_map/ppermute | solution.py:959
  53.2 15.2 %collective-permute-start.5 = (f32[2,168,256]{2,1,0:T(8,128)S(1)}, f32[2,168,256]{2,1,0:T(8,128)S(1)}, u32[]{:S(2)}, u32[]{:S(2)}) collective-permute-start(f32[2,168,256]{2,1,0:T(8,128)S(1)} %combine.1.refs_0_), channel_id=1, source_target_pairs={{0,3},{1,2},{2,1},{3,0},{4,7},{5,6},{6,5},{7,4},{8,11},{9,10},{10,... | collective-permute-start | bytes 1032200 | tf_op jit(solution)/shard_map/ppermute | solution.py:959
  62.1 6.3 %copy-start.11 = (f32[2,168,256]{2,1,0:T(8,128)}, f32[2,168,256]{2,1,0:T(8,128)S(1)}, u32[]{:S(2)}) copy-start(f32[2,168,256]{2,1,0:T(8,128)S(1)} %collective-permute-done.3.refs_1_) | copy-start | bytes 1032196
  68.4 0.7 copy-start.12
  68.4 0.8 copy-start.13
  106.9 10.1 %collective-permute-start.6 = (f32[800,256]{1,0:T(8,128)}, f32[800,256]{1,0:T(8,128)S(1)}, u32[]{:S(2)}, u32[]{:S(2)}) collective-permute-start(f32[800,256]{1,0:T(8,128)} %get-tuple-element.154), channel_id=1, source_target_pairs={{0,4},{4,0},{8,12},{12,8},{16,20},{20,16},{24,28},{28,24},{1,5},{5... | collective-permute-start | bytes 2457608 | tf_op jit(solution)/shard_map/ppermute | solution.py:959
  107.1 9.9 %copy-start.7 = (f32[800,256]{1,0:T(8,128)S(1)}, f32[800,256]{1,0:T(8,128)}, u32[]{:S(2)}) copy-start(f32[800,256]{1,0:T(8,128)} %get-tuple-element.153) | copy-start | bytes 2457604
  117.3 26.5 %collective-permute-start.7 = (f32[200,256]{1,0:T(8,128)S(1)}, f32[200,256]{1,0:T(8,128)S(1)}, u32[]{:S(2)}, u32[]{:S(2)}) collective-permute-start(f32[200,256]{1,0:T(8,128)S(1)} %get-tuple-element.251), channel_id=1, source_target_pairs={{0,8},{4,12},{8,0},{12,4},{16,24},{20,28},{24,16},{28,20},{1,9},{5... | collective-permute-start | bytes 614408 | tf_op jit(solution)/shard_map/ppermute | solution.py:959
  118.9 24.8 %collective-permute-start.8 = (f32[200,256]{1,0:T(8,128)S(1)}, f32[200,256]{1,0:T(8,128)S(1)}, u32[]{:S(2)}, u32[]{:S(2)}) collective-permute-start(f32[200,256]{1,0:T(8,128)S(1)} %get-tuple-element.250), channel_id=1, source_target_pairs={{0,16},{4,20},{8,24},{12,28},{16,0},{20,4},{24,8},{28,12},{1,17},{... | collective-permute-start | bytes 614408 | tf_op jit(solution)/shard_map/ppermute | solution.py:959
  121.5 22.3 %collective-permute-start.9 = (f32[200,256]{1,0:T(8,128)S(1)}, f32[200,256]{1,0:T(8,128)S(1)}, u32[]{:S(2)}, u32[]{:S(2)}) collective-permute-start(f32[200,256]{1,0:T(8,128)S(1)} %get-tuple-element.249), channel_id=1, source_target_pairs={{0,24},{4,28},{8,16},{12,20},{16,8},{20,12},{24,0},{28,4},{1,25},{... | collective-permute-start | bytes 614408 | tf_op jit(solution)/shard_map/ppermute | solution.py:959
  121.7 22.0 %collective-permute-start.10 = (f32[2,104,256]{2,1,0:T(8,128)}, f32[2,104,256]{2,1,0:T(8,128)S(1)}, u32[]{:S(2)}, u32[]{:S(2)}) collective-permute-start(f32[2,104,256]{2,1,0:T(8,128)} %get-tuple-element.173), channel_id=1, source_target_pairs={{0,3},{1,2},{2,1},{3,0},{4,7},{5,6},{6,5},{7,4},{8,11},{9,10},{10,... | collective-permute-start | bytes 638984 | tf_op jit(solution)/shard_map/ppermute | solution.py:959
  143.8 13.6 %collective-permute-start.11 = (f32[2,104,256]{2,1,0:T(8,128)}, f32[2,104,256]{2,1,0:T(8,128)S(1)}, u32[]{:S(2)}, u32[]{:S(2)}) collective-permute-start(f32[2,104,256]{2,1,0:T(8,128)} %get-tuple-element.178), channel_id=1, source_target_pairs={{0,1},{1,0},{2,3},{3,2},{4,5},{5,4},{6,7},{7,6},{8,9},{9,8},{10,11... | collective-permute-start | bytes 638984 | tf_op jit(solution)/shard_map/ppermute | solution.py:959
  144.8 12.6 %collective-permute-start.12 = (f32[2,104,256]{2,1,0:T(8,128)}, f32[2,104,256]{2,1,0:T(8,128)S(1)}, u32[]{:S(2)}, u32[]{:S(2)}) collective-permute-start(f32[2,104,256]{2,1,0:T(8,128)} %get-tuple-element.179), channel_id=1, source_target_pairs={{0,2},{1,3},{2,0},{3,1},{4,6},{5,7},{6,4},{7,5},{8,10},{9,11},{10,... | collective-permute-start | bytes 638984 | tf_op jit(solution)/shard_map/ppermute | solution.py:959
  146.4 11.0 %collective-permute-start.13 = (f32[200,256]{1,0:T(8,128)S(1)}, f32[200,256]{1,0:T(8,128)S(1)}, u32[]{:S(2)}, u32[]{:S(2)}) collective-permute-start(f32[200,256]{1,0:T(8,128)S(1)} %add_add_fusion), channel_id=1, source_target_pairs={{0,16},{4,20},{8,24},{12,28},{16,0},{20,4},{24,8},{28,12},{1,17},{... | collective-permute-start | bytes 614408 | tf_op jit(solution)/shard_map/ppermute | solution.py:959
  148.1 11.0 %copy-start = (f32[544,256]{1,0:T(8,128)S(1)}, f32[544,256]{1,0:T(8,128)}, u32[]{:S(2)}) copy-start(f32[544,256]{1,0:T(8,128)} %get-tuple-element.188.refs_4_) | copy-start | bytes 1671172
  148.1 11.0 %copy-start.4 = (f32[2,104,256]{2,1,0:T(8,128)S(1)}, f32[2,104,256]{2,1,0:T(8,128)}, u32[]{:S(2)}) copy-start(f32[2,104,256]{2,1,0:T(8,128)} %get-tuple-element.184.refs_0_) | copy-start | bytes 638980
  148.1 11.0 %copy-start.5 = (s32[4]{0:T(128)S(1)}, s32[4]{0:T(128)}, u32[]{:S(2)}) copy-start(s32[4]{0:T(128)} %pad_add_fusion.me_ref.refs_0_) | copy-start | bytes 52
  157.5 11.9 %collective-permute-start.15 = (f32[400,256]{1,0:T(8,128)S(1)}, f32[400,256]{1,0:T(8,128)S(1)}, u32[]{:S(2)}, u32[]{:S(2)}) collective-permute-start(f32[400,256]{1,0:T(8,128)S(1)} %pad_maximum_fusion.4), channel_id=1, source_target_pairs={{0,8},{4,12},{8,0},{12,4},{16,24},{20,28},{24,16},{28,20},{1,9},{5... | collective-permute-start | bytes 1228808 | tf_op jit(solution)/shard_map/ppermute | solution.py:959
  159.8 0.7 copy-start.1
  160.5 8.9 %collective-permute-start.14 = (f32[344,256]{1,0:T(8,128)S(1)}, f32[344,256]{1,0:T(8,128)S(1)}, u32[]{:S(2)}, u32[]{:S(2)}) collective-permute-start(f32[344,256]{1,0:T(8,128)S(1)} %get-tuple-element.195), channel_id=1, source_target_pairs={{0,1},{1,0},{2,3},{3,2},{4,5},{5,4},{6,7},{7,6},{8,9},{9,8},{10,11... | collective-permute-start | bytes 1056776 | tf_op jit(solution)/shard_map/ppermute | solution.py:959
  169.4 0.7 copy-start.8
  170.2 31.9 %collective-permute-start.18 = (f32[800,256]{1,0:T(8,128)S(1)}, f32[800,256]{1,0:T(8,128)S(1)}, u32[]{:S(2)}, u32[]{:S(2)}) collective-permute-start(f32[800,256]{1,0:T(8,128)S(1)} %pad_maximum_fusion.refs_0_), channel_id=1, source_target_pairs={{0,4},{4,0},{8,12},{12,8},{16,20},{20,16},{24,28},{28,24},{1,5},{5... | collective-permute-start | bytes 2457608 | tf_op jit(solution)/shard_map/ppermute | solution.py:959
  170.3 18.7 %collective-permute-start.19 = (f32[344,256]{1,0:T(8,128)S(1)}, f32[344,256]{1,0:T(8,128)S(1)}, u32[]{:S(2)}, u32[]{:S(2)}) collective-permute-start(f32[344,256]{1,0:T(8,128)S(1)} %get-tuple-element.203), channel_id=1, source_target_pairs={{0,2},{1,3},{2,0},{3,1},{4,6},{5,7},{6,4},{7,5},{8,10},{9,11},{10,... | collective-permute-start | bytes 1056776 | tf_op jit(solution)/shard_map/ppermute | solution.py:959
  171.4 17.6 %collective-permute-start.20 = (f32[344,256]{1,0:T(8,128)S(1)}, f32[344,256]{1,0:T(8,128)S(1)}, u32[]{:S(2)}, u32[]{:S(2)}) collective-permute-start(f32[344,256]{1,0:T(8,128)S(1)} %get-tuple-element.204), channel_id=1, source_target_pairs={{0,3},{1,2},{2,1},{3,0},{4,7},{5,6},{6,5},{7,4},{8,11},{9,10},{10,... | collective-permute-start | bytes 1056776 | tf_op jit(solution)/shard_map/ppermute | solution.py:959
  173.3 28.8 %collective-permute-start.16 = (f32[400,256]{1,0:T(8,128)S(1)}, f32[400,256]{1,0:T(8,128)S(1)}, u32[]{:S(2)}, u32[]{:S(2)}) collective-permute-start(f32[400,256]{1,0:T(8,128)S(1)} %get-tuple-element.248), channel_id=1, source_target_pairs={{0,1},{1,0},{2,3},{3,2},{4,5},{5,4},{6,7},{7,6},{8,9},{9,8},{10,11... | collective-permute-start | bytes 1228808 | tf_op jit(solution)/shard_map/ppermute | solution.py:959
  173.8 28.3 %collective-permute-start.17 = (f32[400,256]{1,0:T(8,128)S(1)}, f32[400,256]{1,0:T(8,128)S(1)}, u32[]{:S(2)}, u32[]{:S(2)}) collective-permute-start(f32[400,256]{1,0:T(8,128)S(1)} %get-tuple-element.247), channel_id=1, source_target_pairs={{0,2},{1,3},{2,0},{3,1},{4,6},{5,7},{6,4},{7,5},{8,10},{9,11},{10,... | collective-permute-start | bytes 1228808 | tf_op jit(solution)/shard_map/ppermute | solution.py:959
  188.9 0.7 copy-start.9
  189.7 0.7 copy-start.10
  194.6 1.5 collective-permute-start.21
  197.0 5.1 %collective-permute-start.22 = (f32[104,256]{1,0:T(8,128)S(1)}, f32[104,256]{1,0:T(8,128)S(1)}, u32[]{:S(2)}, u32[]{:S(2)}) collective-permute-start(f32[104,256]{1,0:T(8,128)S(1)} %add.90), channel_id=1, source_target_pairs={{0,8},{4,12},{8,0},{12,4},{16,24},{20,28},{24,16},{28,20},{1,9},{5... | collective-permute-start | bytes 319496 | tf_op jit(solution)/shard_map/ppermute | solution.py:959
  203.0 20.8 %collective-permute-start.24 = (f32[800,256]{1,0:T(8,128)}, f32[800,256]{1,0:T(8,128)S(1)}, u32[]{:S(2)}, u32[]{:S(2)}) collective-permute-start(f32[800,256]{1,0:T(8,128)} %pad_maximum_fusion.2), channel_id=1, source_target_pairs={{0,1},{1,0},{2,3},{3,2},{4,5},{5,4},{6,7},{7,6},{8,9},{9,8},{10,11... | collective-permute-start | bytes 2457608 | tf_op jit(solution)/shard_map/ppermute | solution.py:959
  205.4 19.4 %collective-permute-start.23 = (f32[800,256]{1,0:T(8,128)}, f32[800,256]{1,0:T(8,128)S(1)}, u32[]{:S(2)}, u32[]{:S(2)}) collective-permute-start(f32[800,256]{1,0:T(8,128)} %pad_maximum_fusion.1), channel_id=1, source_target_pairs={{0,2},{1,3},{2,0},{3,1},{4,6},{5,7},{6,4},{7,5},{8,10},{9,11},{10,... | collective-permute-start | bytes 2457608 | tf_op jit(solution)/shard_map/ppermute | solution.py:959
  205.9 17.8 %collective-permute-start.25 = (f32[400,256]{1,0:T(8,128)S(1)}, f32[400,256]{1,0:T(8,128)}, u32[]{:S(2)}, u32[]{:S(2)}) collective-permute-start(f32[400,256]{1,0:T(8,128)S(1)} %collective-permute-done.16.refs_1_), channel_id=1, source_target_pairs={{0,4},{4,0},{8,12},{12,8},{16,20},{20,16},{24,28},{28,24},{1,5},{5... | collective-permute-start | bytes 1228808 | tf_op jit(solution)/shard_map/ppermute | solution.py:959
  206.0 17.8 %collective-permute-start.26 = (f32[400,256]{1,0:T(8,128)S(1)}, f32[400,256]{1,0:T(8,128)}, u32[]{:S(2)}, u32[]{:S(2)}) collective-permute-start(f32[400,256]{1,0:T(8,128)S(1)} %collective-permute-done.17.refs_2_), channel_id=1, source_target_pairs={{0,4},{4,0},{8,12},{12,8},{16,20},{20,16},{24,28},{28,24},{1,5},{5... | collective-permute-start | bytes 1228808 | tf_op jit(solution)/shard_map/ppermute | solution.py:959
  207.1 28.7 %copy-start.6 = (s32[4]{0:T(128)S(1)}, s32[4]{0:T(128)}, u32[]{:S(2)}) copy-start(s32[4]{0:T(128)} %pad_add_fusion.me_ref.refs_0_) | copy-start | bytes 52
  207.1 16.7 %collective-permute-start.27 = (f32[104,256]{1,0:T(8,128)}, f32[104,256]{1,0:T(8,128)}, u32[]{:S(2)}, u32[]{:S(2)}) collective-permute-start(f32[104,256]{1,0:T(8,128)} %add.91), channel_id=1, source_target_pairs={{0,16},{4,20},{8,24},{12,28},{16,0},{20,4},{24,8},{28,12},{1,17},{... | collective-permute-start | bytes 319496 | tf_op jit(solution)/shard_map/ppermute | solution.py:959
  224.8 11.0 %collective-permute-start.28 = (f32[800,256]{1,0:T(8,128)S(1)}, f32[800,256]{1,0:T(8,128)S(1)}, u32[]{:S(2)}, u32[]{:S(2)}) collective-permute-start(f32[800,256]{1,0:T(8,128)S(1)} %collective-permute-done.23.refs_3_), channel_id=1, source_target_pairs={{0,4},{4,0},{8,12},{12,8},{16,20},{20,16},{24,28},{28,24},{1,5},{5... | collective-permute-start | bytes 2457608 | tf_op jit(solution)/shard_map/ppermute | solution.py:959
  224.8 11.0 %collective-permute-start.29 = (f32[800,256]{1,0:T(8,128)S(1)}, f32[800,256]{1,0:T(8,128)S(1)}, u32[]{:S(2)}, u32[]{:S(2)}) collective-permute-start(f32[800,256]{1,0:T(8,128)S(1)} %collective-permute-done.24.refs_4_), channel_id=1, source_target_pairs={{0,4},{4,0},{8,12},{12,8},{16,20},{20,16},{24,28},{28,24},{1,5},{5... | collective-permute-start | bytes 2457608 | tf_op jit(solution)/shard_map/ppermute | solution.py:959
  226.3 5.8 %collective-permute-start.30 = (f32[104,256]{1,0:T(8,128)S(1)}, f32[104,256]{1,0:T(8,128)S(1)}, u32[]{:S(2)}, u32[]{:S(2)}) collective-permute-start(f32[104,256]{1,0:T(8,128)S(1)} %add.92), channel_id=1, source_target_pairs={{0,1},{1,0},{2,3},{3,2},{4,5},{5,4},{6,7},{7,6},{8,9},{9,8},{10,11... | collective-permute-start | bytes 319496 | tf_op jit(solution)/shard_map/ppermute | solution.py:959
  227.0 7.0 %collective-permute-start.31 = (f32[104,256]{1,0:T(8,128)S(1)}, f32[104,256]{1,0:T(8,128)S(1)}, u32[]{:S(2)}, u32[]{:S(2)}) collective-permute-start(f32[104,256]{1,0:T(8,128)S(1)} %add.92), channel_id=1, source_target_pairs={{0,2},{1,3},{2,0},{3,1},{4,6},{5,7},{6,4},{7,5},{8,10},{9,11},{10,... | collective-permute-start | bytes 319496 | tf_op jit(solution)/shard_map/ppermute | solution.py:959
  228.0 6.0 %collective-permute-start.32 = (f32[104,256]{1,0:T(8,128)S(1)}, f32[104,256]{1,0:T(8,128)S(1)}, u32[]{:S(2)}, u32[]{:S(2)}) collective-permute-start(f32[104,256]{1,0:T(8,128)S(1)} %add.92), channel_id=1, source_target_pairs={{0,3},{1,2},{2,1},{3,0},{4,7},{5,6},{6,5},{7,4},{8,11},{9,10},{10,... | collective-permute-start | bytes 319496 | tf_op jit(solution)/shard_map/ppermute | solution.py:959
  234.0 1.8 collective-permute-start.33
